TPU v7x, 256 devices: a whole 4x4x8 slice. The times are simulated.
256 devices in a mesh: row: 32 (over z, y), col: 4 (over x), depth: 2 (over core).
Axes of the slice: x: 4, y: 4, z: 8, core: 2. Of those that a mesh axis runs over, the one named last changes fastest.
Arguments:
- regions: float32 [16384, 1024], P('row'), may hold values from -4 to 4
- captions: float32 [16384, 1024], P(('row', 'col')), may hold values from -4 to 4
- positive: int32 [16384], P('row'), may hold values from 0 to 16383, each once
Outputs:
- mean_objective: float32 [], replicated
- region_grad: float32 [16384, 1024], P(('row', 'col', 'depth'))
- text_derivative: float32 [16384, 1024], P(('row', 'col'))
Inputs may be any that keep to these rules, and one draw needn't show every extreme that they name: positive is a permutation: every caption is the match of exactly one region.
All inputs are finite; a program needn't handle non-finite values.
Results may differ from a plain program's by a relative error of at most 0.0015.
The roundings to bfloat16 on the way count: a program that leaves them out, or rounds other values in their place, can miss the bound.
Values may be sent and summed in bfloat16 or wider, within the bound.
No kernel may reach another device: no remote copies, remote signals or barrier semaphores. Data moves between devices by JAX's collectives and lax.ppermute only.
A program may use at most 192 MiB of HBM per device.

v0:
```python
import jax
import jax.numpy as jnp
from jax import lax
from jax.sharding import PartitionSpec as P

logit_scaling = 0.07
far_below = -1e30


def shifted_2(value, axis, by):
    count = lax.axis_size(axis)
    return lax.ppermute(value, axis, [(i, (i + by) % count) for i in range(count)])


def joined_2(value, axis, join):
    pieces = jax.tree.map(lambda part: lax.all_gather(part, axis), value)
    head = jax.tree.map(lambda part: part[0], pieces)
    tail = jax.tree.map(lambda part: part[1:], pieces)
    running, _ = lax.scan(lambda running, slab: (join(running, slab), None), head, tail)
    return running


def score_tile(region_bf, caption_block):
    return (
        lax.dot_general(
            region_bf, caption_block, (((1,), (1,)), ((), ())), preferred_element_type=jnp.float32
        )
        / logit_scaling
    )


def tile_stats(scores, start_row, positive):
    row_max = jnp.max(scores, axis=1)
    row_sum = jnp.sum(jnp.exp(scores - row_max[:, None]), axis=1)
    col_max = jnp.max(scores, axis=0)
    col_sum = jnp.sum(jnp.exp(scores - col_max[None, :]), axis=0)
    caption_ids = start_row + lax.iota(jnp.int32, scores.shape[1])
    positive_sum = jnp.sum(jnp.where(positive[:, None] == caption_ids[None, :], scores, 0.0))
    return (row_max, row_sum, col_max, col_sum, positive_sum)


def merge_pair(former, latter):
    new_max = jnp.maximum(former[0], latter[0])
    return (
        new_max,
        former[1] * jnp.exp(former[0] - new_max) + latter[1] * jnp.exp(latter[0] - new_max),
    )


def shards(regions, captions, positive):
    region_count = regions.shape[0]
    feature_dim = regions.shape[1]
    block_rows = captions.shape[0]
    row_count = lax.axis_size("row")
    col_count = lax.axis_size("col")
    cycle_steps = row_count // 2
    row_id = lax.axis_index("row")
    col_id = lax.axis_index("col")
    depth_id = lax.axis_index("depth")
    region_bf = regions.astype(jnp.bfloat16)
    text_lowbits = captions.astype(jnp.bfloat16)
    stride = 1
    shifted = shifted_2(text_lowbits, "row", cycle_steps)
    opening = jnp.where(depth_id == 0, text_lowbits, shifted)
    step_index = jnp.arange(cycle_steps, dtype=jnp.int32)
    owners = (row_id - depth_id * cycle_steps - stride * step_index) % row_count
    starts = (owners * col_count + col_id) * block_rows

    def advance(current, start_row):
        following = shifted_2(current, "row", stride)
        scores = score_tile(region_bf, current)
        return (following, (scores, current) + tile_stats(scores, start_row, positive))

    last_block, stacked = lax.scan(advance, opening, starts[:-1])
    last_scores = score_tile(region_bf, last_block)
    finals = (last_scores, last_block) + tile_stats(last_scores, starts[-1], positive)
    joined = tuple(
        (
            jnp.concatenate([earlier_steps, final_step[None]], axis=0)
            for earlier_steps, final_step in zip(stacked, finals)
        )
    )
    all_scores, all_blocks, row_maxes, row_sums, col_maxes, col_sums, positive_sums = joined
    row_max = jnp.max(row_maxes, axis=0)
    row_sum = jnp.sum(row_sums * jnp.exp(row_maxes - row_max[None, :]), axis=0)
    chosen = owners[:, None] == jnp.arange(row_count, dtype=jnp.int32)[None, :]
    table_max = jnp.max(jnp.where(chosen[:, :, None], col_maxes[:, None, :], far_below), axis=0)
    table_sum = jnp.sum(jnp.where(chosen[:, :, None], col_sums[:, None, :], 0.0), axis=0)
    row_max, row_sum = joined_2((row_max, row_sum), ("col", "depth"), merge_pair)
    table_max, table_sum = joined_2((table_max, table_sum), ("row", "depth"), merge_pair)
    row_lse = row_max + jnp.log(row_sum)
    caption_lse = table_max + jnp.log(table_sum)
    region_share = region_count // (2 * col_count)
    region_part = jnp.sum(
        lax.dynamic_slice_in_dim(row_lse, (col_id * 2 + depth_id) * region_share, region_share)
    )
    caption_share = block_rows // 2
    caption_part = jnp.sum(
        lax.dynamic_slice_in_dim(
            caption_lse.reshape(-1), (row_id * 2 + 1 - depth_id) * caption_share, caption_share
        )
    )
    local_loss = 0.5 * (region_part + caption_part) - jnp.sum(positive_sums)
    mean_objective = lax.psum(local_loss, ("row", "col", "depth")) / (region_count * row_count)

    def grad_tile(scores, caption_block, owner_row, start_row):
        caption_row = lax.dynamic_index_in_dim(caption_lse, owner_row, 0, keepdims=False)
        caption_ids = start_row + lax.iota(jnp.int32, scores.shape[1])
        weight = 0.5 * (jnp.exp(scores - row_lse[:, None]) + jnp.exp(scores - caption_row[None, :]))
        weight = weight - jnp.where(positive[:, None] == caption_ids[None, :], 1.0, 0.0)
        coefficient_lowbits = weight.astype(jnp.bfloat16)
        region_term = jnp.dot(
            coefficient_lowbits, caption_block, preferred_element_type=jnp.float32
        )
        caption_term = lax.dot_general(
            coefficient_lowbits,
            region_bf,
            (((0,), (0,)), ((), ())),
            preferred_element_type=jnp.float32,
        )
        return (region_term, caption_term)

    steps_in = (all_scores, all_blocks, owners, starts)
    region_zero = jnp.zeros((region_count, feature_dim), jnp.float32)

    def travel(running, inputs):
        region_sum, moving = running
        region_term, caption_term = grad_tile(*inputs)
        passed_on = shifted_2(moving + caption_term, "row", stride)
        return ((region_sum + region_term, passed_on), None)

    (region_sum, moving), unused = lax.scan(
        travel, (region_zero, jnp.zeros((block_rows, feature_dim), jnp.float32)), steps_in
    )
    returned = shifted_2(moving, "row", cycle_steps)
    fix_depth = 0
    diagonal_fraction = jnp.where(depth_id == fix_depth, returned, moving)
    text_derivative = lax.psum(diagonal_fraction, "depth") / logit_scaling
    region_grad = (
        lax.psum_scatter(region_sum, ("col", "depth"), scatter_dimension=0, tiled=True)
        / logit_scaling
    )
    return (mean_objective, region_grad, text_derivative)


def solution(mesh):
    return jax.shard_map(
        shards,
        mesh=mesh,
        in_specs=(P("row", None), P(("row", "col"), None), P("row")),
        out_specs=(P(), P(("row", "col", "depth"), None), P(("row", "col"), None)),
        check_vma=False,
    )
```

profile of v0, /device:TPU:1, one launch (start us, length us, event | category | flops | bytes accessed | tf_op | source)
XLA Modules:
  0.0 839.9 jit_solution(6853806963166954744)
XLA Ops:
  8.4 7.8 collective-permute-start.2
  21.7 147.8 %while.61 = (s32[]{:T(128)}, bf16[128,1024]{1,0:T(8,128)(2,1)S(1)}, f32[15,512,128]{2,1,0:T(8,128)}, bf16[15,128,1024]{2,1,0:T(8,128)(2,1)}, f32[15,512]{1,0:T(8...) while((s32[]{:T(128)}, bf16[128,1024]{1,0:T(8,128)(2,1)S(1)}, ...), condition=%wide.region_6.7_spmd, body=%wide.region_0.6_spmd.sunk | while | flops 134871936 | bytes 4477677 | solution.py:74
  29.7 8.9 %collective-permute-done = bf16[128,1024]{1,0:T(8,128)(2,1)S(1)} collective-permute-done((bf16[128,1024]{1,0:T(8,128)(2,1)S(1)}, bf16[128,1024]{1,0:T(8,128)(2,1)S(1)}, u32[]{:S(2)}, u32[]{:S(2)}) %collective-permute-start) | collective-permute-done | bytes 262176 | tf_op jit(solution)/shard_map/while/body/eval_jaxpr/ppermute | solution.py:12
  43.7 4.9 collective-permute-done
  107.1 5.7 collective-permute-done
  118.0 6.0 collective-permute-done
  129.2 5.1 collective-permute-done
  171.8 27.8 %all-gather.4 = f32[8,1,512]{2,1,0:T(1,128)S(1)} all-gather(f32[1,1,512]{2,1,0:T(1,128)S(1)} %bitcast.154), channel_id=2, replica_groups=mesh['row'=32,'col'=4,'depth'=2] {'col','depth'}, dimensions={0}, use_global_device_ids=true | all-gather | bytes 18432 | tf_op jit(solution)/shard_map/all_gather | solution.py:16
  199.6 11.2 %all-gather.3 = f32[8,1,512]{2,1,0:T(1,128)S(1)} all-gather(f32[1,1,512]{2,1,0:T(1,128)S(1)} %maximum_bitcast_fusion), channel_id=1, replica_groups=mesh['row'=32,'col'=4,'depth'=2] {'col','depth'}, dimensions={0}, use_global_device_ids=true | all-gather | bytes 18432 | tf_op jit(solution)/shard_map/all_gather | solution.py:16
  212.7 4.7 pad_maximum_fusion
  220.1 45.2 %all-gather.8.cloned.1.call-done = f32[2048,128]{1,0:T(8,128)} async-done(((f32[32,128]{1,0:T(8,128)}), f32[2048,128]{1,0:T(8,128)}) %all-gather.8.cloned.1.call-update) | async-done | bytes 1048592 | tf_op jit(solution)/shard_map/all_gather | solution.py:16
  267.7 74.5 %all-gather.10.cloned.1.call-done = f32[2048,128]{1,0:T(8,128)} async-done(((f32[32,128]{1,0:T(8,128)}), f32[2048,128]{1,0:T(8,128)}) %all-gather.10.cloned.1.call-update) | async-done | bytes 1048592 | tf_op jit(solution)/shard_map/all_gather | solution.py:16
  345.2 48.7 %while.63 = (s32[]{:T(128)}, f32[32,128]{1,0:T(8,128)S(1)}, f32[32,128]{1,0:T(8,128)S(1)}, f32[63,32,128]{2,1,0:T(8,128)}, f32[63,32,128]{2,1,0:T(8,128)}, /*index=5*/s32[]{:T(128)}) while((s32[]{:T(128)}, f32[32,128]{1,0:T(8,128)S(1)}, f32[32,128]{1,0:T(8,128)S(1)}, f32[63,32,128]{2,1,0:T(8,128)}, f32[63,32,128]{2,1,0:T(8,128)}, ...), condition=%wide.region_19.20_spmd, body=%wide.region_18.19_spmd.sunk | while | flops 24578 | bytes 98377 | solution.py:19
  394.8 327.1 %while.64 = (s32[]{:T(128)}, f32[512,1024]{1,0:T(8,128)S(1)}, f32[128,1024]{1,0:T(8,128)}, f32[16,512,128]{2,1,0:T(8,128)}, f32[512]{0:T(512)S(1)}, /*index=5*/s...) while((s32[]{:T(128)}, f32[512,1024]{1,0:T(8,128)S(1)}, ...), condition=%wide.region_25.26_spmd.clone, body=%wide.region_24.25_spmd.clone.sunk | while | flops 270663808 | bytes 9188612 | solution.py:132
  403.1 14.9 %collective-permute-done.1 = f32[128,1024]{1,0:T(8,128)} collective-permute-done((f32[128,1024]{1,0:T(8,128)}, f32[128,1024]{1,0:T(8,128)}, u32[]{:S(2)}, u32[]{:S(2)}) %collective-permute-start.1) | collective-permute-done | bytes 524320 | tf_op jit(solution)/shard_map/while/body/eval_jaxpr/ppermute | solution.py:12
  426.1 14.2 %collective-permute-done.1 = f32[128,1024]{1,0:T(8,128)} collective-permute-done((f32[128,1024]{1,0:T(8,128)}, f32[128,1024]{1,0:T(8,128)}, u32[]{:S(2)}, u32[]{:S(2)}) %collective-permute-start.1) | collective-permute-done | bytes 524320 | tf_op jit(solution)/shard_map/while/body/eval_jaxpr/ppermute | solution.py:12
  448.3 13.3 %collective-permute-done.1 = f32[128,1024]{1,0:T(8,128)} collective-permute-done((f32[128,1024]{1,0:T(8,128)}, f32[128,1024]{1,0:T(8,128)}, u32[]{:S(2)}, u32[]{:S(2)}) %collective-permute-start.1) | collective-permute-done | bytes 524320 | tf_op jit(solution)/shard_map/while/body/eval_jaxpr/ppermute | solution.py:12
  469.6 12.4 %collective-permute-done.1 = f32[128,1024]{1,0:T(8,128)} collective-permute-done((f32[128,1024]{1,0:T(8,128)}, f32[128,1024]{1,0:T(8,128)}, u32[]{:S(2)}, u32[]{:S(2)}) %collective-permute-start.1) | collective-permute-done | bytes 524320 | tf_op jit(solution)/shard_map/while/body/eval_jaxpr/ppermute | solution.py:12
  490.1 11.4 %collective-permute-done.1 = f32[128,1024]{1,0:T(8,128)} collective-permute-done((f32[128,1024]{1,0:T(8,128)}, f32[128,1024]{1,0:T(8,128)}, u32[]{:S(2)}, u32[]{:S(2)}) %collective-permute-start.1) | collective-permute-done | bytes 524320 | tf_op jit(solution)/shard_map/while/body/eval_jaxpr/ppermute | solution.py:12
  509.6 10.5 %collective-permute-done.1 = f32[128,1024]{1,0:T(8,128)} collective-permute-done((f32[128,1024]{1,0:T(8,128)}, f32[128,1024]{1,0:T(8,128)}, u32[]{:S(2)}, u32[]{:S(2)}) %collective-permute-start.1) | collective-permute-done | bytes 524320 | tf_op jit(solution)/shard_map/while/body/eval_jaxpr/ppermute | solution.py:12
  528.1 9.9 %collective-permute-done.1 = f32[128,1024]{1,0:T(8,128)} collective-permute-done((f32[128,1024]{1,0:T(8,128)}, f32[128,1024]{1,0:T(8,128)}, u32[]{:S(2)}, u32[]{:S(2)}) %collective-permute-start.1) | collective-permute-done | bytes 524320 | tf_op jit(solution)/shard_map/while/body/eval_jaxpr/ppermute | solution.py:12
  546.1 9.9 %collective-permute-done.1 = f32[128,1024]{1,0:T(8,128)} collective-permute-done((f32[128,1024]{1,0:T(8,128)}, f32[128,1024]{1,0:T(8,128)}, u32[]{:S(2)}, u32[]{:S(2)}) %collective-permute-start.1) | collective-permute-done | bytes 524320 | tf_op jit(solution)/shard_map/while/body/eval_jaxpr/ppermute | solution.py:12
  564.0 9.9 %collective-permute-done.1 = f32[128,1024]{1,0:T(8,128)} collective-permute-done((f32[128,1024]{1,0:T(8,128)}, f32[128,1024]{1,0:T(8,128)}, u32[]{:S(2)}, u32[]{:S(2)}) %collective-permute-start.1) | collective-permute-done | bytes 524320 | tf_op jit(solution)/shard_map/while/body/eval_jaxpr/ppermute | solution.py:12
  581.9 9.9 %collective-permute-done.1 = f32[128,1024]{1,0:T(8,128)} collective-permute-done((f32[128,1024]{1,0:T(8,128)}, f32[128,1024]{1,0:T(8,128)}, u32[]{:S(2)}, u32[]{:S(2)}) %collective-permute-start.1) | collective-permute-done | bytes 524320 | tf_op jit(solution)/shard_map/while/body/eval_jaxpr/ppermute | solution.py:12
  599.8 9.9 %collective-permute-done.1 = f32[128,1024]{1,0:T(8,128)} collective-permute-done((f32[128,1024]{1,0:T(8,128)}, f32[128,1024]{1,0:T(8,128)}, u32[]{:S(2)}, u32[]{:S(2)}) %collective-permute-start.1) | collective-permute-done | bytes 524320 | tf_op jit(solution)/shard_map/while/body/eval_jaxpr/ppermute | solution.py:12
  617.8 9.9 %collective-permute-done.1 = f32[128,1024]{1,0:T(8,128)} collective-permute-done((f32[128,1024]{1,0:T(8,128)}, f32[128,1024]{1,0:T(8,128)}, u32[]{:S(2)}, u32[]{:S(2)}) %collective-permute-start.1) | collective-permute-done | bytes 524320 | tf_op jit(solution)/shard_map/while/body/eval_jaxpr/ppermute | solution.py:12
  635.7 9.9 %collective-permute-done.1 = f32[128,1024]{1,0:T(8,128)} collective-permute-done((f32[128,1024]{1,0:T(8,128)}, f32[128,1024]{1,0:T(8,128)}, u32[]{:S(2)}, u32[]{:S(2)}) %collective-permute-start.1) | collective-permute-done | bytes 524320 | tf_op jit(solution)/shard_map/while/body/eval_jaxpr/ppermute | solution.py:12
  653.6 10.6 %collective-permute-done.1 = f32[128,1024]{1,0:T(8,128)} collective-permute-done((f32[128,1024]{1,0:T(8,128)}, f32[128,1024]{1,0:T(8,128)}, u32[]{:S(2)}, u32[]{:S(2)}) %collective-permute-start.1) | collective-permute-done | bytes 524320 | tf_op jit(solution)/shard_map/while/body/eval_jaxpr/ppermute | solution.py:12
  672.3 11.7 %collective-permute-done.1 = f32[128,1024]{1,0:T(8,128)} collective-permute-done((f32[128,1024]{1,0:T(8,128)}, f32[128,1024]{1,0:T(8,128)}, u32[]{:S(2)}, u32[]{:S(2)}) %collective-permute-start.1) | collective-permute-done | bytes 524320 | tf_op jit(solution)/shard_map/while/body/eval_jaxpr/ppermute | solution.py:12
  692.0 30.0 %collective-permute-done.1 = f32[128,1024]{1,0:T(8,128)} collective-permute-done((f32[128,1024]{1,0:T(8,128)}, f32[128,1024]{1,0:T(8,128)}, u32[]{:S(2)}, u32[]{:S(2)}) %collective-permute-start.1) | collective-permute-done | bytes 524320 | tf_op jit(solution)/shard_map/while/body/eval_jaxpr/ppermute | solution.py:12
  724.8 9.4 %collective-permute-done.3 = f32[128,1024]{1,0:T(8,128)S(1)} collective-permute-done((f32[128,1024]{1,0:T(8,128)}, f32[128,1024]{1,0:T(8,128)S(1)}, u32[]{:S(2)}, u32[]{:S(2)}) %collective-permute-start.3) | collective-permute-done | bytes 524320 | tf_op jit(solution)/shard_map/ppermute | solution.py:12
  741.2 86.7 %psum.14 = f32[]{:T(128)} all-reduce(f32[]{:T(128)S(6)} %sub.115), channel_id=1, replica_groups=mesh['row'=32,'col'=4,'depth'=2] {'row','col','depth'}, use_global_device_ids=true, to_apply=%region_23.24 | all-reduce | flops 1 | bytes 8 | tf_op jit(solution)/shard_map/psum | solution.py:104
  (470 shorter events, 292.8 us)
Async XLA Ops:
  7.2 258.1 %all-gather.8.cloned.1.call-start = ((), (), s32[]{:S(2)}) async-start(), calls=%async_computation.3 | async-start | bytes 1064960 | tf_op jit(solution)/shard_map/all_gather | solution.py:16
  8.4 13.3 %collective-permute-start.2 = (bf16[128,1024]{1,0:T(8,128)(2,1)S(1)}, bf16[128,1024]{1,0:T(8,128)(2,1)S(1)}, u32[]{:S(2)}, u32[]{:S(2)}) collective-permute-start(bf16[128,1024]{1,0:T(8,128)(2,1)S(1)} %convert_element_type.14), channel_id=1, source_target_pairs={{0,128},{8,136},{16,144},{24,152},{32,160},{40,168},{48,176},{56,1... | collective-permute-start | bytes 786440 | tf_op jit(solution)/shard_map/ppermute | solution.py:12
  21.8 16.8 %collective-permute-start = (bf16[128,1024]{1,0:T(8,128)(2,1)S(1)}, bf16[128,1024]{1,0:T(8,128)(2,1)S(1)}, u32[]{:S(2)}, u32[]{:S(2)}) collective-permute-start(bf16[128,1024]{1,0:T(8,128)(2,1)S(1)} %copy.32), channel_id=1, source_target_pairs={{0,8},{8,16},{16,24},{24,32},{32,40},{40,48},{48,56},{56,64},{64,7... | collective-permute-start | bytes 786440 | tf_op jit(solution)/shard_map/while/body/eval_jaxpr/ppermute | solution.py:12
  38.6 10.0 %collective-permute-start = (bf16[128,1024]{1,0:T(8,128)(2,1)S(1)}, bf16[128,1024]{1,0:T(8,128)(2,1)S(1)}, u32[]{:S(2)}, u32[]{:S(2)}) collective-permute-start(bf16[128,1024]{1,0:T(8,128)(2,1)S(1)} %copy.32), channel_id=1, source_target_pairs={{0,8},{8,16},{16,24},{24,32},{32,40},{40,48},{48,56},{56,64},{64,7... | collective-permute-start | bytes 786440 | tf_op jit(solution)/shard_map/while/body/eval_jaxpr/ppermute | solution.py:12
  48.5 9.1 %collective-permute-start = (bf16[128,1024]{1,0:T(8,128)(2,1)S(1)}, bf16[128,1024]{1,0:T(8,128)(2,1)S(1)}, u32[]{:S(2)}, u32[]{:S(2)}) collective-permute-start(bf16[128,1024]{1,0:T(8,128)(2,1)S(1)} %copy.32), channel_id=1, source_target_pairs={{0,8},{8,16},{16,24},{24,32},{32,40},{40,48},{48,56},{56,64},{64,7... | collective-permute-start | bytes 786440 | tf_op jit(solution)/shard_map/while/body/eval_jaxpr/ppermute | solution.py:12
  57.6 8.6 %collective-permute-start = (bf16[128,1024]{1,0:T(8,128)(2,1)S(1)}, bf16[128,1024]{1,0:T(8,128)(2,1)S(1)}, u32[]{:S(2)}, u32[]{:S(2)}) collective-permute-start(bf16[128,1024]{1,0:T(8,128)(2,1)S(1)} %copy.32), channel_id=1, source_target_pairs={{0,8},{8,16},{16,24},{24,32},{32,40},{40,48},{48,56},{56,64},{64,7... | collective-permute-start | bytes 786440 | tf_op jit(solution)/shard_map/while/body/eval_jaxpr/ppermute | solution.py:12
  66.3 8.6 %collective-permute-start = (bf16[128,1024]{1,0:T(8,128)(2,1)S(1)}, bf16[128,1024]{1,0:T(8,128)(2,1)S(1)}, u32[]{:S(2)}, u32[]{:S(2)}) collective-permute-start(bf16[128,1024]{1,0:T(8,128)(2,1)S(1)} %copy.32), channel_id=1, source_target_pairs={{0,8},{8,16},{16,24},{24,32},{32,40},{40,48},{48,56},{56,64},{64,7... | collective-permute-start | bytes 786440 | tf_op jit(solution)/shard_map/while/body/eval_jaxpr/ppermute | solution.py:12
  92.2 9.8 %collective-permute-start = (bf16[128,1024]{1,0:T(8,128)(2,1)S(1)}, bf16[128,1024]{1,0:T(8,128)(2,1)S(1)}, u32[]{:S(2)}, u32[]{:S(2)}) collective-permute-start(bf16[128,1024]{1,0:T(8,128)(2,1)S(1)} %copy.32), channel_id=1, source_target_pairs={{0,8},{8,16},{16,24},{24,32},{32,40},{40,48},{48,56},{56,64},{64,7... | collective-permute-start | bytes 786440 | tf_op jit(solution)/shard_map/while/body/eval_jaxpr/ppermute | solution.py:12
  102.0 10.8 %collective-permute-start = (bf16[128,1024]{1,0:T(8,128)(2,1)S(1)}, bf16[128,1024]{1,0:T(8,128)(2,1)S(1)}, u32[]{:S(2)}, u32[]{:S(2)}) collective-permute-start(bf16[128,1024]{1,0:T(8,128)(2,1)S(1)} %copy.32), channel_id=1, source_target_pairs={{0,8},{8,16},{16,24},{24,32},{32,40},{40,48},{48,56},{56,64},{64,7... | collective-permute-start | bytes 786440 | tf_op jit(solution)/shard_map/while/body/eval_jaxpr/ppermute | solution.py:12
  112.8 11.2 %collective-permute-start = (bf16[128,1024]{1,0:T(8,128)(2,1)S(1)}, bf16[128,1024]{1,0:T(8,128)(2,1)S(1)}, u32[]{:S(2)}, u32[]{:S(2)}) collective-permute-start(bf16[128,1024]{1,0:T(8,128)(2,1)S(1)} %copy.32), channel_id=1, source_target_pairs={{0,8},{8,16},{16,24},{24,32},{32,40},{40,48},{48,56},{56,64},{64,7... | collective-permute-start | bytes 786440 | tf_op jit(solution)/shard_map/while/body/eval_jaxpr/ppermute | solution.py:12
  124.0 10.2 %collective-permute-start = (bf16[128,1024]{1,0:T(8,128)(2,1)S(1)}, bf16[128,1024]{1,0:T(8,128)(2,1)S(1)}, u32[]{:S(2)}, u32[]{:S(2)}) collective-permute-start(bf16[128,1024]{1,0:T(8,128)(2,1)S(1)} %copy.32), channel_id=1, source_target_pairs={{0,8},{8,16},{16,24},{24,32},{32,40},{40,48},{48,56},{56,64},{64,7... | collective-permute-start | bytes 786440 | tf_op jit(solution)/shard_map/while/body/eval_jaxpr/ppermute | solution.py:12
  134.3 9.3 %collective-permute-start = (bf16[128,1024]{1,0:T(8,128)(2,1)S(1)}, bf16[128,1024]{1,0:T(8,128)(2,1)S(1)}, u32[]{:S(2)}, u32[]{:S(2)}) collective-permute-start(bf16[128,1024]{1,0:T(8,128)(2,1)S(1)} %copy.32), channel_id=1, source_target_pairs={{0,8},{8,16},{16,24},{24,32},{32,40},{40,48},{48,56},{56,64},{64,7... | collective-permute-start | bytes 786440 | tf_op jit(solution)/shard_map/while/body/eval_jaxpr/ppermute | solution.py:12
  171.7 170.5 %all-gather.10.cloned.1.call-start = ((), (), s32[]{:S(2)}) async-start(), calls=%async_computation.4 | async-start | bytes 1064960 | tf_op jit(solution)/shard_map/all_gather | solution.py:16
  212.7 616.0 %all-reduce.2.cloned.1.call-start = ((), (), s32[]{:S(2)}) async-start(), calls=%async_computation.2 | async-start | bytes 1048576 | tf_op jit(solution)/shard_map/psum | solution.py:138
  401.1 16.9 %collective-permute-start.1 = (f32[128,1024]{1,0:T(8,128)}, f32[128,1024]{1,0:T(8,128)}, u32[]{:S(2)}, u32[]{:S(2)}) collective-permute-start(f32[128,1024]{1,0:T(8,128)} %convolution_add_fusion.2), channel_id=1, source_target_pairs={{0,8},{8,16},{16,24},{24,32},{32,40},{40,48},{48,56},{56,64},{64,7... | collective-permute-start | bytes 1572872 | tf_op jit(solution)/shard_map/while/body/eval_jaxpr/ppermute | solution.py:12
  424.3 16.0 %collective-permute-start.1 = (f32[128,1024]{1,0:T(8,128)}, f32[128,1024]{1,0:T(8,128)}, u32[]{:S(2)}, u32[]{:S(2)}) collective-permute-start(f32[128,1024]{1,0:T(8,128)} %convolution_add_fusion.2), channel_id=1, source_target_pairs={{0,8},{8,16},{16,24},{24,32},{32,40},{40,48},{48,56},{56,64},{64,7... | collective-permute-start | bytes 1572872 | tf_op jit(solution)/shard_map/while/body/eval_jaxpr/ppermute | solution.py:12
  446.5 15.1 %collective-permute-start.1 = (f32[128,1024]{1,0:T(8,128)}, f32[128,1024]{1,0:T(8,128)}, u32[]{:S(2)}, u32[]{:S(2)}) collective-permute-start(f32[128,1024]{1,0:T(8,128)} %convolution_add_fusion.2), channel_id=1, source_target_pairs={{0,8},{8,16},{16,24},{24,32},{32,40},{40,48},{48,56},{56,64},{64,7... | collective-permute-start | bytes 1572872 | tf_op jit(solution)/shard_map/while/body/eval_jaxpr/ppermute | solution.py:12
  467.9 14.2 %collective-permute-start.1 = (f32[128,1024]{1,0:T(8,128)}, f32[128,1024]{1,0:T(8,128)}, u32[]{:S(2)}, u32[]{:S(2)}) collective-permute-start(f32[128,1024]{1,0:T(8,128)} %convolution_add_fusion.2), channel_id=1, source_target_pairs={{0,8},{8,16},{16,24},{24,32},{32,40},{40,48},{48,56},{56,64},{64,7... | collective-permute-start | bytes 1572872 | tf_op jit(solution)/shard_map/while/body/eval_jaxpr/ppermute | solution.py:12
  488.3 13.2 %collective-permute-start.1 = (f32[128,1024]{1,0:T(8,128)}, f32[128,1024]{1,0:T(8,128)}, u32[]{:S(2)}, u32[]{:S(2)}) collective-permute-start(f32[128,1024]{1,0:T(8,128)} %convolution_add_fusion.2), channel_id=1, source_target_pairs={{0,8},{8,16},{16,24},{24,32},{32,40},{40,48},{48,56},{56,64},{64,7... | collective-permute-start | bytes 1572872 | tf_op jit(solution)/shard_map/while/body/eval_jaxpr/ppermute | solution.py:12
  507.8 12.3 %collective-permute-start.1 = (f32[128,1024]{1,0:T(8,128)}, f32[128,1024]{1,0:T(8,128)}, u32[]{:S(2)}, u32[]{:S(2)}) collective-permute-start(f32[128,1024]{1,0:T(8,128)} %convolution_add_fusion.2), channel_id=1, source_target_pairs={{0,8},{8,16},{16,24},{24,32},{32,40},{40,48},{48,56},{56,64},{64,7... | collective-permute-start | bytes 1572872 | tf_op jit(solution)/shard_map/while/body/eval_jaxpr/ppermute | solution.py:12
  526.3 11.7 %collective-permute-start.1 = (f32[128,1024]{1,0:T(8,128)}, f32[128,1024]{1,0:T(8,128)}, u32[]{:S(2)}, u32[]{:S(2)}) collective-permute-start(f32[128,1024]{1,0:T(8,128)} %convolution_add_fusion.2), channel_id=1, source_target_pairs={{0,8},{8,16},{16,24},{24,32},{32,40},{40,48},{48,56},{56,64},{64,7... | collective-permute-start | bytes 1572872 | tf_op jit(solution)/shard_map/while/body/eval_jaxpr/ppermute | solution.py:12
  544.3 11.7 %collective-permute-start.1 = (f32[128,1024]{1,0:T(8,128)}, f32[128,1024]{1,0:T(8,128)}, u32[]{:S(2)}, u32[]{:S(2)}) collective-permute-start(f32[128,1024]{1,0:T(8,128)} %convolution_add_fusion.2), channel_id=1, source_target_pairs={{0,8},{8,16},{16,24},{24,32},{32,40},{40,48},{48,56},{56,64},{64,7... | collective-permute-start | bytes 1572872 | tf_op jit(solution)/shard_map/while/body/eval_jaxpr/ppermute | solution.py:12
  562.2 11.7 %collective-permute-start.1 = (f32[128,1024]{1,0:T(8,128)}, f32[128,1024]{1,0:T(8,128)}, u32[]{:S(2)}, u32[]{:S(2)}) collective-permute-start(f32[128,1024]{1,0:T(8,128)} %convolution_add_fusion.2), channel_id=1, source_target_pairs={{0,8},{8,16},{16,24},{24,32},{32,40},{40,48},{48,56},{56,64},{64,7... | collective-permute-start | bytes 1572872 | tf_op jit(solution)/shard_map/while/body/eval_jaxpr/ppermute | solution.py:12
  580.1 11.7 %collective-permute-start.1 = (f32[128,1024]{1,0:T(8,128)}, f32[128,1024]{1,0:T(8,128)}, u32[]{:S(2)}, u32[]{:S(2)}) collective-permute-start(f32[128,1024]{1,0:T(8,128)} %convolution_add_fusion.2), channel_id=1, source_target_pairs={{0,8},{8,16},{16,24},{24,32},{32,40},{40,48},{48,56},{56,64},{64,7... | collective-permute-start | bytes 1572872 | tf_op jit(solution)/shard_map/while/body/eval_jaxpr/ppermute | solution.py:12
  598.0 11.7 %collective-permute-start.1 = (f32[128,1024]{1,0:T(8,128)}, f32[128,1024]{1,0:T(8,128)}, u32[]{:S(2)}, u32[]{:S(2)}) collective-permute-start(f32[128,1024]{1,0:T(8,128)} %convolution_add_fusion.2), channel_id=1, source_target_pairs={{0,8},{8,16},{16,24},{24,32},{32,40},{40,48},{48,56},{56,64},{64,7... | collective-permute-start | bytes 1572872 | tf_op jit(solution)/shard_map/while/body/eval_jaxpr/ppermute | solution.py:12
  616.0 11.7 %collective-permute-start.1 = (f32[128,1024]{1,0:T(8,128)}, f32[128,1024]{1,0:T(8,128)}, u32[]{:S(2)}, u32[]{:S(2)}) collective-permute-start(f32[128,1024]{1,0:T(8,128)} %convolution_add_fusion.2), channel_id=1, source_target_pairs={{0,8},{8,16},{16,24},{24,32},{32,40},{40,48},{48,56},{56,64},{64,7... | collective-permute-start | bytes 1572872 | tf_op jit(solution)/shard_map/while/body/eval_jaxpr/ppermute | solution.py:12
  633.9 11.7 %collective-permute-start.1 = (f32[128,1024]{1,0:T(8,128)}, f32[128,1024]{1,0:T(8,128)}, u32[]{:S(2)}, u32[]{:S(2)}) collective-permute-start(f32[128,1024]{1,0:T(8,128)} %convolution_add_fusion.2), channel_id=1, source_target_pairs={{0,8},{8,16},{16,24},{24,32},{32,40},{40,48},{48,56},{56,64},{64,7... | collective-permute-start | bytes 1572872 | tf_op jit(solution)/shard_map/while/body/eval_jaxpr/ppermute | solution.py:12
  651.8 12.4 %collective-permute-start.1 = (f32[128,1024]{1,0:T(8,128)}, f32[128,1024]{1,0:T(8,128)}, u32[]{:S(2)}, u32[]{:S(2)}) collective-permute-start(f32[128,1024]{1,0:T(8,128)} %convolution_add_fusion.2), channel_id=1, source_target_pairs={{0,8},{8,16},{16,24},{24,32},{32,40},{40,48},{48,56},{56,64},{64,7... | collective-permute-start | bytes 1572872 | tf_op jit(solution)/shard_map/while/body/eval_jaxpr/ppermute | solution.py:12
  670.5 13.5 %collective-permute-start.1 = (f32[128,1024]{1,0:T(8,128)}, f32[128,1024]{1,0:T(8,128)}, u32[]{:S(2)}, u32[]{:S(2)}) collective-permute-start(f32[128,1024]{1,0:T(8,128)} %convolution_add_fusion.2), channel_id=1, source_target_pairs={{0,8},{8,16},{16,24},{24,32},{32,40},{40,48},{48,56},{56,64},{64,7... | collective-permute-start | bytes 1572872 | tf_op jit(solution)/shard_map/while/body/eval_jaxpr/ppermute | solution.py:12
  690.2 31.7 %collective-permute-start.1 = (f32[128,1024]{1,0:T(8,128)}, f32[128,1024]{1,0:T(8,128)}, u32[]{:S(2)}, u32[]{:S(2)}) collective-permute-start(f32[128,1024]{1,0:T(8,128)} %convolution_add_fusion.2), channel_id=1, source_target_pairs={{0,8},{8,16},{16,24},{24,32},{32,40},{40,48},{48,56},{56,64},{64,7... | collective-permute-start | bytes 1572872 | tf_op jit(solution)/shard_map/while/body/eval_jaxpr/ppermute | solution.py:12
  721.9 12.3 %collective-permute-start.3 = (f32[128,1024]{1,0:T(8,128)}, f32[128,1024]{1,0:T(8,128)S(1)}, u32[]{:S(2)}, u32[]{:S(2)}) collective-permute-start(f32[128,1024]{1,0:T(8,128)} %get-tuple-element.199), channel_id=1, source_target_pairs={{0,128},{8,136},{16,144},{24,152},{32,160},{40,168},{48,176},{56,1... | collective-permute-start | bytes 1572872 | tf_op jit(solution)/shard_map/ppermute | solution.py:12
  736.1 94.4 %reduce-scatter.2.cloned.1.call-start = ((), (), s32[]{:S(2)}) async-start(), calls=%async_computation.1 | async-start | bytes 2359296 | tf_op jit(solution)/shard_map/reduce_scatter | solution.py:140
  (15 other events, 201.7 us)
Sparse Core Ops, SparseCore 0:
  171.8 93.4 all-gather.7
  268.1 74.0 all-gather.9
  736.2 39.3 all-reduce.1
  778.2 34.3 reduce-scatter.1
where the time goes:
time: 853 us; the launch traced here: 840 us
  waiting for transfers between devices  398 us (47%)
  blocking collectives  126 us (15%)
  other arithmetic  102 us (12%)
  matrix products  85.9 us (10%)
  local copies, waits for them, and re-layouts  61.2 us (7%)
  loops' own time  33.2 us (4%)
  between operations  18.4 us (2%)
  starting transfers between devices  15.2 us (2%)
    ppermute x33, waiting for transfers between devices, shifted_2(): lax.ppermute(value, axis, [(i, (i + by) % count) for i in range(count)])  278 us
    all_gather x2, waiting for transfers between devices, joined_2(): pieces = jax.tree.map(lambda part: lax.all_gather(part, axis), value)  120 us
    psum x1, blocking collectives, shards(): lax.psum(local_loss, ('row', 'col', 'depth')) / (region_count * row_count)  86.7 us
    add x70, other arithmetic, merge_pair(): former[1] * jnp.exp(former[0] - new_max)  48 us
    dot_general x16, matrix products, grad_tile(): lax.dot_general(coefficient_lowbits, region_bf, (((0,), (0,)), ((), ())),...  39.5 us
    all_gather x2, blocking collectives, joined_2(): pieces = jax.tree.map(lambda part: lax.all_gather(part, axis), value)  39 us
    another operation x1, loops' own time, shards(): lax.scan(travel, (region_zero, jnp.zeros((block_rows, feature_dim), jnp.f...  31.5 us
    dot_general x16, matrix products, grad_tile(): jnp.dot(coefficient_lowbits, caption_block, preferred_element_type=jnp.fl...  28.5 us
  transfers between devices with their start and end apart: 37, of which 35 were waited for; matrix products, arithmetic and copies ran while one was open for 15% of the time, Pallas kernels for 0%

commit v1 on v0

v1 whole, which is shorter than its diff:
```python
import functools

import jax
import jax.numpy as jnp
from jax import lax
from jax.experimental import pallas as pl
from jax.experimental.pallas import tpu as pltpu
from jax.sharding import Mesh
from jax.sharding import PartitionSpec as P

logit_scaling = 0.07
far_below = -1e30
head_room = 3.5
tiny = 1e-30
AXES = ("z", "y", "col", "depth")
NZ, NY, NX = 8, 4, 4
FEATURES = 1024
GROUP = 64
BLOCK = 128
TILE = 1024
BF = jnp.bfloat16
F32 = jnp.float32
WIRE = jnp.float16
VMEM = pltpu.VMEM
SMEM = pltpu.SMEM


def index_of(z, y, x, c):
    return ((z % NZ * NY + y % NY) * NX + x % NX) * 2 + c


def moved(value, target):
    pairs = []
    for z in range(NZ):
        for y in range(NY):
            for x in range(NX):
                for c in range(2):
                    to = target(z, y, x, c)
                    if to is not None:
                        pairs.append((index_of(z, y, x, c), index_of(*to)))
    return lax.ppermute(value, AXES, pairs)


def swapped(value):
    return moved(value, lambda z, y, x, c: (z, y, x, 1 - c))


def from_y(value, by):
    return moved(value, lambda z, y, x, c: (z, y - by, x, c))


def from_x(value, by):
    return moved(value, lambda z, y, x, c: (z, y, x - by, c))


def along_z(value, by):
    return moved(value, lambda z, y, x, c: (z + by if c == 0 else z - by, y, x, c))


def call(kernel, outs, *args, limit=48 << 20):
    specs = [
        pl.BlockSpec(memory_space=SMEM if arg.dtype == jnp.int32 else VMEM) for arg in args
    ]
    return pl.pallas_call(
        kernel,
        in_specs=specs,
        out_specs=[pl.BlockSpec(memory_space=VMEM) for _ in outs],
        out_shape=[jax.ShapeDtypeStruct(shape, dtype) for shape, dtype in outs],
        compiler_params=pltpu.CompilerParams(vmem_limit_bytes=limit),
    )(*args)


def place_rows(ref, offset, rows):
    ref[pl.ds(pl.multiple_of(offset, GROUP), GROUP), :] = rows


def column(row):
    return jnp.transpose(jnp.broadcast_to(row, (BLOCK, BLOCK)))


def line(col):
    return jnp.transpose(jnp.broadcast_to(col, (BLOCK, BLOCK)))[0:1, :]


def slot_z(slot, z, c):
    way = 1 - 2 * c
    if slot == 0:
        return z
    if slot <= 3:
        return (z + way * slot + NZ) % NZ
    if slot <= 6:
        return (z - way * (slot - 3) + NZ) % NZ
    return (z + 4) % NZ


def largest(ref):
    best = jnp.abs(ref[0:16, :])
    for start in range(16, TILE, 16):
        best = jnp.maximum(best, jnp.abs(ref[start : start + 16, :]))
    return jnp.max(best.astype(F32))


def score_kernel(
    place, h0, h1, h3, g0, g1, g3, g2, own, near, far, s_out, r_out, c_out, keep, give
):
    z, y, x, c = place[0], place[1], place[2], place[3]

    def put(rows, yy, xx):
        yy, xx = yy % NY, xx % NX
        place_rows(r_out, jnp.where(c == 0, yy * 256 + xx * 64, xx * 256 + yy * 64), rows)

    for ref, by in ((h0, 0), (h1, 1), (h3, 3)):
        for xx in range(NX):
            put(ref[xx * GROUP : (xx + 1) * GROUP, :], y + by, xx)
    for ref, by in ((g0, 0), (g1, 1), (g3, 3), (g2, 2)):
        put(ref[0:GROUP, :], y + 2, x + by)

    c_out[0:128, :] = own[...]
    c_out[128:512, :] = near[0:384, :]
    c_out[512:896, :] = far[0:384, :]
    place_rows(c_out, 896 + c * GROUP, near[384:448, :])
    place_rows(c_out, 896 + (1 - c) * GROUP, far[384:448, :])

    positive = jnp.zeros((8, TILE), F32)
    for ref, by, start in ((h0, 0, 256), (h1, 1, 256), (h3, 3, 256), (g0, 2, 64)):
        coded = ref[start : start + 16, :].astype(F32)
        number = jnp.broadcast_to(coded[0:1, :] * 128.0 + coded[1:2, :], (8, TILE))
        shift = (y + by) % NY * jnp.where(c == 0, 256, 64)
        positive = positive + pltpu.roll(number, shift, 1)
    positive = positive[0:1, :].astype(jnp.int32)

    regions = r_out[...]
    row_max = jnp.full((1, TILE), far_below, F32)
    row_sum = jnp.zeros((1, TILE), F32)
    matched = jnp.zeros((1, TILE), F32)
    cap_maxes = [None] * 8
    cap_sums = [None] * 8
    for slot in range(8):
        chunk = pl.ds(slot * BLOCK, BLOCK)
        scores = lax.dot_general(
            c_out[chunk, :], regions, (((1,), (1,)), ((), ())), preferred_element_type=F32
        ) * (1.0 / logit_scaling)
        s_out[chunk, :] = scores
        owner = slot_z(slot, z, c)
        first = ((owner * NY + y) * NX + x) * BLOCK
        local = positive - first
        ids = lax.broadcasted_iota(jnp.int32, (BLOCK, TILE), 0)
        matched = matched + jnp.sum(
            jnp.where(ids == local, scores, 0.0), axis=0, keepdims=True
        )
        new_max = jnp.maximum(row_max, jnp.max(scores, axis=0, keepdims=True))
        row_sum = row_sum * jnp.exp(row_max - new_max) + jnp.sum(
            jnp.exp(scores - new_max), axis=0, keepdims=True
        )
        row_max = new_max
        cap_max = jnp.max(scores, axis=1, keepdims=True)
        cap_sum = jnp.sum(jnp.exp(scores - cap_max), axis=1, keepdims=True)
        cap_maxes[slot] = line(cap_max)
        cap_sums[slot] = line(cap_sum)

    keep[...] = jnp.zeros((8, TILE), F32)
    give[...] = jnp.zeros((8, TILE), F32)
    for slot in range(8):
        lanes = pl.ds(pl.multiple_of(slot_z(slot, z, c) * BLOCK, BLOCK), BLOCK)
        give[0:1, lanes] = cap_maxes[slot]
        give[2:3, lanes] = cap_sums[slot]
    cap_row_max = give[0:1, :]
    cap_row_sum = give[2:3, :]
    total = jnp.broadcast_to(jnp.sum(matched), (1, TILE))
    caption_top = jnp.broadcast_to(largest(c_out), (1, TILE))
    region_top = jnp.broadcast_to(largest(r_out), (1, TILE))
    zero = jnp.zeros((1, TILE), F32)
    by_row = (row_max, row_sum, total, caption_top)
    by_cap = (cap_row_max, cap_row_sum, zero, region_top)
    for line_at, rows, caps in zip((0, 2, 4, 5), by_row, by_cap):
        keep[line_at : line_at + 1, :] = jnp.where(c == 0, rows, caps)
        give[line_at : line_at + 1, :] = jnp.where(c == 0, caps, rows)


def pair_kernel(place, keep, came, out):
    first = place[3] == 0
    m0, m1, s0, s1 = keep[0:1, :], came[0:1, :], keep[2:3, :], came[2:3, :]
    top = jnp.maximum(m0, m1)
    merged = s0 * jnp.exp(m0 - top) + s1 * jnp.exp(m1 - top)
    zero = jnp.zeros((1, TILE), F32)
    out[0:1, :] = jnp.where(first, m0, top)
    out[1:2, :] = jnp.where(first, m1, zero)
    out[2:3, :] = jnp.where(first, s0, merged)
    out[3:4, :] = jnp.where(first, s1, zero)
    out[4:5, :] = keep[4:5, :] + came[4:5, :]
    out[5:6, :] = jnp.maximum(keep[5:6, :], came[5:6, :])
    out[6:8, :] = jnp.zeros((2, TILE), F32)


def merged_four(own, a, b, opposite):
    maxes = [part[0:2, :] for part in (own, opposite, a, b)]
    top = jnp.maximum(jnp.maximum(maxes[0], maxes[1]), jnp.maximum(maxes[2], maxes[3]))
    parts = [
        part[2:4, :] * jnp.exp(m - top) for part, m in zip((own, opposite, a, b), maxes)
    ]
    sums = (parts[0] + parts[1]) + (parts[2] + parts[3])
    total = (own[4:5, :] + opposite[4:5, :]) + (a[4:5, :] + b[4:5, :])
    peak = jnp.maximum(
        jnp.maximum(own[5:6, :], opposite[5:6, :]), jnp.maximum(a[5:6, :], b[5:6, :])
    )
    return top, sums, total, peak


def four_kernel(own, a, b, opposite, out):
    top, sums, total, peak = merged_four(own[...], a[...], b[...], opposite[...])
    out[0:2, :] = top
    out[2:4, :] = sums
    out[4:5, :] = total
    out[5:6, :] = peak
    out[6:8, :] = jnp.zeros((2, TILE), F32)


def last_kernel(place, own, a, b, opposite, out):
    first = place[3] == 0
    lines = lax.broadcasted_iota(jnp.int32, (8, TILE), 0)
    empty = jnp.where(lines < 2, far_below, 0.0)
    top, sums, total, peak = merged_four(
        own[...],
        a[...],
        jnp.where(first, b[...], empty),
        jnp.where(first, opposite[...], empty),
    )
    lse = top + jnp.log(jnp.where(jnp.logical_or(first, lines[0:2, :] == 0), sums, 1.0))
    both = 0.5 * jnp.sum(lse[0:1, :]) + jnp.where(first, 0.5 * jnp.sum(lse[1:2, :]), 0.0)
    out[0:1, :] = lse[0:1, :]
    out[1:2, :] = jnp.where(first, lse[1:2, :], lse[0:1, :])
    out[2:4, :] = jnp.zeros((2, TILE), F32)
    out[4:5, :] = jnp.broadcast_to(both, (1, TILE)) - total
    out[5:6, :] = peak
    out[6:8, :] = jnp.zeros((2, TILE), F32)


def caption_kernel(
    place, scores, regions, mine, came, h0, h1, h3, g0, w_out, keep, give, own
):
    z, y, x, c = place[0], place[1], place[2], place[3]
    first_core = c == 0
    row_lse = jnp.where(first_core, mine[0:1, :], came[1:2, :])
    region_top = jnp.where(first_core, came[5:6, :], mine[5:6, :])
    scale = head_room / jnp.maximum(region_top, tiny)
    positive = jnp.zeros((8, TILE), F32)
    for ref, by, start in ((h0, 0, 256), (h1, 1, 256), (h3, 3, 256), (g0, 2, 64)):
        coded = ref[start : start + 16, :].astype(F32)
        number = jnp.broadcast_to(coded[0:1, :] * 128.0 + coded[1:2, :], (8, TILE))
        shift = (y + by) % NY * jnp.where(c == 0, 256, 64)
        positive = positive + pltpu.roll(number, shift, 1)
    positive = positive[0:1, :].astype(jnp.int32)
    region_rows = regions[...]
    for slot in (4, 5, 6, 7, 1, 2, 3, 0):
        chunk = pl.ds(slot * BLOCK, BLOCK)
        owner = slot_z(slot, z, c)
        lanes = pl.ds(pl.multiple_of(owner * BLOCK, BLOCK), BLOCK)
        cap_line = jnp.where(first_core, came[1:2, lanes], mine[0:1, lanes])
        cap_lse = jnp.concatenate([column(cap_line)] * 8, axis=1)
        first = ((owner * NY + y) * NX + x) * BLOCK
        ids = lax.broadcasted_iota(jnp.int32, (BLOCK, TILE), 0)
        s = scores[chunk, :]
        weight = 0.5 * (jnp.exp(s - row_lse) + jnp.exp(s - cap_lse))
        weight = weight - jnp.where(ids == positive - first, 1.0, 0.0)
        low = weight.astype(BF)
        w_out[chunk, :] = low
        part = jnp.dot(low, region_rows, preferred_element_type=F32) * scale
        if slot == 0:
            own[...] = part
        elif slot <= 3:
            keep[(slot - 1) * BLOCK : slot * BLOCK, :] = part
        elif slot <= 6:
            give[(slot - 4) * BLOCK : (slot - 3) * BLOCK, :] = part
        else:
            keep[384:448, :] = jnp.where(first_core, part[0:64, :], part[64:128, :])
            give[384:448, :] = jnp.where(first_core, part[64:128, :], part[0:64, :])


def region_kernel(place, weights, captions, mine, came, o0, o1, o3, o2):
    y, x, c = place[1], place[2], place[3]
    first_core = c == 0
    caption_top = jnp.where(first_core, mine[5:6, :], came[5:6, :])
    scale = head_room / jnp.maximum(caption_top, tiny)
    major = jnp.where(first_core, y, x)
    caption_rows = captions[...]
    for ref, by in ((o2, 2), (o1, 1), (o3, 3), (o0, 0)):
        lanes = pl.ds(pl.multiple_of((major + by) % 4 * 256, 256), 256)
        part = lax.dot_general(
            weights[:, lanes], caption_rows, (((0,), (0,)), ((), ())), preferred_element_type=F32
        )
        ref[...] = part * scale


def shards(regions, captions, positive):
    z = lax.axis_index("z")
    y = lax.axis_index("y")
    x = lax.axis_index("col")
    c = lax.axis_index("depth")
    place = jnp.stack([z, y, x, c]).astype(jnp.int32)
    first_core = c == 0
    big = (TILE, FEATURES)

    half = lax.dynamic_index_in_dim(
        regions.reshape(NX, 2, GROUP, FEATURES), c, 1, keepdims=False
    )
    matches = lax.dynamic_index_in_dim(positive.reshape(NX, 2, GROUP), c, 1, keepdims=False)
    packed = jnp.pad(matches.reshape(256), (0, 768))
    spread = jnp.pad(matches, ((0, 0), (0, 192))).reshape(TILE)
    row = jnp.where(first_core, packed, spread)
    coded = jnp.pad(jnp.stack([row // 128, row % 128]), ((0, 14), (0, 0))).astype(BF)
    own_half = jnp.concatenate([half.reshape(256, FEATURES).astype(BF), coded], axis=0)
    own_group = jnp.concatenate(
        [
            lax.dynamic_index_in_dim(half, x, 0, keepdims=False).astype(BF),
            coded,
        ],
        axis=0,
    )
    text = captions.astype(BF)

    two = along_z(text, -2)
    g0 = from_y(own_group, 2)
    one = along_z(text, -1)
    h1 = from_y(own_half, 1)
    h3 = from_y(own_half, 3)
    three = along_z(two, -1)
    four = along_z(lax.dynamic_slice_in_dim(two, c * GROUP, GROUP, 0), -2)
    group = g0[0:GROUP]
    g1 = from_x(group, 1)
    g3 = from_x(group, 3)
    g2 = from_x(group, 2)
    near = jnp.concatenate([one, two, three, four], axis=0)
    far = swapped(near)

    scores, region_rows, caption_rows, keep, give = call(
        score_kernel,
        [(big, F32), (big, BF), (big, BF), ((8, TILE), F32), ((8, TILE), F32)],
        place, own_half, h1, h3, g0, g1, g3, g2, text, near, far,
    )

    small = [((8, TILE), F32)]
    (stats,) = call(pair_kernel, small, place, keep, swapped(give))

    def stage_one(by_y, by_z):
        return moved(
            stats, lambda z, y, x, c: (z, y - by_y, x, c) if c == 0 else (z - by_z, y, x, c)
        )

    (stats,) = call(
        four_kernel, small, stats, stage_one(1, 2), stage_one(3, 6), stage_one(2, 4)
    )
    a = moved(stats, lambda z, y, x, c: (z, y, x - 1, c) if c == 0 else (z ^ 1, y, x, c))
    b = moved(stats, lambda z, y, x, c: (z, y, x - 3, c) if c == 0 else None)
    opposite = moved(stats, lambda z, y, x, c: (z, y, x - 2, c) if c == 0 else None)
    (lse,) = call(last_kernel, small, place, stats, a, b, opposite)
    came = swapped(lse)

    weights, keep, give, own = call(
        caption_kernel,
        [(big, BF), ((448, FEATURES), F32), ((448, FEATURES), F32), ((BLOCK, FEATURES), F32)],
        place, scores, region_rows, lse, came, own_half, h1, h3, g0,
    )
    got = swapped(give.astype(WIRE))
    quarter = ((256, FEATURES), F32)
    r0, r1, r3, r2 = call(
        region_kernel, [quarter] * 4, place, weights, caption_rows, lse, came
    )

    def major_from(value, by):
        return moved(
            value, lambda z, y, x, c: (z, y + by, x, c) if c == 0 else (z, y, x + by, c)
        )

    def minor_from(value, by):
        return moved(
            value, lambda z, y, x, c: (z, y, x + by, c) if c == 0 else (z, y + by, x, c)
        )

    q2 = major_from(r2.astype(WIRE), 2)
    q1 = major_from(r1.astype(WIRE), 1)
    q3 = major_from(r3.astype(WIRE), 3)

    total = keep + got.astype(F32)
    ahead = along_z(
        jnp.concatenate([total[0:128], total[256:384]], axis=0).astype(WIRE), 1
    )
    skipped = along_z(total[384:448].astype(WIRE), 2)
    summed = ((r0 + q2.astype(F32)) + (q1.astype(F32) + q3.astype(F32))).reshape(
        4, GROUP, FEATURES
    )
    minor = jnp.where(first_core, x, y)

    def piece(by):
        return lax.dynamic_index_in_dim(summed, (minor + by) % 4, 0, keepdims=False)

    t2 = minor_from(piece(2).astype(WIRE), 2)
    t1 = minor_from(piece(1).astype(WIRE), 1)
    t3 = minor_from(piece(3).astype(WIRE), 3)
    skipped_rows = lax.dynamic_update_slice_in_dim(
        jnp.zeros((BLOCK, FEATURES), F32), skipped.astype(F32), c * GROUP, 0
    )
    onward = total[128:256] + ahead[128:256].astype(F32) + skipped_rows
    passed = along_z(onward.astype(WIRE), 2)
    mine = own + ahead[0:128].astype(F32) + passed.astype(F32)

    share = lse[4:5, 0:128] * jnp.ones((8, 1), F32)
    for bit in range(4):
        def partner(z, y, x, c, bit=bit):
            if c == 0:
                return (z ^ (1 << bit), y, x, c) if bit < 3 else None
            return (z, y ^ (1 << bit), x, c) if bit < 2 else (z, y, x ^ (1 << (bit - 2)), c)

        share = share + moved(share, partner)
    share = share + swapped(share)
    mean_objective = share[0, 0] / (NZ * NY * regions.shape[0])

    caption_top = jnp.where(first_core, lse[5, 0], came[5, 0])
    region_top = jnp.where(first_core, came[5, 0], lse[5, 0])
    unscale = 1.0 / (head_room * logit_scaling)
    region_grad = ((piece(0) + t2.astype(F32)) + (t1.astype(F32) + t3.astype(F32))) * (
        jnp.maximum(caption_top, tiny) * unscale
    )
    text_derivative = (mine + swapped(mine)) * (jnp.maximum(region_top, tiny) * unscale)
    return mean_objective, region_grad, text_derivative


def solution(mesh):
    grid = Mesh(mesh.devices.reshape(NZ, NY, NX, 2), AXES)
    return jax.shard_map(
        shards,
        mesh=grid,
        in_specs=(P(("z", "y"), None), P(("z", "y", "col"), None), P(("z", "y"))),
        out_specs=(
            P(),
            P(("z", "y", "col", "depth"), None),
            P(("z", "y", "col"), None),
        ),
        check_vma=False,
    )
```

time: 853 us -> 168 us (0.20); the launches traced: 840 us -> 167 us
  waiting for transfers between devices: 398 us -> 52.1 us
  blocking collectives: 126 us -> 0 us
  other arithmetic: 102 us -> 12.4 us
  matrix products: 85.9 us -> 0 us
  local copies, waits for them, and re-layouts: 61.2 us -> 8.43 us
  starting transfers between devices: 15.2 us -> 65.8 us
  loops' own time: 33.2 us -> 0 us
  Pallas kernels: 0 us -> 23.1 us
  between operations: 18.4 us -> 5.3 us
    ppermute x33 -> x35, waiting for transfers between devices: 278 us -> 52.1 us  [moved(): return lax.ppermute(value, AXES, pairs)]
    all_gather x2 -> x0, waiting for transfers between devices: 120 us -> none  [joined_2(): pieces = jax.tree.map(lambda part: lax.all_gather(part, axis), value)]
    psum x1 -> x0, blocking collectives: 86.7 us -> none  [shards(): lax.psum(local_loss, ('row', 'col', 'depth')) / (region_count * row_count)]
    dot_general x48 -> x0, matrix products: 85.9 us -> none  [the longest x16 39.5 us: grad_tile(): lax.dot_general(coefficient_lowbits, region_bf, (((0,), (0,)), ((), ())),...]
    add x104 -> x9, other arithmetic: 68.7 us -> 3.46 us  [the longest x1 1.86 us: shards(): mine = own + ahead[0:128].astype(F32) + passed.astype(F32)]
    ppermute x33 -> x35, starting transfers between devices: 15 us -> 65.8 us  [moved(): return lax.ppermute(value, AXES, pairs)]
    all_gather x2 -> x0, blocking collectives: 39 us -> none  [joined_2(): pieces = jax.tree.map(lambda part: lax.all_gather(part, axis), value)]
    another operation x4 -> x0, loops' own time: 33.2 us -> none  [the longest x1 31.5 us: shards(): lax.scan(travel, (region_zero, jnp.zeros((block_rows, feature_dim), jnp.f...]
  transfers between devices with their start and end apart: 37 -> 35, of which waited for: 35 -> 21; matrix products, arithmetic and copies ran while one was open for 15% -> 8% of each run, Pallas kernels for 0% -> 3%
where the time goes in v1:
time: 168 us; the launch traced here: 167 us
  starting transfers between devices  65.8 us (39%)
  waiting for transfers between devices  52.1 us (31%)
  Pallas kernels  23.1 us (14%)
  other arithmetic  12.4 us (7%)
  local copies, waits for them, and re-layouts  8.43 us (5%)
  between operations  5.3 us (3%)
    ppermute x35, starting transfers between devices, moved(): return lax.ppermute(value, AXES, pairs)  65.8 us
    ppermute x35, waiting for transfers between devices, moved(): return lax.ppermute(value, AXES, pairs)  52.1 us
    pallas_call x6, Pallas kernels, call(): pl.pallas_call(kernel, in_specs=specs, out_specs=[pl.BlockSpec(memory_spa...  23.1 us
  transfers between devices with their start and end apart: 35, of which 21 were waited for; matrix products, arithmetic and copies ran while one was open for 8% of the time, Pallas kernels for 3%

profile of v1, /device:TPU:1, one launch (start us, length us, event | category | flops | bytes accessed | tf_op | source)
XLA Modules:
  0.0 167.1 jit_solution(14436160678781500746)
XLA Ops:
  1.9 3.9 %collective-permute-start.7 = (bf16[128,1024]{1,0:T(8,128)(2,1)S(1)}, bf16[128,1024]{1,0:T(8,128)(2,1)S(1)}, u32[]{:S(2)}, u32[]{:S(2)}) collective-permute-start(bf16[128,1024]{1,0:T(8,128)(2,1)S(1)} %convert_element_type.88.own), channel_id=1, source_target_pairs={{0,192},{1,65},{2,194},{3,67},{4,196},{5,69},{6,198},{7,71},{8,200... | collective-permute-start | bytes 786440 | tf_op jit(solution)/shard_map/ppermute | solution.py:41
  9.5 3.6 %collective-permute-done.7 = bf16[128,1024]{1,0:T(8,128)(2,1)S(1)} collective-permute-done((bf16[128,1024]{1,0:T(8,128)(2,1)S(1)}, bf16[128,1024]{1,0:T(8,128)(2,1)S(1)}, u32[]{:S(2)}, u32[]{:S(2)}) %collective-permute-start.7) | collective-permute-done | bytes 262176 | tf_op jit(solution)/shard_map/ppermute | solution.py:41
  13.2 3.1 %collective-permute-start.8 = (bf16[128,1024]{1,0:T(8,128)(2,1)S(1)}, bf16[128,1024]{1,0:T(8,128)(2,1)S(1)}, u32[]{:S(2)}, u32[]{:S(2)}) collective-permute-start(bf16[128,1024]{1,0:T(8,128)(2,1)S(1)} %collective-permute-done.7), channel_id=1, source_target_pairs={{0,224},{1,33},{2,226},{3,35},{4,228},{5,37},{6,230},{7,39},{8,232... | collective-permute-start | bytes 786440 | tf_op jit(solution)/shard_map/ppermute | solution.py:41
  21.7 2.7 %collective-permute-done.9 = bf16[64,1024]{1,0:T(8,128)(2,1)S(1)} collective-permute-done((bf16[64,1024]{1,0:T(8,128)(2,1)S(1)}, bf16[64,1024]{1,0:T(8,128)(2,1)S(1)}, u32[]{:S(2)}, u32[]{:S(2)}) %collective-permute-start.9) | collective-permute-done | bytes 131104 | tf_op jit(solution)/shard_map/ppermute | solution.py:41
  25.1 3.5 %collective-permute-start.10 = (bf16[448,1024]{1,0:T(8,128)(2,1)}, bf16[448,1024]{1,0:T(8,128)(2,1)}, u32[]{:S(2)}, u32[]{:S(2)}) collective-permute-start(bf16[448,1024]{1,0:T(8,128)(2,1)} %constant_dynamic-update-slice_fusion.near), channel_id=1, source_target_pairs={{0,1},{1,0},{2,3},{3,2},{4,5},{5,4},{6,7},{7,6},{8,9},{9,8},{10,11... | collective-permute-start | bytes 2752520 | tf_op jit(solution)/shard_map/ppermute | solution.py:41
  31.6 15.9 %collective-permute-done.2.g0 = bf16[80,1024]{1,0:T(8,128)(2,1)S(1)} collective-permute-done((bf16[80,1024]{1,0:T(8,128)(2,1)S(1)}, bf16[80,1024]{1,0:T(8,128)(2,1)S(1)}, u32[]{:S(2)}, u32[]{:S(2)}) %collective-permute-start.2) | collective-permute-done | bytes 163872 | tf_op jit(solution)/shard_map/ppermute | solution.py:41
  48.2 2.5 %collective-permute-start.3 = (bf16[64,1024]{1,0:T(8,128)(2,1)}, bf16[64,1024]{1,0:T(8,128)(2,1)S(1)}, u32[]{:S(2)}, u32[]{:S(2)}) collective-permute-start(bf16[64,1024]{1,0:T(8,128)(2,1)} %slice.49), channel_id=1, source_target_pairs={{0,6},{1,7},{2,0},{3,1},{4,2},{5,3},{6,4},{7,5},{8,14},{9,15},{10,... | collective-permute-start | bytes 393224 | tf_op jit(solution)/shard_map/ppermute | solution.py:41
  50.7 2.3 %collective-permute-done.3.g1 = bf16[64,1024]{1,0:T(8,128)(2,1)S(1)} collective-permute-done((bf16[64,1024]{1,0:T(8,128)(2,1)}, bf16[64,1024]{1,0:T(8,128)(2,1)S(1)}, u32[]{:S(2)}, u32[]{:S(2)}) %collective-permute-start.3) | collective-permute-done | bytes 131104 | tf_op jit(solution)/shard_map/ppermute | solution.py:41
  53.0 2.0 %collective-permute-start.5 = (bf16[64,1024]{1,0:T(8,128)(2,1)}, bf16[64,1024]{1,0:T(8,128)(2,1)}, u32[]{:S(2)}, u32[]{:S(2)}) collective-permute-start(bf16[64,1024]{1,0:T(8,128)(2,1)} %slice.49), channel_id=1, source_target_pairs={{0,4},{1,5},{2,6},{3,7},{4,0},{5,1},{6,2},{7,3},{8,12},{9,13},{10,... | collective-permute-start | bytes 393224 | tf_op jit(solution)/shard_map/ppermute | solution.py:41
  56.0 2.7 %collective-permute-done.5.g2 = bf16[64,1024]{1,0:T(8,128)(2,1)} collective-permute-done((bf16[64,1024]{1,0:T(8,128)(2,1)}, bf16[64,1024]{1,0:T(8,128)(2,1)}, u32[]{:S(2)}, u32[]{:S(2)}) %collective-permute-start.5) | collective-permute-done | bytes 131104 | tf_op jit(solution)/shard_map/ppermute | solution.py:41
  59.7 10.5 %shard_map.58 = (f32[1024,1024]{1,0:T(8,128)}, bf16[1024,1024]{1,0:T(8,128)(2,1)}, bf16[1024,1024]{1,0:T(8,128)(2,1)}, f32[8,1024]{1,0:T(8,128)S(1)}, f32[8,1024]{1,0:T(8,128)S(1)}) custom-call(s32[4]{0:T(128)S(1)} %pad_add_fusion.place, bf16[272,1024]{1,0:T(8,128)(2,1)S(1)} %pad_maximum_fusion.h0, bf16[272,1024]{1,0:T(8,128)(2,1)S(1)} %collective-permute-done.h1, ...), custom_call_target="tpu_custom_call" | custom-call | tf_op jit(solution)/shard_map/pallas_call | solution.py:64
  70.2 3.0 %collective-permute-start.11 = (f32[8,1024]{1,0:T(8,128)S(1)}, f32[8,1024]{1,0:T(8,128)S(1)}, u32[]{:S(2)}, u32[]{:S(2)}) collective-permute-start(f32[8,1024]{1,0:T(8,128)S(1)} %get-tuple-element.17), channel_id=1, source_target_pairs={{0,1},{1,0},{2,3},{3,2},{4,5},{5,4},{6,7},{7,6},{8,9},{9,8},{10,11... | collective-permute-start | bytes 98312 | tf_op jit(solution)/shard_map/ppermute | solution.py:41
  74.7 3.4 %collective-permute-start.12 = (f32[8,1024]{1,0:T(8,128)S(1)}, f32[8,1024]{1,0:T(8,128)S(1)}, u32[]{:S(2)}, u32[]{:S(2)}) collective-permute-start(f32[8,1024]{1,0:T(8,128)S(1)} %shard_map.59.own), channel_id=1, source_target_pairs={{0,24},{1,193},{2,26},{3,195},{4,28},{5,197},{6,30},{7,199},{8,0},... | collective-permute-start | bytes 98312 | tf_op jit(solution)/shard_map/ppermute | solution.py:41
  78.1 2.2 %collective-permute-start.14 = (f32[8,1024]{1,0:T(8,128)S(1)}, f32[8,1024]{1,0:T(8,128)S(1)}, u32[]{:S(2)}, u32[]{:S(2)}) collective-permute-start(f32[8,1024]{1,0:T(8,128)S(1)} %shard_map.59.own), channel_id=1, source_target_pairs={{0,16},{1,129},{2,18},{3,131},{4,20},{5,133},{6,22},{7,135},{8,24}... | collective-permute-start | bytes 98312 | tf_op jit(solution)/shard_map/ppermute | solution.py:41
  80.3 3.0 %collective-permute-done.13.b = f32[8,1024]{1,0:T(8,128)S(1)} collective-permute-done((f32[8,1024]{1,0:T(8,128)S(1)}, f32[8,1024]{1,0:T(8,128)S(1)}, u32[]{:S(2)}, u32[]{:S(2)}) %collective-permute-start.13) | collective-permute-done | bytes 32800 | tf_op jit(solution)/shard_map/ppermute | solution.py:41
  88.4 8.1 %collective-permute-start.23 = (f32[8,1024]{1,0:T(8,128)S(1)}, f32[8,1024]{1,0:T(8,128)S(1)}, u32[]{:S(2)}, u32[]{:S(2)}) collective-permute-start(f32[8,1024]{1,0:T(8,128)S(1)} %shard_map.61.mine), channel_id=1, source_target_pairs={{0,1},{1,0},{2,3},{3,2},{4,5},{5,4},{6,7},{7,6},{8,9},{9,8},{10,11... | collective-permute-start | bytes 98312 | tf_op jit(solution)/shard_map/ppermute | solution.py:41
  97.4 6.6 %shard_map.62 = (bf16[1024,1024]{1,0:T(8,128)(2,1)}, f32[448,1024]{1,0:T(8,128)S(1)}, f32[448,1024]{1,0:T(8,128)S(1)}, f32[128,1024]{1,0:T(8,128)S(1)}) custom-call(s32[4]{0:T(128)S(1)} %pad_add_fusion.place, f32[1024,1024]{1,0:T(8,128)} %get-tuple-element.18.scores, bf16[1024,1024]{1,0:T(8,128)(2,1)} %get-tuple-element.19.regions, ...), custom_call_target="tpu_custom_call" | custom-call | tf_op jit(solution)/shard_map/pallas_call | solution.py:64
  104.6 2.1 %collective-permute-done.30 = f16[448,1024]{1,0:T(8,128)(2,1)S(1)} collective-permute-done((f16[448,1024]{1,0:T(8,128)(2,1)S(1)}, f16[448,1024]{1,0:T(8,128)(2,1)S(1)}, u32[]{:S(2)}, u32[]{:S(2)}) %collective-permute-start.30) | collective-permute-done | bytes 917536 | tf_op jit(solution)/shard_map/ppermute | solution.py:41
  109.4 3.1 %collective-permute-start.31 = (f16[256,1024]{1,0:T(8,128)(2,1)}, f16[256,1024]{1,0:T(8,128)(2,1)}, u32[]{:S(2)}, u32[]{:S(2)}) collective-permute-start(f16[256,1024]{1,0:T(8,128)(2,1)} %pad_maximum_fusion.1), channel_id=1, source_target_pairs={{0,32},{1,225},{2,34},{3,227},{4,36},{5,229},{6,38},{7,231},{8,40}... | collective-permute-start | bytes 1572872 | tf_op jit(solution)/shard_map/ppermute | solution.py:41
  112.5 4.6 %shard_map.63 = (f32[256,1024]{1,0:T(8,128)S(1)}, f32[256,1024]{1,0:T(8,128)S(1)}, f32[256,1024]{1,0:T(8,128)S(1)}, f32[256,1024]{1,0:T(8,128)S(1)}) custom-call(s32[4]{0:T(128)S(1)} %pad_add_fusion.place, bf16[1024,1024]{1,0:T(8,128)(2,1)} %get-tuple-element.20.weights, bf16[1024,1024]{1,0:T(8,128)(2,1)} %get-tuple-element.21.captions, ...), custom_call_target="tpu_custom_call" | custom-call | tf_op jit(solution)/shard_map/pallas_call | solution.py:64
  118.6 2.4 %collective-permute-start.25 = (f16[256,1024]{1,0:T(8,128)(2,1)S(1)}, f16[256,1024]{1,0:T(8,128)(2,1)S(1)}, u32[]{:S(2)}, u32[]{:S(2)}) collective-permute-start(f16[256,1024]{1,0:T(8,128)(2,1)S(1)} %convert_element_type.91), channel_id=1, source_target_pairs={{0,8},{1,3},{2,10},{3,5},{4,12},{5,7},{6,14},{7,1},{8,16},{9,11},{... | collective-permute-start | bytes 1572872 | tf_op jit(solution)/shard_map/ppermute | solution.py:41
  121.6 2.2 %collective-permute-start.19 = (f32[8,128]{1,0:T(8,128)S(1)}, f32[8,128]{1,0:T(8,128)S(1)}, u32[]{:S(2)}, u32[]{:S(2)}) collective-permute-start(f32[8,128]{1,0:T(8,128)S(1)} %broadcast_add_fusion), channel_id=1, source_target_pairs={{0,64},{1,17},{2,66},{3,19},{4,68},{5,21},{6,70},{7,23},{8,72},{9,... | collective-permute-start | bytes 12296 | tf_op jit(solution)/shard_map/ppermute | solution.py:41
  123.8 2.0 %collective-permute-start.32 = (f16[64,1024]{1,0:T(8,128)(2,1)S(1)}, f16[64,1024]{1,0:T(8,128)(2,1)S(1)}, u32[]{:S(2)}, u32[]{:S(2)}) collective-permute-start(f16[64,1024]{1,0:T(8,128)(2,1)S(1)} %slice.58), channel_id=1, source_target_pairs={{0,64},{1,193},{2,66},{3,195},{4,68},{5,197},{6,70},{7,199},{8,72}... | collective-permute-start | bytes 393224 | tf_op jit(solution)/shard_map/ppermute | solution.py:41
  126.9 2.0 %collective-permute-done.32 = f16[64,1024]{1,0:T(8,128)(2,1)S(1)} collective-permute-done((f16[64,1024]{1,0:T(8,128)(2,1)S(1)}, f16[64,1024]{1,0:T(8,128)(2,1)S(1)}, u32[]{:S(2)}, u32[]{:S(2)}) %collective-permute-start.32) | collective-permute-done | bytes 131104 | tf_op jit(solution)/shard_map/ppermute | solution.py:41
  129.0 3.4 %collective-permute-start.33 = (f16[128,1024]{1,0:T(8,128)(2,1)S(1)}, f16[128,1024]{1,0:T(8,128)(2,1)S(1)}, u32[]{:S(2)}, u32[]{:S(2)}) collective-permute-start(f16[128,1024]{1,0:T(8,128)(2,1)S(1)} %convert_element_type.109), channel_id=1, source_target_pairs={{0,64},{1,193},{2,66},{3,195},{4,68},{5,197},{6,70},{7,199},{8,72}... | collective-permute-start | bytes 786440 | tf_op jit(solution)/shard_map/ppermute | solution.py:41
  133.5 4.8 %collective-permute-done.33 = f16[128,1024]{1,0:T(8,128)(2,1)S(1)} collective-permute-done((f16[128,1024]{1,0:T(8,128)(2,1)S(1)}, f16[128,1024]{1,0:T(8,128)(2,1)S(1)}, u32[]{:S(2)}, u32[]{:S(2)}) %collective-permute-start.33) | collective-permute-done | bytes 262176 | tf_op jit(solution)/shard_map/ppermute | solution.py:41
  138.2 1.9 %convert_add_fusion.1 = f32[128,1024]{1,0:T(8,128)} fusion(f16[128,1024]{1,0:T(8,128)(2,1)S(1)} %collective-permute-done.33, f32[128,1024]{1,0:T(8,128)S(1)} %copy-done.4, f16[256,1024]{1,0:T(8,128)(2,1)} %collective-permute-done.31), kind=kLoop, calls=%fused_computation.7 | loop fusion | flops 524288 | bytes 1572864 | tf_op jit(solution)/shard_map/add | solution.py:404
  140.1 2.3 %collective-permute-start.34 = (f32[128,1024]{1,0:T(8,128)}, f32[128,1024]{1,0:T(8,128)}, u32[]{:S(2)}, u32[]{:S(2)}) collective-permute-start(f32[128,1024]{1,0:T(8,128)} %convert_add_fusion.1), channel_id=1, source_target_pairs={{0,1},{1,0},{2,3},{3,2},{4,5},{5,4},{6,7},{7,6},{8,9},{9,8},{10,11... | collective-permute-start | bytes 1572872 | tf_op jit(solution)/shard_map/ppermute | solution.py:41
  143.6 2.6 %collective-permute-start.29 = (f16[64,1024]{1,0:T(8,128)(2,1)S(1)}, f16[64,1024]{1,0:T(8,128)(2,1)}, u32[]{:S(2)}, u32[]{:S(2)}) collective-permute-start(f16[64,1024]{1,0:T(8,128)(2,1)S(1)} %get-tuple-element.34), channel_id=1, source_target_pairs={{0,6},{1,25},{2,0},{3,27},{4,2},{5,29},{6,4},{7,31},{8,14},{9,1},{... | collective-permute-start | bytes 393224 | tf_op jit(solution)/shard_map/ppermute | solution.py:41
  146.5 2.6 %collective-permute-done.20 = f32[8,128]{1,0:T(8,128)S(1)} collective-permute-done((f32[8,128]{1,0:T(8,128)S(1)}, f32[8,128]{1,0:T(8,128)S(1)}, u32[]{:S(2)}, u32[]{:S(2)}) %collective-permute-start.20) | collective-permute-done | bytes 4128 | tf_op jit(solution)/shard_map/ppermute | solution.py:41
  149.1 4.5 %collective-permute-start.21 = (f32[8,128]{1,0:T(8,128)S(1)}, f32[8,128]{1,0:T(8,128)S(1)}, u32[]{:S(2)}, u32[]{:S(2)}) collective-permute-start(f32[8,128]{1,0:T(8,128)S(1)} %add.125), channel_id=1, source_target_pairs={{1,5},{3,7},{5,1},{7,3},{9,13},{11,15},{13,9},{15,11},{17,21},{19,... | collective-permute-start | bytes 12296 | tf_op jit(solution)/shard_map/ppermute | solution.py:41
  163.9 2.1 %add_multiply_fusion = f32[128,1024]{1,0:T(8,128)} fusion(f32[128,1024]{1,0:T(8,128)} %convert_add_fusion.1, f32[128,1024]{1,0:T(8,128)} %collective-permute-done.34, f32[]{:T(128)S(6)} %mul.35), kind=kLoop, calls=%fused_computation.6 | loop fusion | flops 262144 | bytes 1572868 | tf_op jit(solution)/shard_map/mul | solution.py:423
  (102 shorter events, 40.1 us)
Async XLA Ops:
  1.9 11.3 %collective-permute-start.7 = (bf16[128,1024]{1,0:T(8,128)(2,1)S(1)}, bf16[128,1024]{1,0:T(8,128)(2,1)S(1)}, u32[]{:S(2)}, u32[]{:S(2)}) collective-permute-start(bf16[128,1024]{1,0:T(8,128)(2,1)S(1)} %convert_element_type.88.own), channel_id=1, source_target_pairs={{0,192},{1,65},{2,194},{3,67},{4,196},{5,69},{6,198},{7,71},{8,200... | collective-permute-start | bytes 786440 | tf_op jit(solution)/shard_map/ppermute | solution.py:41
  5.8 12.0 %collective-permute-start.6 = (bf16[128,1024]{1,0:T(8,128)(2,1)S(1)}, bf16[128,1024]{1,0:T(8,128)(2,1)S(1)}, u32[]{:S(2)}, u32[]{:S(2)}) collective-permute-start(bf16[128,1024]{1,0:T(8,128)(2,1)S(1)} %convert_element_type.88.own), channel_id=1, source_target_pairs={{0,224},{1,33},{2,226},{3,35},{4,228},{5,37},{6,230},{7,39},{8,232... | collective-permute-start | bytes 786440 | tf_op jit(solution)/shard_map/ppermute | solution.py:41
  13.2 7.8 %collective-permute-start.8 = (bf16[128,1024]{1,0:T(8,128)(2,1)S(1)}, bf16[128,1024]{1,0:T(8,128)(2,1)S(1)}, u32[]{:S(2)}, u32[]{:S(2)}) collective-permute-start(bf16[128,1024]{1,0:T(8,128)(2,1)S(1)} %collective-permute-done.7), channel_id=1, source_target_pairs={{0,224},{1,33},{2,226},{3,35},{4,228},{5,37},{6,230},{7,39},{8,232... | collective-permute-start | bytes 786440 | tf_op jit(solution)/shard_map/ppermute | solution.py:41
  16.2 8.2 %collective-permute-start.9 = (bf16[64,1024]{1,0:T(8,128)(2,1)S(1)}, bf16[64,1024]{1,0:T(8,128)(2,1)S(1)}, u32[]{:S(2)}, u32[]{:S(2)}) collective-permute-start(bf16[64,1024]{1,0:T(8,128)(2,1)S(1)} %constant_dynamic-slice_fusion), channel_id=1, source_target_pairs={{0,192},{1,65},{2,194},{3,67},{4,196},{5,69},{6,198},{7,71},{8,200... | collective-permute-start | bytes 393224 | tf_op jit(solution)/shard_map/ppermute | solution.py:41
  25.1 33.6 %collective-permute-start.10 = (bf16[448,1024]{1,0:T(8,128)(2,1)}, bf16[448,1024]{1,0:T(8,128)(2,1)}, u32[]{:S(2)}, u32[]{:S(2)}) collective-permute-start(bf16[448,1024]{1,0:T(8,128)(2,1)} %constant_dynamic-update-slice_fusion.near), channel_id=1, source_target_pairs={{0,1},{1,0},{2,3},{3,2},{4,5},{5,4},{6,7},{7,6},{8,9},{9,8},{10,11... | collective-permute-start | bytes 2752520 | tf_op jit(solution)/shard_map/ppermute | solution.py:41
  28.8 29.9 %collective-permute-start = (bf16[272,1024]{1,0:T(8,128)(2,1)S(1)}, bf16[272,1024]{1,0:T(8,128)(2,1)S(1)}, u32[]{:S(2)}, u32[]{:S(2)}) collective-permute-start(bf16[272,1024]{1,0:T(8,128)(2,1)S(1)} %pad_maximum_fusion.h0), channel_id=1, source_target_pairs={{0,24},{1,25},{2,26},{3,27},{4,28},{5,29},{6,30},{7,31},{8,0},{9,1... | collective-permute-start | bytes 1671176 | tf_op jit(solution)/shard_map/ppermute | solution.py:41
  29.9 28.8 %collective-permute-start.1 = (bf16[272,1024]{1,0:T(8,128)(2,1)S(1)}, bf16[272,1024]{1,0:T(8,128)(2,1)}, u32[]{:S(2)}, u32[]{:S(2)}) collective-permute-start(bf16[272,1024]{1,0:T(8,128)(2,1)S(1)} %pad_maximum_fusion.h0), channel_id=1, source_target_pairs={{0,8},{1,9},{2,10},{3,11},{4,12},{5,13},{6,14},{7,15},{8,16},{9,17... | collective-permute-start | bytes 1671176 | tf_op jit(solution)/shard_map/ppermute | solution.py:41
  30.4 17.2 %collective-permute-start.2 = (bf16[80,1024]{1,0:T(8,128)(2,1)S(1)}, bf16[80,1024]{1,0:T(8,128)(2,1)S(1)}, u32[]{:S(2)}, u32[]{:S(2)}) collective-permute-start(bf16[80,1024]{1,0:T(8,128)(2,1)S(1)} %pad_maximum_fusion.2), channel_id=1, source_target_pairs={{0,16},{1,17},{2,18},{3,19},{4,20},{5,21},{6,22},{7,23},{8,24},{9,... | collective-permute-start | bytes 491528 | tf_op jit(solution)/shard_map/ppermute | solution.py:41
  48.2 4.7 %collective-permute-start.3 = (bf16[64,1024]{1,0:T(8,128)(2,1)}, bf16[64,1024]{1,0:T(8,128)(2,1)S(1)}, u32[]{:S(2)}, u32[]{:S(2)}) collective-permute-start(bf16[64,1024]{1,0:T(8,128)(2,1)} %slice.49), channel_id=1, source_target_pairs={{0,6},{1,7},{2,0},{3,1},{4,2},{5,3},{6,4},{7,5},{8,14},{9,15},{10,... | collective-permute-start | bytes 393224 | tf_op jit(solution)/shard_map/ppermute | solution.py:41
  50.7 5.3 %collective-permute-start.4 = (bf16[64,1024]{1,0:T(8,128)(2,1)}, bf16[64,1024]{1,0:T(8,128)(2,1)}, u32[]{:S(2)}, u32[]{:S(2)}) collective-permute-start(bf16[64,1024]{1,0:T(8,128)(2,1)} %slice.49), channel_id=1, source_target_pairs={{0,2},{1,3},{2,4},{3,5},{4,6},{5,7},{6,0},{7,1},{8,10},{9,11},{10,... | collective-permute-start | bytes 393224 | tf_op jit(solution)/shard_map/ppermute | solution.py:41
  53.0 5.7 %collective-permute-start.5 = (bf16[64,1024]{1,0:T(8,128)(2,1)}, bf16[64,1024]{1,0:T(8,128)(2,1)}, u32[]{:S(2)}, u32[]{:S(2)}) collective-permute-start(bf16[64,1024]{1,0:T(8,128)(2,1)} %slice.49), channel_id=1, source_target_pairs={{0,4},{1,5},{2,6},{3,7},{4,0},{5,1},{6,2},{7,3},{8,12},{9,13},{10,... | collective-permute-start | bytes 393224 | tf_op jit(solution)/shard_map/ppermute | solution.py:41
  70.2 3.9 %collective-permute-start.11 = (f32[8,1024]{1,0:T(8,128)S(1)}, f32[8,1024]{1,0:T(8,128)S(1)}, u32[]{:S(2)}, u32[]{:S(2)}) collective-permute-start(f32[8,1024]{1,0:T(8,128)S(1)} %get-tuple-element.17), channel_id=1, source_target_pairs={{0,1},{1,0},{2,3},{3,2},{4,5},{5,4},{6,7},{7,6},{8,9},{9,8},{10,11... | collective-permute-start | bytes 98312 | tf_op jit(solution)/shard_map/ppermute | solution.py:41
  74.7 5.6 %collective-permute-start.12 = (f32[8,1024]{1,0:T(8,128)S(1)}, f32[8,1024]{1,0:T(8,128)S(1)}, u32[]{:S(2)}, u32[]{:S(2)}) collective-permute-start(f32[8,1024]{1,0:T(8,128)S(1)} %shard_map.59.own), channel_id=1, source_target_pairs={{0,24},{1,193},{2,26},{3,195},{4,28},{5,197},{6,30},{7,199},{8,0},... | collective-permute-start | bytes 98312 | tf_op jit(solution)/shard_map/ppermute | solution.py:41
  78.1 5.2 %collective-permute-start.13 = (f32[8,1024]{1,0:T(8,128)S(1)}, f32[8,1024]{1,0:T(8,128)S(1)}, u32[]{:S(2)}, u32[]{:S(2)}) collective-permute-start(f32[8,1024]{1,0:T(8,128)S(1)} %shard_map.59.own), channel_id=1, source_target_pairs={{0,8},{1,65},{2,10},{3,67},{4,12},{5,69},{6,14},{7,71},{8,16},{9,7... | collective-permute-start | bytes 98312 | tf_op jit(solution)/shard_map/ppermute | solution.py:41
  78.1 6.7 %collective-permute-start.14 = (f32[8,1024]{1,0:T(8,128)S(1)}, f32[8,1024]{1,0:T(8,128)S(1)}, u32[]{:S(2)}, u32[]{:S(2)}) collective-permute-start(f32[8,1024]{1,0:T(8,128)S(1)} %shard_map.59.own), channel_id=1, source_target_pairs={{0,16},{1,129},{2,18},{3,131},{4,20},{5,133},{6,22},{7,135},{8,24}... | collective-permute-start | bytes 98312 | tf_op jit(solution)/shard_map/ppermute | solution.py:41
  84.8 2.8 %collective-permute-start.15 = (f32[8,1024]{1,0:T(8,128)S(1)}, f32[8,1024]{1,0:T(8,128)S(1)}, u32[]{:S(2)}, u32[]{:S(2)}) collective-permute-start(f32[8,1024]{1,0:T(8,128)S(1)} %shard_map.60.own), channel_id=1, source_target_pairs={{0,6},{1,33},{2,0},{3,35},{4,2},{5,37},{6,4},{7,39},{8,14},{9,41},... | collective-permute-start | bytes 98312 | tf_op jit(solution)/shard_map/ppermute | solution.py:41
  88.4 8.9 %collective-permute-start.23 = (f32[8,1024]{1,0:T(8,128)S(1)}, f32[8,1024]{1,0:T(8,128)S(1)}, u32[]{:S(2)}, u32[]{:S(2)}) collective-permute-start(f32[8,1024]{1,0:T(8,128)S(1)} %shard_map.61.mine), channel_id=1, source_target_pairs={{0,1},{1,0},{2,3},{3,2},{4,5},{5,4},{6,7},{7,6},{8,9},{9,8},{10,11... | collective-permute-start | bytes 98312 | tf_op jit(solution)/shard_map/ppermute | solution.py:41
  109.4 14.4 %collective-permute-start.31 = (f16[256,1024]{1,0:T(8,128)(2,1)}, f16[256,1024]{1,0:T(8,128)(2,1)}, u32[]{:S(2)}, u32[]{:S(2)}) collective-permute-start(f16[256,1024]{1,0:T(8,128)(2,1)} %pad_maximum_fusion.1), channel_id=1, source_target_pairs={{0,32},{1,225},{2,34},{3,227},{4,36},{5,229},{6,38},{7,231},{8,40}... | collective-permute-start | bytes 1572872 | tf_op jit(solution)/shard_map/ppermute | solution.py:41
  112.5 9.1 %collective-permute-start.18 = (f32[8,128]{1,0:T(8,128)S(1)}, f32[8,128]{1,0:T(8,128)S(1)}, u32[]{:S(2)}, u32[]{:S(2)}) collective-permute-start(f32[8,128]{1,0:T(8,128)S(1)} %mul.31), channel_id=1, source_target_pairs={{0,32},{1,9},{2,34},{3,11},{4,36},{5,13},{6,38},{7,15},{8,40},{9,1... | collective-permute-start | bytes 12296 | tf_op jit(solution)/shard_map/ppermute | solution.py:41
  117.3 15.1 %collective-permute-start.24 = (f16[256,1024]{1,0:T(8,128)(2,1)S(1)}, f16[256,1024]{1,0:T(8,128)(2,1)S(1)}, u32[]{:S(2)}, u32[]{:S(2)}) collective-permute-start(f16[256,1024]{1,0:T(8,128)(2,1)S(1)} %convert_element_type.89), channel_id=1, source_target_pairs={{0,16},{1,5},{2,18},{3,7},{4,20},{5,1},{6,22},{7,3},{8,24},{9,13},... | collective-permute-start | bytes 1572872 | tf_op jit(solution)/shard_map/ppermute | solution.py:41
  118.6 13.9 %collective-permute-start.25 = (f16[256,1024]{1,0:T(8,128)(2,1)S(1)}, f16[256,1024]{1,0:T(8,128)(2,1)S(1)}, u32[]{:S(2)}, u32[]{:S(2)}) collective-permute-start(f16[256,1024]{1,0:T(8,128)(2,1)S(1)} %convert_element_type.91), channel_id=1, source_target_pairs={{0,8},{1,3},{2,10},{3,5},{4,12},{5,7},{6,14},{7,1},{8,16},{9,11},{... | collective-permute-start | bytes 1572872 | tf_op jit(solution)/shard_map/ppermute | solution.py:41
  121.1 12.0 %collective-permute-start.26 = (f16[256,1024]{1,0:T(8,128)(2,1)S(1)}, f16[256,1024]{1,0:T(8,128)(2,1)S(1)}, u32[]{:S(2)}, u32[]{:S(2)}) collective-permute-start(f16[256,1024]{1,0:T(8,128)(2,1)S(1)} %convert_element_type.93), channel_id=1, source_target_pairs={{0,24},{1,7},{2,26},{3,1},{4,28},{5,3},{6,30},{7,5},{8,0},{9,15},{... | collective-permute-start | bytes 1572872 | tf_op jit(solution)/shard_map/ppermute | solution.py:41
  121.6 24.6 %collective-permute-start.19 = (f32[8,128]{1,0:T(8,128)S(1)}, f32[8,128]{1,0:T(8,128)S(1)}, u32[]{:S(2)}, u32[]{:S(2)}) collective-permute-start(f32[8,128]{1,0:T(8,128)S(1)} %broadcast_add_fusion), channel_id=1, source_target_pairs={{0,64},{1,17},{2,66},{3,19},{4,68},{5,21},{6,70},{7,23},{8,72},{9,... | collective-permute-start | bytes 12296 | tf_op jit(solution)/shard_map/ppermute | solution.py:41
  123.8 5.1 %collective-permute-start.32 = (f16[64,1024]{1,0:T(8,128)(2,1)S(1)}, f16[64,1024]{1,0:T(8,128)(2,1)S(1)}, u32[]{:S(2)}, u32[]{:S(2)}) collective-permute-start(f16[64,1024]{1,0:T(8,128)(2,1)S(1)} %slice.58), channel_id=1, source_target_pairs={{0,64},{1,193},{2,66},{3,195},{4,68},{5,197},{6,70},{7,199},{8,72}... | collective-permute-start | bytes 393224 | tf_op jit(solution)/shard_map/ppermute | solution.py:41
  129.0 9.3 %collective-permute-start.33 = (f16[128,1024]{1,0:T(8,128)(2,1)S(1)}, f16[128,1024]{1,0:T(8,128)(2,1)S(1)}, u32[]{:S(2)}, u32[]{:S(2)}) collective-permute-start(f16[128,1024]{1,0:T(8,128)(2,1)S(1)} %convert_element_type.109), channel_id=1, source_target_pairs={{0,64},{1,193},{2,66},{3,195},{4,68},{5,197},{6,70},{7,199},{8,72}... | collective-permute-start | bytes 786440 | tf_op jit(solution)/shard_map/ppermute | solution.py:41
  140.1 23.8 %collective-permute-start.34 = (f32[128,1024]{1,0:T(8,128)}, f32[128,1024]{1,0:T(8,128)}, u32[]{:S(2)}, u32[]{:S(2)}) collective-permute-start(f32[128,1024]{1,0:T(8,128)} %convert_add_fusion.1), channel_id=1, source_target_pairs={{0,1},{1,0},{2,3},{3,2},{4,5},{5,4},{6,7},{7,6},{8,9},{9,8},{10,11... | collective-permute-start | bytes 1572872 | tf_op jit(solution)/shard_map/ppermute | solution.py:41
  143.2 18.9 %collective-permute-start.27 = (f16[64,1024]{1,0:T(8,128)(2,1)}, f16[64,1024]{1,0:T(8,128)(2,1)}, u32[]{:S(2)}, u32[]{:S(2)}) collective-permute-start(f16[64,1024]{1,0:T(8,128)(2,1)} %get-tuple-element.33), channel_id=1, source_target_pairs={{0,4},{1,17},{2,6},{3,19},{4,0},{5,21},{6,2},{7,23},{8,12},{9,25},... | collective-permute-start | bytes 393224 | tf_op jit(solution)/shard_map/ppermute | solution.py:41
  143.5 18.5 %collective-permute-start.28 = (f16[64,1024]{1,0:T(8,128)(2,1)}, f16[64,1024]{1,0:T(8,128)(2,1)}, u32[]{:S(2)}, u32[]{:S(2)}) collective-permute-start(f16[64,1024]{1,0:T(8,128)(2,1)} %get-tuple-element.35), channel_id=1, source_target_pairs={{0,2},{1,9},{2,4},{3,11},{4,6},{5,13},{6,0},{7,15},{8,10},{9,17},{... | collective-permute-start | bytes 393224 | tf_op jit(solution)/shard_map/ppermute | solution.py:41
  143.6 18.5 %collective-permute-start.29 = (f16[64,1024]{1,0:T(8,128)(2,1)S(1)}, f16[64,1024]{1,0:T(8,128)(2,1)}, u32[]{:S(2)}, u32[]{:S(2)}) collective-permute-start(f16[64,1024]{1,0:T(8,128)(2,1)S(1)} %get-tuple-element.34), channel_id=1, source_target_pairs={{0,6},{1,25},{2,0},{3,27},{4,2},{5,29},{6,4},{7,31},{8,14},{9,1},{... | collective-permute-start | bytes 393224 | tf_op jit(solution)/shard_map/ppermute | solution.py:41
  146.2 2.9 %collective-permute-start.20 = (f32[8,128]{1,0:T(8,128)S(1)}, f32[8,128]{1,0:T(8,128)S(1)}, u32[]{:S(2)}, u32[]{:S(2)}) collective-permute-start(f32[8,128]{1,0:T(8,128)S(1)} %fusion.15), channel_id=1, source_target_pairs={{0,128},{1,3},{2,130},{3,1},{4,132},{5,7},{6,134},{7,5},{8,136},{9... | collective-permute-start | bytes 12296 | tf_op jit(solution)/shard_map/ppermute | solution.py:41
  149.1 6.1 %collective-permute-start.21 = (f32[8,128]{1,0:T(8,128)S(1)}, f32[8,128]{1,0:T(8,128)S(1)}, u32[]{:S(2)}, u32[]{:S(2)}) collective-permute-start(f32[8,128]{1,0:T(8,128)S(1)} %add.125), channel_id=1, source_target_pairs={{1,5},{3,7},{5,1},{7,3},{9,13},{11,15},{13,9},{15,11},{17,21},{19,... | collective-permute-start | bytes 12296 | tf_op jit(solution)/shard_map/ppermute | solution.py:41
  155.3 2.6 %collective-permute-start.22 = (f32[8,128]{1,0:T(8,128)S(1)}, f32[8,128]{1,0:T(8,128)S(1)}, u32[]{:S(2)}, u32[]{:S(2)}) collective-permute-start(f32[8,128]{1,0:T(8,128)S(1)} %add.126), channel_id=1, source_target_pairs={{0,1},{1,0},{2,3},{3,2},{4,5},{5,4},{6,7},{7,6},{8,9},{9,8},{10,11... | collective-permute-start | bytes 12296 | tf_op jit(solution)/shard_map/ppermute | solution.py:41
  (8 other events, 70.8 us)

commit v2 on v1

v2 whole, which is shorter than its diff:
```python
import functools

import jax
import jax.numpy as jnp
from jax import lax
from jax.experimental import pallas as pl
from jax.experimental.pallas import tpu as pltpu
from jax.sharding import Mesh
from jax.sharding import PartitionSpec as P

logit_scaling = 0.07
far_below = -1e30
head_room = 3.5
tiny = 1e-30
AXES = ("z", "y", "col", "depth")
NZ, NY, NX = 8, 4, 4
FEATURES = 1024
GROUP = 64
BLOCK = 128
TILE = 1024
BF = jnp.bfloat16
F32 = jnp.float32
WIRE = jnp.float16
VMEM = pltpu.VMEM
SMEM = pltpu.SMEM


def index_of(z, y, x, c):
    return ((z % NZ * NY + y % NY) * NX + x % NX) * 2 + c


def moved(value, target):
    pairs = []
    for z in range(NZ):
        for y in range(NY):
            for x in range(NX):
                for c in range(2):
                    to = target(z, y, x, c)
                    if to is not None:
                        pairs.append((index_of(z, y, x, c), index_of(*to)))
    return lax.ppermute(value, AXES, pairs)


def swapped(value):
    return moved(value, lambda z, y, x, c: (z, y, x, 1 - c))


def from_y(value, by):
    return moved(value, lambda z, y, x, c: (z, y - by, x, c))


def from_x(value, by):
    return moved(value, lambda z, y, x, c: (z, y, x - by, c))


def along_z(value, by):
    return moved(value, lambda z, y, x, c: (z + by if c == 0 else z - by, y, x, c))


def call(kernel, outs, *args, limit=12 << 20, scratch=(), us=1.0):
    specs = [pl.BlockSpec(memory_space=SMEM if arg.ndim == 1 else VMEM) for arg in args]
    return pl.pallas_call(
        kernel,
        in_specs=specs,
        out_specs=[pl.BlockSpec(memory_space=VMEM) for _ in outs],
        out_shape=[jax.ShapeDtypeStruct(shape, dtype) for shape, dtype in outs],
        scratch_shapes=scratch,
        cost_estimate=pl.CostEstimate(
            flops=int(us * 1.1e9), bytes_accessed=int(us * 3e6), transcendentals=0
        ),
        compiler_params=pltpu.CompilerParams(vmem_limit_bytes=limit),
    )(*args)


def place_rows(ref, offset, rows):
    ref[pl.ds(pl.multiple_of(offset, GROUP), GROUP), :] = rows


def column(row):
    return jnp.transpose(jnp.broadcast_to(row, (BLOCK, BLOCK)))


def line(col):
    return jnp.transpose(jnp.broadcast_to(col, (BLOCK, BLOCK)))[0:1, :]


WAYS = (-1, -3, -2, 4, 1, 3, 2, 0)


def slot_z(slot, z, c):
    return (z + (1 - 2 * c) * WAYS[slot] + NZ) % NZ


def positives(place, own, full, far, pair):
    y, x, c = place[1], place[2], place[3]
    positive = jnp.zeros((8, TILE), F32)
    for ref, by, start in (
        (own, 0, 512),
        (full, 1 + 2 * c, 512),
        (far, 3 - 2 * c, 258),
        (pair, 2, 128),
    ):
        base = start // 16 * 16
        coded = ref[base : base + 16, :].astype(F32)
        at = start - base
        number = jnp.broadcast_to(
            coded[at : at + 1, :] * 128.0 + coded[at + 1 : at + 2, :], (8, TILE)
        )
        shift = jnp.where(c == 0, by * 256, (y + by) % NY * 64 + TILE - x * 256)
        positive = positive + pltpu.roll(number, shift % TILE, 1)
    return positive[0:1, :].astype(jnp.int32)


def largest(ref):
    best = jnp.abs(ref[0:16, :])
    for start in range(16, TILE, 16):
        best = jnp.maximum(best, jnp.abs(ref[start : start + 16, :]))
    return jnp.max(best.astype(F32))


def coded_matches(place, matches):
    c = place[3]
    lane = lax.broadcasted_iota(jnp.int32, (8, TILE), 1)
    at = lax.broadcasted_iota(jnp.int32, (8, TILE), 0)
    coded = jnp.zeros((8, TILE), F32)
    for step in range(2):
        which = c if step == 0 else 1 - c
        wide = jnp.zeros((8, TILE), F32)
        for xx in range(NX):
            line_of = jnp.concatenate(
                [
                    jnp.broadcast_to(matches[xx : xx + 1, :].astype(F32), (8, BLOCK)),
                    jnp.zeros((8, TILE - BLOCK), F32),
                ],
                axis=1,
            )
            mine = jnp.logical_and(lane >= which * GROUP, lane < which * GROUP + GROUP)
            shift = TILE - which * GROUP + xx * jnp.where(which == 0, 64, 256)
            wide = wide + pltpu.roll(jnp.where(mine, line_of, 0.0), shift % TILE, 1)
        high = jnp.floor(wide * (1.0 / 128.0))
        low = wide - high * 128.0
        coded = jnp.where(at == 2 * step, high, jnp.where(at == 2 * step + 1, low, coded))
    return jnp.concatenate([coded, jnp.zeros((8, TILE), F32)], axis=0).astype(BF)


def part_kernel(place, regions, matches, part):
    x, c = place[2], place[3]
    for at in range(2):
        start = pl.multiple_of(((x % 2 * 2 + at) * 2 + c) * GROUP, GROUP)
        part[at * GROUP : (at + 1) * GROUP, :] = regions[pl.ds(start, GROUP), :].astype(BF)
    part[128:144, :] = coded_matches(place, matches)


def whole_kernel(place, regions, part, whole):
    c = place[3]
    whole[512:528, :] = part[128:144, :]
    for step in range(2):
        which = c if step == 0 else 1 - c
        for xx in range(NX):
            start = pl.multiple_of((xx * 2 + which) * GROUP, GROUP)
            to = (step * NX + xx) * GROUP
            whole[to : to + GROUP, :] = regions[pl.ds(start, GROUP), :].astype(BF)


def text_kernel(captions, text):
    text[...] = captions[...].astype(BF)


def skip_kernel(place, one, two, out):
    out[0:128, :] = one[...]
    out[128:192, :] = two[pl.ds(pl.multiple_of(place[3] * GROUP, GROUP), GROUP), :]


def score_kernel(
    place, own, full, far, pair, other, text, one, two, skip, s_out, r_out, c_out, keep, give
):
    z, y, x, c = place[0], place[1], place[2], place[3]

    def put(by, xx, rows):
        offset = jnp.where(
            c == 0, by * 256 + xx * 64, (xx + NX - x) % NX * 256 + (y + by) % NY * 64
        )
        place_rows(r_out, offset, rows)

    for ref, by in ((own, 0), (full, 1 + 2 * c), (far, 3 - 2 * c)):
        for xx in range(NX):
            put(by, xx, ref[xx * GROUP : (xx + 1) * GROUP, :])
    for at in range(2):
        rows = pl.ds(at * GROUP, GROUP)
        put(2, x % 2 * 2 + at, pair[rows, :])
        put(2, (1 - x % 2) * 2 + at, other[rows, :])
    c_out[0:128, :] = far[272:400, :]
    c_out[128:256, :] = far[528:656, :]
    c_out[256:384, :] = far[400:528, :]
    place_rows(c_out, 384 + c * GROUP, skip[128:192, :])
    place_rows(c_out, 384 + (1 - c) * GROUP, far[656:720, :])
    c_out[512:640, :] = one[...]
    c_out[640:768, :] = skip[0:128, :]
    c_out[768:896, :] = two[...]
    c_out[896:1024, :] = text[...]

    positive = positives(place, own, full, far, pair)
    regions = r_out[...]
    for part in range(2):
        chunk = pl.ds(part * 512, 512)
        s_out[chunk, :] = lax.dot_general(
            c_out[chunk, :], regions, (((1,), (1,)), ((), ())), preferred_element_type=F32
        ) * (1.0 / logit_scaling)

    row_max = jnp.full((1, TILE), far_below, F32)
    row_sum = jnp.zeros((1, TILE), F32)
    matched = jnp.zeros((1, TILE), F32)
    ids = lax.broadcasted_iota(jnp.int32, (BLOCK, TILE), 0)
    for slot in range(8):
        scores = s_out[slot * BLOCK : (slot + 1) * BLOCK, :]
        owner = slot_z(slot, z, c)
        first = ((owner * NY + y) * NX + x) * BLOCK
        matched = matched + jnp.sum(
            jnp.where(ids == positive - first, scores, 0.0), axis=0, keepdims=True
        )
        new_max = jnp.maximum(row_max, jnp.max(scores, axis=0, keepdims=True))
        row_sum = row_sum * jnp.exp(row_max - new_max) + jnp.sum(
            jnp.exp(scores - new_max), axis=0, keepdims=True
        )
        row_max = new_max
        cap_max = jnp.max(scores, axis=1, keepdims=True)
        cap_sum = jnp.sum(jnp.exp(scores - cap_max), axis=1, keepdims=True)
        lanes = pl.ds(pl.multiple_of(owner * BLOCK, BLOCK), BLOCK)
        give[0:1, lanes] = line(cap_max)
        give[2:3, lanes] = line(cap_sum)

    cap_row_max = give[0:1, :]
    cap_row_sum = give[2:3, :]
    total = jnp.broadcast_to(jnp.sum(matched), (1, TILE))
    caption_top = jnp.broadcast_to(largest(c_out), (1, TILE))
    region_top = jnp.broadcast_to(largest(r_out), (1, TILE))
    zero = jnp.zeros((1, TILE), F32)
    two_zeros = jnp.zeros((2, TILE), F32)
    turned = jnp.concatenate([row_max, zero, row_sum, zero, total, caption_top, two_zeros], axis=0)
    turned = pltpu.roll(turned, jnp.where(c == 0, y, x) * 256, 1)
    by_cap = jnp.concatenate(
        [cap_row_max, zero, cap_row_sum, zero, zero, region_top, two_zeros], axis=0
    )
    keep[...] = jnp.where(c == 0, turned, by_cap)
    give[...] = jnp.where(c == 0, by_cap, turned)


def pair_kernel(place, keep, came, out):
    first = place[3] == 0
    m0, m1, s0, s1 = keep[0:1, :], came[0:1, :], keep[2:3, :], came[2:3, :]
    top = jnp.maximum(m0, m1)
    merged = s0 * jnp.exp(m0 - top) + s1 * jnp.exp(m1 - top)
    zero = jnp.zeros((1, TILE), F32)
    out[0:1, :] = jnp.where(first, m0, top)
    out[1:2, :] = jnp.where(first, m1, zero)
    out[2:3, :] = jnp.where(first, s0, merged)
    out[3:4, :] = jnp.where(first, s1, zero)
    out[4:5, :] = keep[4:5, :] + came[4:5, :]
    out[5:6, :] = jnp.maximum(keep[5:6, :], came[5:6, :])
    out[6:8, :] = jnp.zeros((2, TILE), F32)


def merged(own, came):
    top = jnp.maximum(own[0:2, :], came[0:2, :])
    sums = own[2:4, :] * jnp.exp(own[0:2, :] - top) + came[2:4, :] * jnp.exp(came[0:2, :] - top)
    return top, sums, own[4:5, :] + came[4:5, :], jnp.maximum(own[5:6, :], came[5:6, :])


def merge_kernel(own, came, out):
    top, sums, total, peak = merged(own[...], came[...])
    out[0:2, :] = top
    out[2:4, :] = sums
    out[4:5, :] = total
    out[5:6, :] = peak
    out[6:8, :] = jnp.zeros((2, TILE), F32)


def last_kernel(place, own, came, out):
    first = place[3] == 0
    lines = lax.broadcasted_iota(jnp.int32, (8, TILE), 0)
    empty = jnp.where(lines < 2, far_below, 0.0)
    top, sums, total, peak = merged(own[...], jnp.where(first, came[...], empty))
    lse = top + jnp.log(jnp.where(jnp.logical_or(first, lines[0:2, :] == 0), sums, 1.0))
    both = 0.5 * jnp.sum(lse[0:1, :]) + jnp.where(first, 0.5 * jnp.sum(lse[1:2, :]), 0.0)
    out[0:1, :] = lse[0:1, :]
    out[1:2, :] = jnp.where(first, lse[1:2, :], lse[0:1, :])
    out[2:4, :] = jnp.zeros((2, TILE), F32)
    out[4:5, :] = jnp.broadcast_to(both, (1, TILE)) - total
    out[5:6, :] = peak
    out[6:8, :] = jnp.zeros((2, TILE), F32)


def weight_kernel(
    place, scores, regions, mine, came, whole, full, far, pair, w_out, give, kept
):
    z, y, x, c = place[0], place[1], place[2], place[3]
    first_core = c == 0
    row_lse = jnp.where(first_core, mine[0:1, :], came[1:2, :])
    turn = (NX - jnp.where(first_core, y, x)) % NX * 256
    row_lse = pltpu.roll(jnp.broadcast_to(row_lse, (8, TILE)), turn, 1)[0:1, :]
    positive = positives(place, whole, full, far, pair)
    ids = lax.broadcasted_iota(jnp.int32, (BLOCK, TILE), 0)
    for slot in range(8):
        chunk = pl.ds(slot * BLOCK, BLOCK)
        owner = slot_z(slot, z, c)
        lanes = pl.ds(pl.multiple_of(owner * BLOCK, BLOCK), BLOCK)
        cap_line = jnp.where(first_core, came[1:2, lanes], mine[0:1, lanes])
        cap_lse = jnp.concatenate([column(cap_line)] * 8, axis=1)
        first = ((owner * NY + y) * NX + x) * BLOCK
        s = scores[chunk, :]
        weight = 0.5 * (jnp.exp(s - row_lse) + jnp.exp(s - cap_lse))
        weight = weight - jnp.where(ids == positive - first, 1.0, 0.0)
        w_out[chunk, :] = weight.astype(BF)
    scale = region_scale(place, mine, came)
    part = jnp.dot(w_out[0:512, :], regions[...], preferred_element_type=F32) * scale
    nothing = jnp.zeros((16, TILE), F32)
    for at in range(3):
        start = at * 144
        give[start : start + 128, :] = part[at * 128 : (at + 1) * 128, :]
        give[start + 128 : start + 144, :] = nothing
    give[432:496, :] = jnp.where(first_core, part[448:512, :], part[384:448, :])
    give[496:512, :] = nothing
    kept[0:64, :] = jnp.where(first_core, part[384:448, :], part[448:512, :])
    kept[64:80, :] = digits(jnp.where(first_core, mine[4:5, :], came[4:5, :]), z)


def digits(value, index):
    high = jnp.floor(value * 2.0**-20)
    rest = value - high * 2.0**20
    middle = jnp.floor(rest * 2.0**-10)
    rest = rest - middle * 2.0**10
    low = jnp.floor(rest)
    last = jnp.floor((rest - low) * 2.0**10)
    lane = lax.broadcasted_iota(jnp.int32, (16, TILE), 1)
    line_at = lax.broadcasted_iota(jnp.int32, (16, TILE), 0)
    which = lane // 16
    digit = jnp.where(
        which == 0, high, jnp.where(which == 1, middle, jnp.where(which == 2, low, last))
    )
    here = jnp.logical_and(line_at == 0, jnp.logical_and(lane < 64, lane % 16 == index))
    return jnp.where(here, digit, 0.0)


def region_scale(place, mine, came):
    region_top = jnp.where(place[3] == 0, came[5:6, :], mine[5:6, :])
    return head_room / jnp.maximum(region_top, tiny)


def caption_kernel(place, weights, regions, mine, came, near_two, second, own):
    first_core = place[3] == 0
    part = jnp.dot(
        weights[512:1024, :], regions[...], preferred_element_type=F32
    ) * region_scale(place, mine, came)
    code = digits(jnp.where(first_core, mine[4:5, :], came[4:5, :]), place[0])
    near_two[0:128, :] = part[0:128, :]
    near_two[128:144, :] = code
    near_two[144:272, :] = part[128:256, :]
    near_two[272:288, :] = code
    second[0:128, :] = part[256:384, :]
    second[128:144, :] = code
    own[0:128, :] = part[384:512, :]
    own[128:144, :] = jnp.where(first_core, code, 0.0)


def region_kernel(place, weights, captions, mine, came, o0, o1, o2, o3):
    first_core = place[3] == 0
    caption_top = jnp.where(first_core, mine[5:6, :], came[5:6, :])
    scale = head_room / jnp.maximum(caption_top, tiny)
    code = digits(
        jnp.where(first_core, came[4:5, :], mine[4:5, :]), place[1] * NX + place[2]
    )
    part = lax.dot_general(
        weights[...], captions[...], (((0,), (0,)), ((), ())), preferred_element_type=F32
    )
    for by, ref in enumerate((o0, o1, o2, o3)):
        ref[0:256, :] = part[by * 256 : (by + 1) * 256, :] * scale
        ref[256:272, :] = code


def shards(regions, captions, positive):
    z = lax.axis_index("z")
    y = lax.axis_index("y")
    x = lax.axis_index("col")
    c = lax.axis_index("depth")
    place = jnp.stack([z, y, x, c]).astype(jnp.int32)
    first_core = c == 0
    big = (TILE, FEATURES)

    (part,) = call(
        part_kernel, [((144, FEATURES), BF)], place, regions, positive.reshape(NX, BLOCK)
    )
    (whole,) = call(whole_kernel, [((528, FEATURES), BF)], place, regions, part, us=40.0)
    (text,) = call(text_kernel, [((BLOCK, FEATURES), BF)], captions)

    full = moved(whole, lambda z, y, x, c: (z, y - 1 if c == 0 else y + 1, x, c))
    pair = from_y(part, 2)
    other = moved(pair[0:128], lambda z, y, x, c: (z, y, x ^ 1, c))
    one = along_z(text, -1)
    two = along_z(text, -2)
    (passed,) = call(skip_kernel, [((192, FEATURES), BF)], place, one, two, us=40.0)
    skip = along_z(passed, -2)
    full, other, skip = lax.optimization_barrier((full, other, skip))
    far = swapped(jnp.concatenate([full[256:528], one, two, skip], axis=0))

    scores, region_rows, caption_rows, keep, give = call(
        score_kernel,
        [(big, F32), (big, BF), (big, BF), ((8, TILE), F32), ((8, TILE), F32)],
        place, whole, full, far, pair, other, text, one, two, skip,
        us=8.0,
    )

    small = [((8, TILE), F32)]
    (stats,) = call(pair_kernel, small, place, keep, swapped(give))

    def partner(bit):
        def target(z, y, x, c):
            if c == 1:
                return (z ^ (1 << bit), y, x, c) if bit < 3 else None
            return (z, y ^ (1 << bit), x, c) if bit < 2 else (z, y, x ^ (1 << (bit - 2)), c)

        return target

    for bit in range(3):
        (stats,) = call(merge_kernel, small, stats, moved(stats, partner(bit)))
    (lse,) = call(last_kernel, small, place, stats, moved(stats, partner(3)))
    came = swapped(lse)

    weights, give, kept_half = call(
        weight_kernel,
        [(big, BF), ((512, FEATURES), F32), ((80, FEATURES), F32)],
        place, scores, region_rows, lse, came, whole, full, far, pair,
        us=40.0,
    )
    got = swapped(give.astype(WIRE))
    near_two, second, own = call(
        caption_kernel,
        [((288, FEATURES), F32), ((144, FEATURES), F32), ((144, FEATURES), F32)],
        place, weights, region_rows, lse, came,
        us=20.0,
    )
    near_two = (near_two + got[0:288].astype(F32)).astype(WIRE)
    kept_half = (kept_half + got[432:512].astype(F32)).astype(WIRE)
    weights, near_two, kept_half = lax.optimization_barrier((weights, near_two, kept_half))
    ahead = along_z(near_two, 1)
    opposite = along_z(kept_half, 4)
    r0, r1, r2, r3 = call(
        region_kernel, [((272, FEATURES), F32)] * 4, place, weights, caption_rows, lse, came, us=30.0
    )
    r1, r2, r3, ahead = lax.optimization_barrier(
        (r1.astype(WIRE), r2.astype(WIRE), r3.astype(WIRE), ahead)
    )

    def major_from(value, by):
        return moved(
            value, lambda z, y, x, c: (z, y + by, x, c) if c == 0 else (z, y, x + by, c)
        )

    def minor_from(value, by):
        return moved(
            value, lambda z, y, x, c: (z, y, x + by, c) if c == 0 else (z, y + by, x, c)
        )

    onward = (second + got[288:432].astype(F32)) + ahead[144:288].astype(F32)
    passed = along_z(onward.astype(WIRE), 2)
    q2 = major_from(r2, 2)
    q1 = major_from(r1, 1)
    q3 = major_from(r3, 3)
    summed = (r0 + q2.astype(F32)) + (q1.astype(F32) + q3.astype(F32))
    summed, passed, opposite = lax.optimization_barrier((summed, passed, opposite))
    blocks = summed[0:256].reshape(4, GROUP, FEATURES)
    minor = jnp.where(first_core, x, y)

    def piece(by):
        block = lax.dynamic_index_in_dim(blocks, (minor + by) % 4, 0, keepdims=False)
        return jnp.concatenate([block, summed[256:272]], axis=0)

    t2, t1, t3 = (minor_from(piece(by).astype(WIRE), by) for by in (2, 1, 3))
    nothing = jnp.zeros((GROUP, FEATURES), F32)
    late = opposite.astype(F32)
    late = jnp.where(
        first_core,
        jnp.concatenate([late[0:64], nothing, late[64:80]], axis=0),
        jnp.concatenate([nothing, late[0:64], nothing[0:16]], axis=0),
    )
    mine = (own + ahead[0:144].astype(F32)) + (passed.astype(F32) + late)
    both = mine + swapped(mine)
    all_regions = (piece(0) + t2.astype(F32)) + (t1.astype(F32) + t3.astype(F32))

    caption_top = jnp.where(first_core, lse[5:6, :], came[5:6, :])
    region_top = jnp.where(first_core, came[5:6, :], lse[5:6, :])
    unscale = 1.0 / (head_room * logit_scaling)
    region_grad = all_regions[0:64] * (jnp.maximum(caption_top, tiny) * unscale)
    text_derivative = both[0:128] * (jnp.maximum(region_top, tiny) * unscale)
    numbers = both[128:136, 0:128] + all_regions[64:72, 0:128]
    worth = jnp.exp2(20.0 - 10.0 * (jnp.arange(128) // 16).astype(F32))
    worth = jnp.where(jnp.arange(128) < 64, worth, 0.0)
    mean_objective = jnp.sum(numbers * worth[None, :]) / (NZ * NY * regions.shape[0])
    return mean_objective, region_grad, text_derivative


def solution(mesh):
    grid = Mesh(mesh.devices.reshape(NZ, NY, NX, 2), AXES)
    return jax.shard_map(
        shards,
        mesh=grid,
        in_specs=(P(("z", "y"), None), P(("z", "y", "col"), None), P(("z", "y"))),
        out_specs=(
            P(),
            P(("z", "y", "col", "depth"), None),
            P(("z", "y", "col"), None),
        ),
        check_vma=False,
    )
```

time: 168 us -> 123 us (0.73)
  starting transfers between devices: 65.8 us -> 46.4 us
  local copies, waits for them, and re-layouts: 8.43 us -> 1.16 us
  waiting for transfers between devices: 52.1 us -> 44.9 us
  Pallas kernels: 23.1 us -> 16.4 us
  between operations: 5.3 us -> 2.7 us
  other arithmetic: 12.4 us -> 10.7 us
    ppermute x35 -> x24, starting transfers between devices: 65.8 us -> 46.4 us  [moved(): return lax.ppermute(value, AXES, pairs)]
    ppermute x35 -> x24, waiting for transfers between devices: 52.1 us -> 44.9 us  [moved(): return lax.ppermute(value, AXES, pairs)]
    pallas_call x6 -> x13, Pallas kernels: 23.1 us -> 16.4 us  [call(): pl.pallas_call(kernel, in_specs=specs, out_specs=[pl.BlockSpec(memory_spa...]
    slice x6 -> x7, local copies, waits for them, and re-layouts: 2.41 us -> 0.09 us  [the longest x1 0.04 us: shards(): far = swapped(jnp.concatenate([full[256:528], one, two, skip], axis=0))]
    mul x2 -> x3, other arithmetic: 3.88 us -> 1.59 us  [the longest x2 0.87 us: shards(): text_derivative = both[0:128] * (jnp.maximum(region_top, tiny) * unscale)]
    unnamed x15 -> x8, local copies, waits for them, and re-layouts: 3.21 us -> 1.05 us
    convert_element_type x5 -> x6, other arithmetic: 2.19 us -> 3.64 us  [the longest x1 0.91 us: shards(): r3.astype(WIRE)]
    add x9 -> x4, other arithmetic: 3.46 us -> 3.2 us  [the longest x1 1.78 us: shards(): summed = r0 + q2.astype(F32) + (q1.astype(F32) + q3.astype(F32))]
  transfers between devices with their start and end apart: 35 -> 24, of which waited for: 21 -> 17; matrix products, arithmetic and copies ran while one was open for 8% -> 5% of each run, Pallas kernels for 3% -> 5%
where the time goes in v2:
time: 123 us; the launch traced here: 122 us
  starting transfers between devices  46.4 us (38%)
  waiting for transfers between devices  44.9 us (37%)
  Pallas kernels  16.4 us (13%)
  other arithmetic  10.7 us (9%)
  between operations  2.7 us (2%)
    ppermute x24, starting transfers between devices, moved(): return lax.ppermute(value, AXES, pairs)  46.4 us
    ppermute x24, waiting for transfers between devices, moved(): return lax.ppermute(value, AXES, pairs)  44.9 us
    pallas_call x13, Pallas kernels, call(): pl.pallas_call(kernel, in_specs=specs, out_specs=[pl.BlockSpec(memory_spa...  16.4 us
  transfers between devices with their start and end apart: 24, of which 17 were waited for; matrix products, arithmetic and copies ran while one was open for 5% of the time, Pallas kernels for 5%

profile of v2, /device:TPU:1, one launch (start us, length us, event | category | flops | bytes accessed | tf_op | source)
XLA Modules:
  0.0 122.2 jit_solution(15370069330200174618)
XLA Ops:
  1.7 2.5 %collective-permute-start.3 = (bf16[128,1024]{1,0:T(8,128)(2,1)S(1)}, bf16[128,1024]{1,0:T(8,128)(2,1)S(1)}, u32[]{:S(2)}, u32[]{:S(2)}) collective-permute-start(bf16[128,1024]{1,0:T(8,128)(2,1)S(1)} %shard_map.60.text), channel_id=1, source_target_pairs={{0,224},{1,33},{2,226},{3,35},{4,228},{5,37},{6,230},{7,39},{8,232... | collective-permute-start | bytes 786440 | tf_op jit(solution)/shard_map/ppermute | solution.py:41
  4.3 3.0 %collective-permute-start.4 = (bf16[128,1024]{1,0:T(8,128)(2,1)S(1)}, bf16[128,1024]{1,0:T(8,128)(2,1)S(1)}, u32[]{:S(2)}, u32[]{:S(2)}) collective-permute-start(bf16[128,1024]{1,0:T(8,128)(2,1)S(1)} %shard_map.60.text), channel_id=1, source_target_pairs={{0,192},{1,65},{2,194},{3,67},{4,196},{5,69},{6,198},{7,71},{8,200... | collective-permute-start | bytes 786440 | tf_op jit(solution)/shard_map/ppermute | solution.py:41
  8.0 3.0 %collective-permute-start.1 = (bf16[144,1024]{1,0:T(8,128)(2,1)S(1)}, bf16[144,1024]{1,0:T(8,128)(2,1)S(1)}, u32[]{:S(2)}, u32[]{:S(2)}) collective-permute-start(bf16[144,1024]{1,0:T(8,128)(2,1)S(1)} %shard_map.58.part), channel_id=1, source_target_pairs={{0,16},{1,17},{2,18},{3,19},{4,20},{5,21},{6,22},{7,23},{8,24},{9,... | collective-permute-start | bytes 884744 | tf_op jit(solution)/shard_map/ppermute | solution.py:41
  12.1 4.6 %collective-permute-done.4.two = bf16[128,1024]{1,0:T(8,128)(2,1)S(1)} collective-permute-done((bf16[128,1024]{1,0:T(8,128)(2,1)S(1)}, bf16[128,1024]{1,0:T(8,128)(2,1)S(1)}, u32[]{:S(2)}, u32[]{:S(2)}) %collective-permute-start.4) | collective-permute-done | bytes 262176 | tf_op jit(solution)/shard_map/ppermute | solution.py:41
  18.8 4.3 %collective-permute-done.2.other = bf16[128,1024]{1,0:T(8,128)(2,1)S(1)} collective-permute-done((bf16[128,1024]{1,0:T(8,128)(2,1)S(1)}, bf16[128,1024]{1,0:T(8,128)(2,1)S(1)}, u32[]{:S(2)}, u32[]{:S(2)}) %collective-permute-start.2) | collective-permute-done | bytes 262176 | tf_op jit(solution)/shard_map/ppermute | solution.py:41
  23.1 3.2 %collective-permute-done.5.skip = bf16[192,1024]{1,0:T(8,128)(2,1)S(1)} collective-permute-done((bf16[192,1024]{1,0:T(8,128)(2,1)S(1)}, bf16[192,1024]{1,0:T(8,128)(2,1)S(1)}, u32[]{:S(2)}, u32[]{:S(2)}) %collective-permute-start.5) | collective-permute-done | bytes 393248 | tf_op jit(solution)/shard_map/ppermute | solution.py:41
  26.3 4.0 %collective-permute-done.full = bf16[528,1024]{1,0:T(8,128)(2,1)S(1)} collective-permute-done((bf16[528,1024]{1,0:T(8,128)(2,1)S(1)}, bf16[528,1024]{1,0:T(8,128)(2,1)S(1)}, u32[]{:S(2)}, u32[]{:S(2)}) %collective-permute-start) | collective-permute-done | bytes 1081376 | tf_op jit(solution)/shard_map/ppermute | solution.py:41
  30.4 1.4 %collective-permute-start.6 = (bf16[720,1024]{1,0:T(8,128)(2,1)S(1)}, bf16[720,1024]{1,0:T(8,128)(2,1)S(1)}, u32[]{:S(2)}, u32[]{:S(2)}) collective-permute-start(bf16[720,1024]{1,0:T(8,128)(2,1)S(1)} %pad_maximum_fusion), channel_id=1, source_target_pairs={{0,1},{1,0},{2,3},{3,2},{4,5},{5,4},{6,7},{7,6},{8,9},{9,8},{10,11... | collective-permute-start | bytes 4423688 | tf_op jit(solution)/shard_map/ppermute | solution.py:41
  31.9 2.9 %collective-permute-done.6.far = bf16[720,1024]{1,0:T(8,128)(2,1)S(1)} collective-permute-done((bf16[720,1024]{1,0:T(8,128)(2,1)S(1)}, bf16[720,1024]{1,0:T(8,128)(2,1)S(1)}, u32[]{:S(2)}, u32[]{:S(2)}) %collective-permute-start.6) | collective-permute-done | bytes 1474592 | tf_op jit(solution)/shard_map/ppermute | solution.py:41
  34.8 4.9 %shard_map.62 = (f32[1024,1024]{1,0:T(8,128)S(1)}, bf16[1024,1024]{1,0:T(8,128)(2,1)S(1)}, bf16[1024,1024]{1,0:T(8,128)(2,1)S(1)}, f32[8,1024]{1,0:T(8,128)S(1)}, f32[8,1024]{1,0:T(8,128)S(1)}) custom-call(s32[4]{0:T(128)S(1)} %pad_add_fusion.place, bf16[528,1024]{1,0:T(8,128)(2,1)S(1)} %shard_map.59.own.whole, ...), custom_call_target="tpu_custom_call" | custom-call | flops 8800000000 | bytes 24000000 | tf_op jit(solution)/shard_map/pallas_call | solution.py:62
  41.6 2.3 %collective-permute-start.8 = (f32[8,1024]{1,0:T(8,128)S(1)}, f32[8,1024]{1,0:T(8,128)S(1)}, u32[]{:S(2)}, u32[]{:S(2)}) collective-permute-start(f32[8,1024]{1,0:T(8,128)S(1)} %shard_map.63.own), channel_id=1, source_target_pairs={{0,8},{1,33},{2,10},{3,35},{4,12},{5,37},{6,14},{7,39},{8,0},{9,41... | collective-permute-start | bytes 98312 | tf_op jit(solution)/shard_map/ppermute | solution.py:41
  43.9 1.6 %collective-permute-done.8.came = f32[8,1024]{1,0:T(8,128)S(1)} collective-permute-done((f32[8,1024]{1,0:T(8,128)S(1)}, f32[8,1024]{1,0:T(8,128)S(1)}, u32[]{:S(2)}, u32[]{:S(2)}) %collective-permute-start.8) | collective-permute-done | bytes 32800 | tf_op jit(solution)/shard_map/ppermute | solution.py:41
  45.6 2.1 %collective-permute-start.9 = (f32[8,1024]{1,0:T(8,128)S(1)}, f32[8,1024]{1,0:T(8,128)S(1)}, u32[]{:S(2)}, u32[]{:S(2)}) collective-permute-start(f32[8,1024]{1,0:T(8,128)S(1)} %shard_map.64.own), channel_id=1, source_target_pairs={{0,16},{1,65},{2,18},{3,67},{4,20},{5,69},{6,22},{7,71},{8,24},{9,... | collective-permute-start | bytes 98312 | tf_op jit(solution)/shard_map/ppermute | solution.py:41
  47.7 1.6 %collective-permute-done.9.came = f32[8,1024]{1,0:T(8,128)S(1)} collective-permute-done((f32[8,1024]{1,0:T(8,128)S(1)}, f32[8,1024]{1,0:T(8,128)S(1)}, u32[]{:S(2)}, u32[]{:S(2)}) %collective-permute-start.9) | collective-permute-done | bytes 32800 | tf_op jit(solution)/shard_map/ppermute | solution.py:41
  49.3 3.0 %collective-permute-start.10 = (f32[8,1024]{1,0:T(8,128)S(1)}, f32[8,1024]{1,0:T(8,128)S(1)}, u32[]{:S(2)}, u32[]{:S(2)}) collective-permute-start(f32[8,1024]{1,0:T(8,128)S(1)} %shard_map.65.own), channel_id=1, source_target_pairs={{0,2},{1,129},{2,0},{3,131},{4,6},{5,133},{6,4},{7,135},{8,10},{9,... | collective-permute-start | bytes 98312 | tf_op jit(solution)/shard_map/ppermute | solution.py:41
  52.4 3.8 %collective-permute-done.10.came = f32[8,1024]{1,0:T(8,128)S(1)} collective-permute-done((f32[8,1024]{1,0:T(8,128)S(1)}, f32[8,1024]{1,0:T(8,128)S(1)}, u32[]{:S(2)}, u32[]{:S(2)}) %collective-permute-start.10) | collective-permute-done | bytes 32800 | tf_op jit(solution)/shard_map/ppermute | solution.py:41
  57.6 6.2 %collective-permute-start.12 = (f32[8,1024]{1,0:T(8,128)S(1)}, f32[8,1024]{1,0:T(8,128)S(1)}, u32[]{:S(2)}, u32[]{:S(2)}) collective-permute-start(f32[8,1024]{1,0:T(8,128)S(1)} %shard_map.67.mine), channel_id=1, source_target_pairs={{0,1},{1,0},{2,3},{3,2},{4,5},{5,4},{6,7},{7,6},{8,9},{9,8},{10,11... | collective-permute-start | bytes 98312 | tf_op jit(solution)/shard_map/ppermute | solution.py:41
  64.7 3.5 %shard_map.68 = (bf16[1024,1024]{1,0:T(8,128)(2,1)S(1)}, f32[512,1024]{1,0:T(8,128)S(1)}, f32[80,1024]{1,0:T(8,128)S(1)}) custom-call(s32[4]{0:T(128)S(1)} %pad_add_fusion.place, f32[1024,1024]{1,0:T(8,128)S(1)} %get-tuple-element.34.scores, bf16[1024,1024]{1,0:T(8,128)(2,1)S(1)} %get-tuple-element.35.regions, f32[8,1024]{1,0:T(8,128)S(1)} %shard_map.67.mine, ...), custom_call_target="tpu_custom_call" | custom-call | flops 44000002048 | bytes 120000000 | tf_op jit(solution)/shard_map/pallas_call | solution.py:62
  68.8 1.8 %shard_map.69 = (f32[288,1024]{1,0:T(8,128)S(1)}, f32[144,1024]{1,0:T(8,128)S(1)}, f32[144,1024]{1,0:T(8,128)S(1)}) custom-call(s32[4]{0:T(128)S(1)} %pad_add_fusion.place, bf16[1024,1024]{1,0:T(8,128)(2,1)S(1)} %get-tuple-element.43.weights, bf16[1024,1024]{1,0:T(8,128)(2,1)S(1)} %get-tuple-element.35.regions, f32[8,1024]{1,0:T(8,128)S(1)} %shard_map.67.mine, ...), custom_call_target="tpu_custom_call" | custom-call | flops 22000001024 | bytes 60000000 | tf_op jit(solution)/shard_map/pallas_call | solution.py:62
  72.1 4.5 %collective-permute-start.14 = (f16[288,1024]{1,0:T(8,128)(2,1)S(1)}, f16[288,1024]{1,0:T(8,128)(2,1)}, u32[]{:S(2)}, u32[]{:S(2)}) collective-permute-start(f16[288,1024]{1,0:T(8,128)(2,1)S(1)} %add_convert_fusion), channel_id=1, source_target_pairs={{0,32},{1,225},{2,34},{3,227},{4,36},{5,229},{6,38},{7,231},{8,40}... | collective-permute-start | bytes 1769480 | tf_op jit(solution)/shard_map/ppermute | solution.py:41
  76.6 2.9 %shard_map.70 = (f32[272,1024]{1,0:T(8,128)S(1)}, f32[272,1024]{1,0:T(8,128)S(1)}, f32[272,1024]{1,0:T(8,128)S(1)}, f32[272,1024]{1,0:T(8,128)S(1)}) custom-call(s32[4]{0:T(128)S(1)} %pad_add_fusion.place, bf16[1024,1024]{1,0:T(8,128)(2,1)S(1)} %get-tuple-element.43.weights, bf16[1024,1024]{1,0:T(8,128)(2,1)S(1)} %get-tuple-element.44.captions, ...), custom_call_target="tpu_custom_call" | custom-call | flops 32999999488 | bytes 90000000 | tf_op jit(solution)/shard_map/pallas_call | solution.py:62
  83.4 2.7 %collective-permute-start.15 = (f16[272,1024]{1,0:T(8,128)(2,1)}, f16[272,1024]{1,0:T(8,128)(2,1)}, u32[]{:S(2)}, u32[]{:S(2)}) collective-permute-start(f16[272,1024]{1,0:T(8,128)(2,1)} %convert_element_type.76), channel_id=1, source_target_pairs={{0,16},{1,5},{2,18},{3,7},{4,20},{5,1},{6,22},{7,3},{8,24},{9,13},... | collective-permute-start | bytes 1671176 | tf_op jit(solution)/shard_map/ppermute | solution.py:41
  86.5 2.4 %collective-permute-start.17 = (f16[272,1024]{1,0:T(8,128)(2,1)}, f16[272,1024]{1,0:T(8,128)(2,1)}, u32[]{:S(2)}, u32[]{:S(2)}) collective-permute-start(f16[272,1024]{1,0:T(8,128)(2,1)} %convert_element_type.77), channel_id=1, source_target_pairs={{0,24},{1,7},{2,26},{3,1},{4,28},{5,3},{6,30},{7,5},{8,0},{9,15},{... | collective-permute-start | bytes 1671176 | tf_op jit(solution)/shard_map/ppermute | solution.py:41
  88.9 1.6 %collective-permute-start.19 = (f16[80,1024]{1,0:T(8,128)(2,1)}, f16[80,1024]{1,0:T(8,128)(2,1)S(1)}, u32[]{:S(2)}, u32[]{:S(2)}) collective-permute-start(f16[80,1024]{1,0:T(8,128)(2,1)} %add_convert_fusion.2), channel_id=1, source_target_pairs={{0,128},{1,129},{2,130},{3,131},{4,132},{5,133},{6,134},{7,135},{8... | collective-permute-start | bytes 491528 | tf_op jit(solution)/shard_map/ppermute | solution.py:41
  91.5 2.9 %collective-permute-start.18 = (f16[144,1024]{1,0:T(8,128)(2,1)S(1)}, f16[144,1024]{1,0:T(8,128)(2,1)S(1)}, u32[]{:S(2)}, u32[]{:S(2)}) collective-permute-start(f16[144,1024]{1,0:T(8,128)(2,1)S(1)} %add_convert_fusion.1), channel_id=1, source_target_pairs={{0,64},{1,193},{2,66},{3,195},{4,68},{5,197},{6,70},{7,199},{8,72}... | collective-permute-start | bytes 884744 | tf_op jit(solution)/shard_map/ppermute | solution.py:41
  94.4 5.5 %collective-permute-done.16 = f16[272,1024]{1,0:T(8,128)(2,1)} collective-permute-done((f16[272,1024]{1,0:T(8,128)(2,1)}, f16[272,1024]{1,0:T(8,128)(2,1)}, u32[]{:S(2)}, u32[]{:S(2)}) %collective-permute-start.16) | collective-permute-done | bytes 557088 | tf_op jit(solution)/shard_map/ppermute | solution.py:41
  100.0 1.8 %add_add_fusion = f32[272,1024]{1,0:T(8,128)S(1)} fusion(f16[272,1024]{1,0:T(8,128)(2,1)} %collective-permute-done.17, f16[272,1024]{1,0:T(8,128)(2,1)} %collective-permute-done.16, f32[272,1024]{1,0:T(8,128)S(1)} %get-tuple-element.50, f16[272,1024]{1,0:T(8,128)(2,1)} %collective-permute-done.15), kind=kLoop, calls=%fused_computation.2 | loop fusion | flops 1671168 | bytes 3899392 | tf_op jit(solution)/shard_map/add | solution.py:468
  101.8 6.5 %collective-permute-done.18 = f16[144,1024]{1,0:T(8,128)(2,1)S(1)} collective-permute-done((f16[144,1024]{1,0:T(8,128)(2,1)S(1)}, f16[144,1024]{1,0:T(8,128)(2,1)S(1)}, u32[]{:S(2)}, u32[]{:S(2)}) %collective-permute-start.18) | collective-permute-done | bytes 294944 | tf_op jit(solution)/shard_map/ppermute | solution.py:41
  110.3 1.9 %collective-permute-start.21 = (f16[80,1024]{1,0:T(8,128)(2,1)S(1)}, f16[80,1024]{1,0:T(8,128)(2,1)S(1)}, u32[]{:S(2)}, u32[]{:S(2)}) collective-permute-start(f16[80,1024]{1,0:T(8,128)(2,1)S(1)} %get-tuple-element.67), channel_id=1, source_target_pairs={{0,4},{1,17},{2,6},{3,19},{4,0},{5,21},{6,2},{7,23},{8,12},{9,25},... | collective-permute-start | bytes 491528 | tf_op jit(solution)/shard_map/ppermute | solution.py:41
  113.2 1.8 %collective-permute-start.23 = (f16[80,1024]{1,0:T(8,128)(2,1)S(1)}, f16[80,1024]{1,0:T(8,128)(2,1)S(1)}, u32[]{:S(2)}, u32[]{:S(2)}) collective-permute-start(f16[80,1024]{1,0:T(8,128)(2,1)S(1)} %get-tuple-element.69), channel_id=1, source_target_pairs={{0,6},{1,25},{2,0},{3,27},{4,2},{5,29},{6,4},{7,31},{8,14},{9,1},{... | collective-permute-start | bytes 491528 | tf_op jit(solution)/shard_map/ppermute | solution.py:41
  114.9 1.4 %collective-permute-done.21 = f16[80,1024]{1,0:T(8,128)(2,1)S(1)} collective-permute-done((f16[80,1024]{1,0:T(8,128)(2,1)S(1)}, f16[80,1024]{1,0:T(8,128)(2,1)S(1)}, u32[]{:S(2)}, u32[]{:S(2)}) %collective-permute-start.21) | collective-permute-done | bytes 163872 | tf_op jit(solution)/shard_map/ppermute | solution.py:41
  116.4 1.8 %collective-permute-done.22 = f16[80,1024]{1,0:T(8,128)(2,1)S(1)} collective-permute-done((f16[80,1024]{1,0:T(8,128)(2,1)S(1)}, f16[80,1024]{1,0:T(8,128)(2,1)S(1)}, u32[]{:S(2)}, u32[]{:S(2)}) %collective-permute-start.22) | collective-permute-done | bytes 163872 | tf_op jit(solution)/shard_map/ppermute | solution.py:41
  (68 shorter events, 21.9 us)
Async XLA Ops:
  0.6 1.0 copy-start.1
  1.7 5.6 %copy-start = (f32[512,1024]{1,0:T(8,128)S(1)}, f32[512,1024]{1,0:T(8,128)}, u32[]{:S(2)}) copy-start(f32[512,1024]{1,0:T(8,128)} %regions.3) | copy-start | bytes 6291460
  1.7 5.7 %copy-start.2 = (s32[512]{0:T(512)S(1)}, s32[512]{0:T(512)}, u32[]{:S(2)}) copy-start(s32[512]{0:T(512)} %param.5) | copy-start | bytes 6148
  1.7 10.4 %collective-permute-start.3 = (bf16[128,1024]{1,0:T(8,128)(2,1)S(1)}, bf16[128,1024]{1,0:T(8,128)(2,1)S(1)}, u32[]{:S(2)}, u32[]{:S(2)}) collective-permute-start(bf16[128,1024]{1,0:T(8,128)(2,1)S(1)} %shard_map.60.text), channel_id=1, source_target_pairs={{0,224},{1,33},{2,226},{3,35},{4,228},{5,37},{6,230},{7,39},{8,232... | collective-permute-start | bytes 786440 | tf_op jit(solution)/shard_map/ppermute | solution.py:41
  4.3 12.5 %collective-permute-start.4 = (bf16[128,1024]{1,0:T(8,128)(2,1)S(1)}, bf16[128,1024]{1,0:T(8,128)(2,1)S(1)}, u32[]{:S(2)}, u32[]{:S(2)}) collective-permute-start(bf16[128,1024]{1,0:T(8,128)(2,1)S(1)} %shard_map.60.text), channel_id=1, source_target_pairs={{0,192},{1,65},{2,194},{3,67},{4,196},{5,69},{6,198},{7,71},{8,200... | collective-permute-start | bytes 786440 | tf_op jit(solution)/shard_map/ppermute | solution.py:41
  8.0 9.4 %collective-permute-start.1 = (bf16[144,1024]{1,0:T(8,128)(2,1)S(1)}, bf16[144,1024]{1,0:T(8,128)(2,1)S(1)}, u32[]{:S(2)}, u32[]{:S(2)}) collective-permute-start(bf16[144,1024]{1,0:T(8,128)(2,1)S(1)} %shard_map.58.part), channel_id=1, source_target_pairs={{0,16},{1,17},{2,18},{3,19},{4,20},{5,21},{6,22},{7,23},{8,24},{9,... | collective-permute-start | bytes 884744 | tf_op jit(solution)/shard_map/ppermute | solution.py:41
  11.7 18.6 %collective-permute-start = (bf16[528,1024]{1,0:T(8,128)(2,1)S(1)}, bf16[528,1024]{1,0:T(8,128)(2,1)S(1)}, u32[]{:S(2)}, u32[]{:S(2)}) collective-permute-start(bf16[528,1024]{1,0:T(8,128)(2,1)S(1)} %shard_map.59.own.whole), channel_id=1, source_target_pairs={{0,24},{1,9},{2,26},{3,11},{4,28},{5,13},{6,30},{7,15},{8,0},{9,17... | collective-permute-start | bytes 3244040 | tf_op jit(solution)/shard_map/ppermute | solution.py:41
  17.4 8.9 %collective-permute-start.5 = (bf16[192,1024]{1,0:T(8,128)(2,1)S(1)}, bf16[192,1024]{1,0:T(8,128)(2,1)S(1)}, u32[]{:S(2)}, u32[]{:S(2)}) collective-permute-start(bf16[192,1024]{1,0:T(8,128)(2,1)S(1)} %shard_map.61), channel_id=1, source_target_pairs={{0,192},{1,65},{2,194},{3,67},{4,196},{5,69},{6,198},{7,71},{8,200... | collective-permute-start | bytes 1179656 | tf_op jit(solution)/shard_map/ppermute | solution.py:41
  17.5 5.6 %collective-permute-start.2 = (bf16[128,1024]{1,0:T(8,128)(2,1)S(1)}, bf16[128,1024]{1,0:T(8,128)(2,1)S(1)}, u32[]{:S(2)}, u32[]{:S(2)}) collective-permute-start(bf16[128,1024]{1,0:T(8,128)(2,1)S(1)} %slice.78), channel_id=1, source_target_pairs={{0,2},{1,3},{2,0},{3,1},{4,6},{5,7},{6,4},{7,5},{8,10},{9,11},{10,... | collective-permute-start | bytes 786440 | tf_op jit(solution)/shard_map/ppermute | solution.py:41
  30.4 4.3 %collective-permute-start.6 = (bf16[720,1024]{1,0:T(8,128)(2,1)S(1)}, bf16[720,1024]{1,0:T(8,128)(2,1)S(1)}, u32[]{:S(2)}, u32[]{:S(2)}) collective-permute-start(bf16[720,1024]{1,0:T(8,128)(2,1)S(1)} %pad_maximum_fusion), channel_id=1, source_target_pairs={{0,1},{1,0},{2,3},{3,2},{4,5},{5,4},{6,7},{7,6},{8,9},{9,8},{10,11... | collective-permute-start | bytes 4423688 | tf_op jit(solution)/shard_map/ppermute | solution.py:41
  39.7 1.3 %collective-permute-start.7 = (f32[8,1024]{1,0:T(8,128)S(1)}, f32[8,1024]{1,0:T(8,128)S(1)}, u32[]{:S(2)}, u32[]{:S(2)}) collective-permute-start(f32[8,1024]{1,0:T(8,128)S(1)} %get-tuple-element.37), channel_id=1, source_target_pairs={{0,1},{1,0},{2,3},{3,2},{4,5},{5,4},{6,7},{7,6},{8,9},{9,8},{10,11... | collective-permute-start | bytes 98312 | tf_op jit(solution)/shard_map/ppermute | solution.py:41
  41.6 3.9 %collective-permute-start.8 = (f32[8,1024]{1,0:T(8,128)S(1)}, f32[8,1024]{1,0:T(8,128)S(1)}, u32[]{:S(2)}, u32[]{:S(2)}) collective-permute-start(f32[8,1024]{1,0:T(8,128)S(1)} %shard_map.63.own), channel_id=1, source_target_pairs={{0,8},{1,33},{2,10},{3,35},{4,12},{5,37},{6,14},{7,39},{8,0},{9,41... | collective-permute-start | bytes 98312 | tf_op jit(solution)/shard_map/ppermute | solution.py:41
  45.6 3.8 %collective-permute-start.9 = (f32[8,1024]{1,0:T(8,128)S(1)}, f32[8,1024]{1,0:T(8,128)S(1)}, u32[]{:S(2)}, u32[]{:S(2)}) collective-permute-start(f32[8,1024]{1,0:T(8,128)S(1)} %shard_map.64.own), channel_id=1, source_target_pairs={{0,16},{1,65},{2,18},{3,67},{4,20},{5,69},{6,22},{7,71},{8,24},{9,... | collective-permute-start | bytes 98312 | tf_op jit(solution)/shard_map/ppermute | solution.py:41
  49.3 6.9 %collective-permute-start.10 = (f32[8,1024]{1,0:T(8,128)S(1)}, f32[8,1024]{1,0:T(8,128)S(1)}, u32[]{:S(2)}, u32[]{:S(2)}) collective-permute-start(f32[8,1024]{1,0:T(8,128)S(1)} %shard_map.65.own), channel_id=1, source_target_pairs={{0,2},{1,129},{2,0},{3,131},{4,6},{5,133},{6,4},{7,135},{8,10},{9,... | collective-permute-start | bytes 98312 | tf_op jit(solution)/shard_map/ppermute | solution.py:41
  56.2 0.7 collective-permute-start.11
  57.6 7.1 %collective-permute-start.12 = (f32[8,1024]{1,0:T(8,128)S(1)}, f32[8,1024]{1,0:T(8,128)S(1)}, u32[]{:S(2)}, u32[]{:S(2)}) collective-permute-start(f32[8,1024]{1,0:T(8,128)S(1)} %shard_map.67.mine), channel_id=1, source_target_pairs={{0,1},{1,0},{2,3},{3,2},{4,5},{5,4},{6,7},{7,6},{8,9},{9,8},{10,11... | collective-permute-start | bytes 98312 | tf_op jit(solution)/shard_map/ppermute | solution.py:41
  68.4 2.7 %collective-permute-start.13 = (f16[512,1024]{1,0:T(8,128)(2,1)S(1)}, f16[512,1024]{1,0:T(8,128)(2,1)S(1)}, u32[]{:S(2)}, u32[]{:S(2)}) collective-permute-start(f16[512,1024]{1,0:T(8,128)(2,1)S(1)} %convert_element_type.70), channel_id=1, source_target_pairs={{0,1},{1,0},{2,3},{3,2},{4,5},{5,4},{6,7},{7,6},{8,9},{9,8},{10,11... | collective-permute-start | bytes 3145736 | tf_op jit(solution)/shard_map/ppermute | solution.py:41
  72.1 11.3 %collective-permute-start.14 = (f16[288,1024]{1,0:T(8,128)(2,1)S(1)}, f16[288,1024]{1,0:T(8,128)(2,1)}, u32[]{:S(2)}, u32[]{:S(2)}) collective-permute-start(f16[288,1024]{1,0:T(8,128)(2,1)S(1)} %add_convert_fusion), channel_id=1, source_target_pairs={{0,32},{1,225},{2,34},{3,227},{4,36},{5,229},{6,38},{7,231},{8,40}... | collective-permute-start | bytes 1769480 | tf_op jit(solution)/shard_map/ppermute | solution.py:41
  83.4 11.0 %collective-permute-start.15 = (f16[272,1024]{1,0:T(8,128)(2,1)}, f16[272,1024]{1,0:T(8,128)(2,1)}, u32[]{:S(2)}, u32[]{:S(2)}) collective-permute-start(f16[272,1024]{1,0:T(8,128)(2,1)} %convert_element_type.76), channel_id=1, source_target_pairs={{0,16},{1,5},{2,18},{3,7},{4,20},{5,1},{6,22},{7,3},{8,24},{9,13},... | collective-permute-start | bytes 1671176 | tf_op jit(solution)/shard_map/ppermute | solution.py:41
  86.2 13.7 %collective-permute-start.16 = (f16[272,1024]{1,0:T(8,128)(2,1)}, f16[272,1024]{1,0:T(8,128)(2,1)}, u32[]{:S(2)}, u32[]{:S(2)}) collective-permute-start(f16[272,1024]{1,0:T(8,128)(2,1)} %convert_element_type.75), channel_id=1, source_target_pairs={{0,8},{1,3},{2,10},{3,5},{4,12},{5,7},{6,14},{7,1},{8,16},{9,11},{... | collective-permute-start | bytes 1671176 | tf_op jit(solution)/shard_map/ppermute | solution.py:41
  86.5 13.5 %collective-permute-start.17 = (f16[272,1024]{1,0:T(8,128)(2,1)}, f16[272,1024]{1,0:T(8,128)(2,1)}, u32[]{:S(2)}, u32[]{:S(2)}) collective-permute-start(f16[272,1024]{1,0:T(8,128)(2,1)} %convert_element_type.77), channel_id=1, source_target_pairs={{0,24},{1,7},{2,26},{3,1},{4,28},{5,3},{6,30},{7,5},{8,0},{9,15},{... | collective-permute-start | bytes 1671176 | tf_op jit(solution)/shard_map/ppermute | solution.py:41
  88.9 13.0 %collective-permute-start.19 = (f16[80,1024]{1,0:T(8,128)(2,1)}, f16[80,1024]{1,0:T(8,128)(2,1)S(1)}, u32[]{:S(2)}, u32[]{:S(2)}) collective-permute-start(f16[80,1024]{1,0:T(8,128)(2,1)} %add_convert_fusion.2), channel_id=1, source_target_pairs={{0,128},{1,129},{2,130},{3,131},{4,132},{5,133},{6,134},{7,135},{8... | collective-permute-start | bytes 491528 | tf_op jit(solution)/shard_map/ppermute | solution.py:41
  91.5 16.9 %collective-permute-start.18 = (f16[144,1024]{1,0:T(8,128)(2,1)S(1)}, f16[144,1024]{1,0:T(8,128)(2,1)S(1)}, u32[]{:S(2)}, u32[]{:S(2)}) collective-permute-start(f16[144,1024]{1,0:T(8,128)(2,1)S(1)} %add_convert_fusion.1), channel_id=1, source_target_pairs={{0,64},{1,193},{2,66},{3,195},{4,68},{5,197},{6,70},{7,199},{8,72}... | collective-permute-start | bytes 884744 | tf_op jit(solution)/shard_map/ppermute | solution.py:41
  101.8 6.6 %copy-start.3 = (f32[272,1024]{1,0:T(8,128)}, f32[272,1024]{1,0:T(8,128)S(1)}, u32[]{:S(2)}) copy-start(f32[272,1024]{1,0:T(8,128)S(1)} %add_add_fusion) | copy-start | bytes 3342340
  108.5 1.6 %slice-start = ((f32[272,1024]{1,0:T(8,128)}), f32[256,1024]{1,0:T(8,128)S(1)}, s32[]{:S(2)}) async-start(f32[272,1024]{1,0:T(8,128)} %copy-done.3), calls=%async_computation | async-start | bytes 2097152 | tf_op jit(solution)/shard_map/slice | solution.py:470
  109.8 9.2 %collective-permute-start.20 = (f32[144,1024]{1,0:T(8,128)S(1)}, f32[144,1024]{1,0:T(8,128)S(1)}, u32[]{:S(2)}, u32[]{:S(2)}) collective-permute-start(f32[144,1024]{1,0:T(8,128)S(1)} %fusion.1), channel_id=1, source_target_pairs={{0,1},{1,0},{2,3},{3,2},{4,5},{5,4},{6,7},{7,6},{8,9},{9,8},{10,11... | collective-permute-start | bytes 1769480 | tf_op jit(solution)/shard_map/ppermute | solution.py:41
  110.3 6.1 %collective-permute-start.21 = (f16[80,1024]{1,0:T(8,128)(2,1)S(1)}, f16[80,1024]{1,0:T(8,128)(2,1)S(1)}, u32[]{:S(2)}, u32[]{:S(2)}) collective-permute-start(f16[80,1024]{1,0:T(8,128)(2,1)S(1)} %get-tuple-element.67), channel_id=1, source_target_pairs={{0,4},{1,17},{2,6},{3,19},{4,0},{5,21},{6,2},{7,23},{8,12},{9,25},... | collective-permute-start | bytes 491528 | tf_op jit(solution)/shard_map/ppermute | solution.py:41
  112.2 5.9 %collective-permute-start.22 = (f16[80,1024]{1,0:T(8,128)(2,1)S(1)}, f16[80,1024]{1,0:T(8,128)(2,1)S(1)}, u32[]{:S(2)}, u32[]{:S(2)}) collective-permute-start(f16[80,1024]{1,0:T(8,128)(2,1)S(1)} %get-tuple-element.68), channel_id=1, source_target_pairs={{0,2},{1,9},{2,4},{3,11},{4,6},{5,13},{6,0},{7,15},{8,10},{9,17},{... | collective-permute-start | bytes 491528 | tf_op jit(solution)/shard_map/ppermute | solution.py:41
  113.2 5.0 %collective-permute-start.23 = (f16[80,1024]{1,0:T(8,128)(2,1)S(1)}, f16[80,1024]{1,0:T(8,128)(2,1)S(1)}, u32[]{:S(2)}, u32[]{:S(2)}) collective-permute-start(f16[80,1024]{1,0:T(8,128)(2,1)S(1)} %get-tuple-element.69), channel_id=1, source_target_pairs={{0,6},{1,25},{2,0},{3,27},{4,2},{5,29},{6,4},{7,31},{8,14},{9,1},{... | collective-permute-start | bytes 491528 | tf_op jit(solution)/shard_map/ppermute | solution.py:41

commit v3 on v2

--- a/solution.py
+++ b/solution.py
@@ -57,14 +57,13 @@
     return moved(value, lambda z, y, x, c: (z + by if c == 0 else z - by, y, x, c))
 
 
-def call(kernel, outs, *args, limit=12 << 20, scratch=(), us=1.0):
+def call(kernel, outs, *args, limit=1 << 20, us=1.0):
     specs = [pl.BlockSpec(memory_space=SMEM if arg.ndim == 1 else VMEM) for arg in args]
     return pl.pallas_call(
         kernel,
         in_specs=specs,
         out_specs=[pl.BlockSpec(memory_space=VMEM) for _ in outs],
         out_shape=[jax.ShapeDtypeStruct(shape, dtype) for shape, dtype in outs],
-        scratch_shapes=scratch,
         cost_estimate=pl.CostEstimate(
             flops=int(us * 1.1e9), bytes_accessed=int(us * 3e6), transcendentals=0
         ),
@@ -172,7 +171,7 @@
 
 
 def score_kernel(
-    place, own, full, far, pair, other, text, one, two, skip, s_out, r_out, c_out, keep, give
+    place, own, full, far, pair, other, text, one, two, skip, s_out, r_out, c_out, p_out, keep, give
 ):
     z, y, x, c = place[0], place[1], place[2], place[3]
 
@@ -200,6 +199,7 @@
     c_out[896:1024, :] = text[...]
 
     positive = positives(place, own, full, far, pair)
+    p_out[...] = jnp.broadcast_to(positive, (8, TILE))
     regions = r_out[...]
     for part in range(2):
         chunk = pl.ds(part * 512, 512)
@@ -245,7 +245,7 @@
     give[...] = jnp.where(c == 0, by_cap, turned)
 
 
-def pair_kernel(place, keep, came, out):
+def pair_kernel(place, keep, came, held, rows, captions, out):
     first = place[3] == 0
     m0, m1, s0, s1 = keep[0:1, :], came[0:1, :], keep[2:3, :], came[2:3, :]
     top = jnp.maximum(m0, m1)
@@ -266,7 +266,7 @@
     return top, sums, own[4:5, :] + came[4:5, :], jnp.maximum(own[5:6, :], came[5:6, :])
 
 
-def merge_kernel(own, came, out):
+def merge_kernel(own, came, held, rows, captions, out):
     top, sums, total, peak = merged(own[...], came[...])
     out[0:2, :] = top
     out[2:4, :] = sums
@@ -275,7 +275,7 @@
     out[6:8, :] = jnp.zeros((2, TILE), F32)
 
 
-def last_kernel(place, own, came, out):
+def last_kernel(place, own, came, held, rows, captions, out):
     first = place[3] == 0
     lines = lax.broadcasted_iota(jnp.int32, (8, TILE), 0)
     empty = jnp.where(lines < 2, far_below, 0.0)
@@ -291,14 +291,14 @@
 
 
 def weight_kernel(
-    place, scores, regions, mine, came, whole, full, far, pair, w_out, give, kept
+    place, scores, regions, mine, came, matches, w_out, give, kept
 ):
     z, y, x, c = place[0], place[1], place[2], place[3]
     first_core = c == 0
     row_lse = jnp.where(first_core, mine[0:1, :], came[1:2, :])
     turn = (NX - jnp.where(first_core, y, x)) % NX * 256
     row_lse = pltpu.roll(jnp.broadcast_to(row_lse, (8, TILE)), turn, 1)[0:1, :]
-    positive = positives(place, whole, full, far, pair)
+    positive = matches[0:1, :]
     ids = lax.broadcasted_iota(jnp.int32, (BLOCK, TILE), 0)
     for slot in range(8):
         chunk = pl.ds(slot * BLOCK, BLOCK)
@@ -313,15 +313,15 @@
         w_out[chunk, :] = weight.astype(BF)
     scale = region_scale(place, mine, came)
     part = jnp.dot(w_out[0:512, :], regions[...], preferred_element_type=F32) * scale
-    nothing = jnp.zeros((16, TILE), F32)
+    nothing = jnp.zeros((8, TILE), F32)
     for at in range(3):
-        start = at * 144
+        start = at * 136
         give[start : start + 128, :] = part[at * 128 : (at + 1) * 128, :]
-        give[start + 128 : start + 144, :] = nothing
-    give[432:496, :] = jnp.where(first_core, part[448:512, :], part[384:448, :])
-    give[496:512, :] = nothing
+        give[start + 128 : start + 136, :] = nothing
+    give[408:472, :] = jnp.where(first_core, part[448:512, :], part[384:448, :])
+    give[472:480, :] = nothing
     kept[0:64, :] = jnp.where(first_core, part[384:448, :], part[448:512, :])
-    kept[64:80, :] = digits(jnp.where(first_core, mine[4:5, :], came[4:5, :]), z)
+    kept[64:72, :] = jnp.where(first_core, digits(mine[4:5, :], z), 0.0)
 
 
 def digits(value, index):
@@ -331,8 +331,8 @@
     rest = rest - middle * 2.0**10
     low = jnp.floor(rest)
     last = jnp.floor((rest - low) * 2.0**10)
-    lane = lax.broadcasted_iota(jnp.int32, (16, TILE), 1)
-    line_at = lax.broadcasted_iota(jnp.int32, (16, TILE), 0)
+    lane = lax.broadcasted_iota(jnp.int32, (8, TILE), 1)
+    line_at = lax.broadcasted_iota(jnp.int32, (8, TILE), 0)
     which = lane // 16
     digit = jnp.where(
         which == 0, high, jnp.where(which == 1, middle, jnp.where(which == 2, low, last))
@@ -353,13 +353,13 @@
     ) * region_scale(place, mine, came)
     code = digits(jnp.where(first_core, mine[4:5, :], came[4:5, :]), place[0])
     near_two[0:128, :] = part[0:128, :]
-    near_two[128:144, :] = code
-    near_two[144:272, :] = part[128:256, :]
-    near_two[272:288, :] = code
+    near_two[128:136, :] = code
+    near_two[136:264, :] = part[128:256, :]
+    near_two[264:272, :] = code
     second[0:128, :] = part[256:384, :]
-    second[128:144, :] = code
+    second[128:136, :] = code
     own[0:128, :] = part[384:512, :]
-    own[128:144, :] = jnp.where(first_core, code, 0.0)
+    own[128:136, :] = jnp.where(first_core, code, 0.0)
 
 
 def region_kernel(place, weights, captions, mine, came, o0, o1, o2, o3):
@@ -374,7 +374,7 @@
     )
     for by, ref in enumerate((o0, o1, o2, o3)):
         ref[0:256, :] = part[by * 256 : (by + 1) * 256, :] * scale
-        ref[256:272, :] = code
+        ref[256:264, :] = code
 
 
 def shards(regions, captions, positive):
@@ -402,53 +402,55 @@
     full, other, skip = lax.optimization_barrier((full, other, skip))
     far = swapped(jnp.concatenate([full[256:528], one, two, skip], axis=0))
 
-    scores, region_rows, caption_rows, keep, give = call(
+    small = ((8, TILE), F32)
+    scores, region_rows, caption_rows, matches, keep, give = call(
         score_kernel,
-        [(big, F32), (big, BF), (big, BF), ((8, TILE), F32), ((8, TILE), F32)],
+        [(big, F32), (big, BF), (big, BF), ((8, TILE), jnp.int32), small, small],
         place, whole, full, far, pair, other, text, one, two, skip,
         us=8.0,
-    )
-
-    small = [((8, TILE), F32)]
-    (stats,) = call(pair_kernel, small, place, keep, swapped(give))
+        limit=8 << 20,
+    )
+
+    tile = (scores, region_rows, caption_rows)
+    (stats,) = call(pair_kernel, [small], place, keep, swapped(give), *tile)
 
     def partner(bit):
         def target(z, y, x, c):
             if c == 1:
-                return (z ^ (1 << bit), y, x, c) if bit < 3 else None
+                return (z ^ (1 << bit % 3), y, x, c)
             return (z, y ^ (1 << bit), x, c) if bit < 2 else (z, y, x ^ (1 << (bit - 2)), c)
 
         return target
 
     for bit in range(3):
-        (stats,) = call(merge_kernel, small, stats, moved(stats, partner(bit)))
-    (lse,) = call(last_kernel, small, place, stats, moved(stats, partner(3)))
+        (stats,) = call(merge_kernel, [small], stats, moved(stats, partner(bit)), *tile)
+    (lse,) = call(last_kernel, [small], place, stats, moved(stats, partner(3)), *tile)
     came = swapped(lse)
 
     weights, give, kept_half = call(
         weight_kernel,
-        [(big, BF), ((512, FEATURES), F32), ((80, FEATURES), F32)],
-        place, scores, region_rows, lse, came, whole, full, far, pair,
+        [(big, BF), ((480, FEATURES), F32), ((72, FEATURES), F32)],
+        place, scores, region_rows, lse, came, matches,
         us=40.0,
+        limit=6 << 20,
     )
     got = swapped(give.astype(WIRE))
+    r0, r1, r2, r3 = call(
+        region_kernel, [((264, FEATURES), F32)] * 4, place, weights, caption_rows, lse, came, us=30.0,
+        limit=8 << 20,
+    )
+    weights, r1, r2, r3 = lax.optimization_barrier(
+        (weights, r1.astype(WIRE), r2.astype(WIRE), r3.astype(WIRE))
+    )
     near_two, second, own = call(
         caption_kernel,
-        [((288, FEATURES), F32), ((144, FEATURES), F32), ((144, FEATURES), F32)],
+        [((272, FEATURES), F32), ((136, FEATURES), F32), ((136, FEATURES), F32)],
         place, weights, region_rows, lse, came,
         us=20.0,
-    )
-    near_two = (near_two + got[0:288].astype(F32)).astype(WIRE)
-    kept_half = (kept_half + got[432:512].astype(F32)).astype(WIRE)
-    weights, near_two, kept_half = lax.optimization_barrier((weights, near_two, kept_half))
-    ahead = along_z(near_two, 1)
-    opposite = along_z(kept_half, 4)
-    r0, r1, r2, r3 = call(
-        region_kernel, [((272, FEATURES), F32)] * 4, place, weights, caption_rows, lse, came, us=30.0
-    )
-    r1, r2, r3, ahead = lax.optimization_barrier(
-        (r1.astype(WIRE), r2.astype(WIRE), r3.astype(WIRE), ahead)
-    )
+        limit=6 << 20,
+    )
+    ahead = along_z((near_two + got[0:272].astype(F32)).astype(WIRE), 1)
+    skipped = along_z((kept_half + got[408:480].astype(F32)).astype(WIRE), 2)
 
     def major_from(value, by):
         return moved(
@@ -460,29 +462,28 @@
             value, lambda z, y, x, c: (z, y, x + by, c) if c == 0 else (z, y + by, x, c)
         )
 
-    onward = (second + got[288:432].astype(F32)) + ahead[144:288].astype(F32)
+    nothing = jnp.zeros((GROUP, FEATURES), F32)
+    late = skipped.astype(F32)
+    late = jnp.where(
+        first_core,
+        jnp.concatenate([late[0:64], nothing, late[64:72]], axis=0),
+        jnp.concatenate([nothing, late], axis=0),
+    )
+    onward = (second + got[272:408].astype(F32)) + (ahead[136:272].astype(F32) + late)
     passed = along_z(onward.astype(WIRE), 2)
     q2 = major_from(r2, 2)
     q1 = major_from(r1, 1)
     q3 = major_from(r3, 3)
     summed = (r0 + q2.astype(F32)) + (q1.astype(F32) + q3.astype(F32))
-    summed, passed, opposite = lax.optimization_barrier((summed, passed, opposite))
     blocks = summed[0:256].reshape(4, GROUP, FEATURES)
     minor = jnp.where(first_core, x, y)
 
     def piece(by):
         block = lax.dynamic_index_in_dim(blocks, (minor + by) % 4, 0, keepdims=False)
-        return jnp.concatenate([block, summed[256:272]], axis=0)
+        return jnp.concatenate([block, summed[256:264]], axis=0)
 
     t2, t1, t3 = (minor_from(piece(by).astype(WIRE), by) for by in (2, 1, 3))
-    nothing = jnp.zeros((GROUP, FEATURES), F32)
-    late = opposite.astype(F32)
-    late = jnp.where(
-        first_core,
-        jnp.concatenate([late[0:64], nothing, late[64:80]], axis=0),
-        jnp.concatenate([nothing, late[0:64], nothing[0:16]], axis=0),
-    )
-    mine = (own + ahead[0:144].astype(F32)) + (passed.astype(F32) + late)
+    mine = (own + ahead[0:136].astype(F32)) + passed.astype(F32)
     both = mine + swapped(mine)
     all_regions = (piece(0) + t2.astype(F32)) + (t1.astype(F32) + t3.astype(F32))
 

time: 123 us -> 115 us (0.935)
  other arithmetic: 10.7 us -> 4.12 us
  waiting for transfers between devices: 44.9 us -> 39.6 us
  local copies, waits for them, and re-layouts: 1.16 us -> 3.5 us
  starting transfers between devices: 46.4 us -> 48.6 us
    ppermute x24, waiting for transfers between devices: 44.9 us -> 39.6 us  [moved(): return lax.ppermute(value, AXES, pairs)]
    ppermute x24, starting transfers between devices: 46.4 us -> 48.6 us  [moved(): return lax.ppermute(value, AXES, pairs)]
    unnamed x8 -> x14, local copies, waits for them, and re-layouts: 1.05 us -> 3.24 us
    add x1, other arithmetic: 1.78 us -> 0.38 us  [shards(): summed = r0 + q2.astype(F32) + (q1.astype(F32) + q3.astype(F32))]
  transfers between devices with their start and end apart: 24 -> 24, of which waited for: 17 -> 16; matrix products, arithmetic and copies ran while one was open for 5% -> 2% of each run, Pallas kernels for 5% -> 3%
where the time goes in v3:
time: 115 us
  starting transfers between devices  48.6 us (42%)
  waiting for transfers between devices  39.6 us (34%)
  Pallas kernels  16.5 us (14%)
  other arithmetic  4.12 us (4%)
  local copies, waits for them, and re-layouts  3.5 us (3%)
  between operations  2.75 us (2%)
    ppermute x24, starting transfers between devices, moved(): return lax.ppermute(value, AXES, pairs)  48.6 us
    ppermute x24, waiting for transfers between devices, moved(): return lax.ppermute(value, AXES, pairs)  39.6 us
    pallas_call x13, Pallas kernels, call(): pl.pallas_call(kernel, in_specs=specs, out_specs=[pl.BlockSpec(memory_spa...  16.5 us
    unnamed x14, local copies, waits for them, and re-layouts  3.24 us
  transfers between devices with their start and end apart: 24, of which 16 were waited for; matrix products, arithmetic and copies ran while one was open for 2% of the time, Pallas kernels for 3%

profile of v3, /device:TPU:1, one launch (start us, length us, event | category | flops | bytes accessed | tf_op | source)
XLA Modules:
  0.0 115.1 jit_solution(52887703822181320)
XLA Ops:
  1.7 2.5 %collective-permute-start.3 = (bf16[128,1024]{1,0:T(8,128)(2,1)S(1)}, bf16[128,1024]{1,0:T(8,128)(2,1)S(1)}, u32[]{:S(2)}, u32[]{:S(2)}) collective-permute-start(bf16[128,1024]{1,0:T(8,128)(2,1)S(1)} %shard_map.60.text), channel_id=1, source_target_pairs={{0,224},{1,33},{2,226},{3,35},{4,228},{5,37},{6,230},{7,39},{8,232... | collective-permute-start | bytes 786440 | tf_op jit(solution)/shard_map/ppermute | solution.py:41
  4.3 3.0 %collective-permute-start.4 = (bf16[128,1024]{1,0:T(8,128)(2,1)S(1)}, bf16[128,1024]{1,0:T(8,128)(2,1)S(1)}, u32[]{:S(2)}, u32[]{:S(2)}) collective-permute-start(bf16[128,1024]{1,0:T(8,128)(2,1)S(1)} %shard_map.60.text), channel_id=1, source_target_pairs={{0,192},{1,65},{2,194},{3,67},{4,196},{5,69},{6,198},{7,71},{8,200... | collective-permute-start | bytes 786440 | tf_op jit(solution)/shard_map/ppermute | solution.py:41
  8.0 3.0 %collective-permute-start.1 = (bf16[144,1024]{1,0:T(8,128)(2,1)S(1)}, bf16[144,1024]{1,0:T(8,128)(2,1)S(1)}, u32[]{:S(2)}, u32[]{:S(2)}) collective-permute-start(bf16[144,1024]{1,0:T(8,128)(2,1)S(1)} %shard_map.58.part), channel_id=1, source_target_pairs={{0,16},{1,17},{2,18},{3,19},{4,20},{5,21},{6,22},{7,23},{8,24},{9,... | collective-permute-start | bytes 884744 | tf_op jit(solution)/shard_map/ppermute | solution.py:41
  12.1 4.6 %collective-permute-done.4.two = bf16[128,1024]{1,0:T(8,128)(2,1)S(1)} collective-permute-done((bf16[128,1024]{1,0:T(8,128)(2,1)S(1)}, bf16[128,1024]{1,0:T(8,128)(2,1)S(1)}, u32[]{:S(2)}, u32[]{:S(2)}) %collective-permute-start.4) | collective-permute-done | bytes 262176 | tf_op jit(solution)/shard_map/ppermute | solution.py:41
  18.8 4.3 %collective-permute-done.2.other = bf16[128,1024]{1,0:T(8,128)(2,1)S(1)} collective-permute-done((bf16[128,1024]{1,0:T(8,128)(2,1)S(1)}, bf16[128,1024]{1,0:T(8,128)(2,1)S(1)}, u32[]{:S(2)}, u32[]{:S(2)}) %collective-permute-start.2) | collective-permute-done | bytes 262176 | tf_op jit(solution)/shard_map/ppermute | solution.py:41
  23.1 3.2 %collective-permute-done.5.skip = bf16[192,1024]{1,0:T(8,128)(2,1)S(1)} collective-permute-done((bf16[192,1024]{1,0:T(8,128)(2,1)S(1)}, bf16[192,1024]{1,0:T(8,128)(2,1)S(1)}, u32[]{:S(2)}, u32[]{:S(2)}) %collective-permute-start.5) | collective-permute-done | bytes 393248 | tf_op jit(solution)/shard_map/ppermute | solution.py:41
  26.3 4.0 %collective-permute-done.full = bf16[528,1024]{1,0:T(8,128)(2,1)S(1)} collective-permute-done((bf16[528,1024]{1,0:T(8,128)(2,1)S(1)}, bf16[528,1024]{1,0:T(8,128)(2,1)S(1)}, u32[]{:S(2)}, u32[]{:S(2)}) %collective-permute-start) | collective-permute-done | bytes 1081376 | tf_op jit(solution)/shard_map/ppermute | solution.py:41
  30.4 1.4 %collective-permute-start.6 = (bf16[720,1024]{1,0:T(8,128)(2,1)S(1)}, bf16[720,1024]{1,0:T(8,128)(2,1)S(1)}, u32[]{:S(2)}, u32[]{:S(2)}) collective-permute-start(bf16[720,1024]{1,0:T(8,128)(2,1)S(1)} %pad_maximum_fusion), channel_id=1, source_target_pairs={{0,1},{1,0},{2,3},{3,2},{4,5},{5,4},{6,7},{7,6},{8,9},{9,8},{10,11... | collective-permute-start | bytes 4423688 | tf_op jit(solution)/shard_map/ppermute | solution.py:41
  31.9 2.9 %collective-permute-done.6.far = bf16[720,1024]{1,0:T(8,128)(2,1)S(1)} collective-permute-done((bf16[720,1024]{1,0:T(8,128)(2,1)S(1)}, bf16[720,1024]{1,0:T(8,128)(2,1)S(1)}, u32[]{:S(2)}, u32[]{:S(2)}) %collective-permute-start.6) | collective-permute-done | bytes 1474592 | tf_op jit(solution)/shard_map/ppermute | solution.py:41
  34.8 5.1 %shard_map.62 = (f32[1024,1024]{1,0:T(8,128)S(1)}, bf16[1024,1024]{1,0:T(8,128)(2,1)S(1)}, bf16[1024,1024]{1,0:T(8,128)(2,1)S(1)}, s32[8,1024]{1,0:T(8,128)S(1)}...) custom-call(s32[4]{0:T(128)S(1)} %pad_add_fusion.place, bf16[528,1024]{1,0:T(8,128)(2,1)S(1)} %shard_map.59.own, ...), custom_call_target="tpu_custom_call" | custom-call | flops 8800000000 | bytes 24000000 | tf_op jit(solution)/shard_map/pallas_call | solution.py:62
  41.8 2.3 %collective-permute-start.8 = (f32[8,1024]{1,0:T(8,128)S(1)}, f32[8,1024]{1,0:T(8,128)S(1)}, u32[]{:S(2)}, u32[]{:S(2)}) collective-permute-start(f32[8,1024]{1,0:T(8,128)S(1)} %shard_map.63.own), channel_id=1, source_target_pairs={{0,8},{1,33},{2,10},{3,35},{4,12},{5,37},{6,14},{7,39},{8,0},{9,41... | collective-permute-start | bytes 98312 | tf_op jit(solution)/shard_map/ppermute | solution.py:41
  44.1 1.6 %collective-permute-done.8.came = f32[8,1024]{1,0:T(8,128)S(1)} collective-permute-done((f32[8,1024]{1,0:T(8,128)S(1)}, f32[8,1024]{1,0:T(8,128)S(1)}, u32[]{:S(2)}, u32[]{:S(2)}) %collective-permute-start.8) | collective-permute-done | bytes 32800 | tf_op jit(solution)/shard_map/ppermute | solution.py:41
  45.7 2.1 %collective-permute-start.9 = (f32[8,1024]{1,0:T(8,128)S(1)}, f32[8,1024]{1,0:T(8,128)S(1)}, u32[]{:S(2)}, u32[]{:S(2)}) collective-permute-start(f32[8,1024]{1,0:T(8,128)S(1)} %shard_map.64.own), channel_id=1, source_target_pairs={{0,16},{1,65},{2,18},{3,67},{4,20},{5,69},{6,22},{7,71},{8,24},{9,... | collective-permute-start | bytes 98312 | tf_op jit(solution)/shard_map/ppermute | solution.py:41
  47.8 1.7 %collective-permute-done.9.came = f32[8,1024]{1,0:T(8,128)S(1)} collective-permute-done((f32[8,1024]{1,0:T(8,128)S(1)}, f32[8,1024]{1,0:T(8,128)S(1)}, u32[]{:S(2)}, u32[]{:S(2)}) %collective-permute-start.9) | collective-permute-done | bytes 32800 | tf_op jit(solution)/shard_map/ppermute | solution.py:41
  49.5 3.0 %collective-permute-start.10 = (f32[8,1024]{1,0:T(8,128)S(1)}, f32[8,1024]{1,0:T(8,128)S(1)}, u32[]{:S(2)}, u32[]{:S(2)}) collective-permute-start(f32[8,1024]{1,0:T(8,128)S(1)} %shard_map.65.own), channel_id=1, source_target_pairs={{0,2},{1,129},{2,0},{3,131},{4,6},{5,133},{6,4},{7,135},{8,10},{9,... | collective-permute-start | bytes 98312 | tf_op jit(solution)/shard_map/ppermute | solution.py:41
  52.5 3.8 %collective-permute-done.10.came = f32[8,1024]{1,0:T(8,128)S(1)} collective-permute-done((f32[8,1024]{1,0:T(8,128)S(1)}, f32[8,1024]{1,0:T(8,128)S(1)}, u32[]{:S(2)}, u32[]{:S(2)}) %collective-permute-start.10) | collective-permute-done | bytes 32800 | tf_op jit(solution)/shard_map/ppermute | solution.py:41
  56.4 1.3 %collective-permute-start.11 = (f32[8,1024]{1,0:T(8,128)S(1)}, f32[8,1024]{1,0:T(8,128)S(1)}, u32[]{:S(2)}, u32[]{:S(2)}) collective-permute-start(f32[8,1024]{1,0:T(8,128)S(1)} %shard_map.66.own), channel_id=1, source_target_pairs={{0,4},{1,33},{2,6},{3,35},{4,0},{5,37},{6,2},{7,39},{8,12},{9,41},... | collective-permute-start | bytes 98312 | tf_op jit(solution)/shard_map/ppermute | solution.py:41
  57.7 1.7 %collective-permute-done.11.came = f32[8,1024]{1,0:T(8,128)S(1)} collective-permute-done((f32[8,1024]{1,0:T(8,128)S(1)}, f32[8,1024]{1,0:T(8,128)S(1)}, u32[]{:S(2)}, u32[]{:S(2)}) %collective-permute-start.11) | collective-permute-done | bytes 32800 | tf_op jit(solution)/shard_map/ppermute | solution.py:41
  60.1 2.1 %collective-permute-start.12 = (f32[8,1024]{1,0:T(8,128)S(1)}, f32[8,1024]{1,0:T(8,128)S(1)}, u32[]{:S(2)}, u32[]{:S(2)}) collective-permute-start(f32[8,1024]{1,0:T(8,128)S(1)} %shard_map.67.mine), channel_id=1, source_target_pairs={{0,1},{1,0},{2,3},{3,2},{4,5},{5,4},{6,7},{7,6},{8,9},{9,8},{10,11... | collective-permute-start | bytes 98312 | tf_op jit(solution)/shard_map/ppermute | solution.py:41
  63.1 2.2 %copy-done.1 = f32[1024,1024]{1,0:T(8,128)S(1)} copy-done((f32[1024,1024]{1,0:T(8,128)S(1)}, f32[1024,1024]{1,0:T(8,128)}, u32[]{:S(2)}) %copy-start.1) | copy-done | bytes 4194328
  65.3 3.4 %shard_map.68 = (bf16[1024,1024]{1,0:T(8,128)(2,1)S(1)}, f32[480,1024]{1,0:T(8,128)S(1)}, f32[72,1024]{1,0:T(8,128)S(1)}) custom-call(s32[4]{0:T(128)S(1)} %pad_add_fusion.place, f32[1024,1024]{1,0:T(8,128)S(1)} %copy-done.1, bf16[1024,1024]{1,0:T(8,128)(2,1)S(1)} %get-tuple-element.30.rows.regions, f32[8,1024]{1,0:T(8,128)S(1)} %shard_map.67.mine, ...), custom_call_target="tpu_custom_call" | custom-call | flops 44000002048 | bytes 120000000 | tf_op jit(solution)/shard_map/pallas_call | solution.py:62
  68.7 2.9 %shard_map.69 = (f32[264,1024]{1,0:T(8,128)S(1)}, f32[264,1024]{1,0:T(8,128)S(1)}, f32[264,1024]{1,0:T(8,128)S(1)}, f32[264,1024]{1,0:T(8,128)S(1)}) custom-call(s32[4]{0:T(128)S(1)} %pad_add_fusion.place, bf16[1024,1024]{1,0:T(8,128)(2,1)S(1)} %get-tuple-element.39.weights, bf16[1024,1024]{1,0:T(8,128)(2,1)S(1)} %copy-done.3, ...), custom_call_target="tpu_custom_call" | custom-call | flops 32999999488 | bytes 90000000 | tf_op jit(solution)/shard_map/pallas_call | solution.py:62
  72.5 2.8 %collective-permute-start.18 = (f16[264,1024]{1,0:T(8,128)(2,1)S(1)}, f16[264,1024]{1,0:T(8,128)(2,1)S(1)}, u32[]{:S(2)}, u32[]{:S(2)}) collective-permute-start(f16[264,1024]{1,0:T(8,128)(2,1)S(1)} %convert_element_type.71), channel_id=1, source_target_pairs={{0,16},{1,5},{2,18},{3,7},{4,20},{5,1},{6,22},{7,3},{8,24},{9,13},... | collective-permute-start | bytes 1622024 | tf_op jit(solution)/shard_map/ppermute | solution.py:41
  75.5 2.4 %collective-permute-start.20 = (f16[264,1024]{1,0:T(8,128)(2,1)S(1)}, f16[264,1024]{1,0:T(8,128)(2,1)S(1)}, u32[]{:S(2)}, u32[]{:S(2)}) collective-permute-start(f16[264,1024]{1,0:T(8,128)(2,1)S(1)} %convert_element_type.72), channel_id=1, source_target_pairs={{0,24},{1,7},{2,26},{3,1},{4,28},{5,3},{6,30},{7,5},{8,0},{9,15},{... | collective-permute-start | bytes 1622024 | tf_op jit(solution)/shard_map/ppermute | solution.py:41
  77.9 1.8 %shard_map.70 = (f32[272,1024]{1,0:T(8,128)S(1)}, f32[136,1024]{1,0:T(8,128)S(1)}, f32[136,1024]{1,0:T(8,128)S(1)}) custom-call(s32[4]{0:T(128)S(1)} %pad_add_fusion.place, bf16[1024,1024]{1,0:T(8,128)(2,1)S(1)} %get-tuple-element.39.weights, bf16[1024,1024]{1,0:T(8,128)(2,1)S(1)} %get-tuple-element.30.rows.regions, f32[8,1024]{1,0:T(8,128)S(1)} %shard_map.67.mine, ...), custom_call_target="tpu_custom_call" | custom-call | flops 22000001024 | bytes 60000000 | tf_op jit(solution)/shard_map/pallas_call | solution.py:62
  80.0 4.5 %collective-permute-start.14 = (f16[272,1024]{1,0:T(8,128)(2,1)S(1)}, f16[272,1024]{1,0:T(8,128)(2,1)S(1)}, u32[]{:S(2)}, u32[]{:S(2)}) collective-permute-start(f16[272,1024]{1,0:T(8,128)(2,1)S(1)} %add_convert_fusion), channel_id=1, source_target_pairs={{0,32},{1,225},{2,34},{3,227},{4,36},{5,229},{6,38},{7,231},{8,40}... | collective-permute-start | bytes 1671176 | tf_op jit(solution)/shard_map/ppermute | solution.py:41
  84.6 3.7 %collective-permute-done.19 = f16[264,1024]{1,0:T(8,128)(2,1)S(1)} collective-permute-done((f16[264,1024]{1,0:T(8,128)(2,1)S(1)}, f16[264,1024]{1,0:T(8,128)(2,1)S(1)}, u32[]{:S(2)}, u32[]{:S(2)}) %collective-permute-start.19) | collective-permute-done | bytes 540704 | tf_op jit(solution)/shard_map/ppermute | solution.py:41
  88.8 5.3 %collective-permute-done.15 = f16[72,1024]{1,0:T(8,128)(2,1)S(1)} collective-permute-done((f16[72,1024]{1,0:T(8,128)(2,1)S(1)}, f16[72,1024]{1,0:T(8,128)(2,1)S(1)}, u32[]{:S(2)}, u32[]{:S(2)}) %collective-permute-start.15) | collective-permute-done | bytes 147488 | tf_op jit(solution)/shard_map/ppermute | solution.py:41
  94.4 4.3 %collective-permute-start.16 = (f16[136,1024]{1,0:T(8,128)(2,1)S(1)}, f16[136,1024]{1,0:T(8,128)(2,1)S(1)}, u32[]{:S(2)}, u32[]{:S(2)}) collective-permute-start(f16[136,1024]{1,0:T(8,128)(2,1)S(1)} %fusion.2), channel_id=1, source_target_pairs={{0,64},{1,193},{2,66},{3,195},{4,68},{5,197},{6,70},{7,199},{8,72}... | collective-permute-start | bytes 835592 | tf_op jit(solution)/shard_map/ppermute | solution.py:41
  99.0 3.0 %collective-permute-start.21 = (f16[72,1024]{1,0:T(8,128)(2,1)S(1)}, f16[72,1024]{1,0:T(8,128)(2,1)S(1)}, u32[]{:S(2)}, u32[]{:S(2)}) collective-permute-start(f16[72,1024]{1,0:T(8,128)(2,1)S(1)} %get-tuple-element.57), channel_id=1, source_target_pairs={{0,4},{1,17},{2,6},{3,19},{4,0},{5,21},{6,2},{7,23},{8,12},{9,25},... | collective-permute-start | bytes 442376 | tf_op jit(solution)/shard_map/ppermute | solution.py:41
  102.4 2.3 %collective-permute-start.23 = (f16[72,1024]{1,0:T(8,128)(2,1)S(1)}, f16[72,1024]{1,0:T(8,128)(2,1)S(1)}, u32[]{:S(2)}, u32[]{:S(2)}) collective-permute-start(f16[72,1024]{1,0:T(8,128)(2,1)S(1)} %get-tuple-element.59), channel_id=1, source_target_pairs={{0,6},{1,25},{2,0},{3,27},{4,2},{5,29},{6,4},{7,31},{8,14},{9,1},{... | collective-permute-start | bytes 442376 | tf_op jit(solution)/shard_map/ppermute | solution.py:41
  105.2 5.1 %collective-permute-start.17 = (f32[136,1024]{1,0:T(8,128)S(1)}, f32[136,1024]{1,0:T(8,128)S(1)}, u32[]{:S(2)}, u32[]{:S(2)}) collective-permute-start(f32[136,1024]{1,0:T(8,128)S(1)} %convert_add_fusion), channel_id=1, source_target_pairs={{0,1},{1,0},{2,3},{3,2},{4,5},{5,4},{6,7},{7,6},{8,9},{9,8},{10,11... | collective-permute-start | bytes 1671176 | tf_op jit(solution)/shard_map/ppermute | solution.py:41
  (72 shorter events, 15.1 us)
Async XLA Ops:
  0.6 1.0 copy-start.5
  1.7 5.6 %copy-start.4 = (f32[512,1024]{1,0:T(8,128)S(1)}, f32[512,1024]{1,0:T(8,128)}, u32[]{:S(2)}) copy-start(f32[512,1024]{1,0:T(8,128)} %regions.3) | copy-start | bytes 6291460
  1.7 5.7 %copy-start.6 = (s32[512]{0:T(512)S(1)}, s32[512]{0:T(512)}, u32[]{:S(2)}) copy-start(s32[512]{0:T(512)} %param.5) | copy-start | bytes 6148
  1.7 10.4 %collective-permute-start.3 = (bf16[128,1024]{1,0:T(8,128)(2,1)S(1)}, bf16[128,1024]{1,0:T(8,128)(2,1)S(1)}, u32[]{:S(2)}, u32[]{:S(2)}) collective-permute-start(bf16[128,1024]{1,0:T(8,128)(2,1)S(1)} %shard_map.60.text), channel_id=1, source_target_pairs={{0,224},{1,33},{2,226},{3,35},{4,228},{5,37},{6,230},{7,39},{8,232... | collective-permute-start | bytes 786440 | tf_op jit(solution)/shard_map/ppermute | solution.py:41
  4.3 12.5 %collective-permute-start.4 = (bf16[128,1024]{1,0:T(8,128)(2,1)S(1)}, bf16[128,1024]{1,0:T(8,128)(2,1)S(1)}, u32[]{:S(2)}, u32[]{:S(2)}) collective-permute-start(bf16[128,1024]{1,0:T(8,128)(2,1)S(1)} %shard_map.60.text), channel_id=1, source_target_pairs={{0,192},{1,65},{2,194},{3,67},{4,196},{5,69},{6,198},{7,71},{8,200... | collective-permute-start | bytes 786440 | tf_op jit(solution)/shard_map/ppermute | solution.py:41
  8.0 9.4 %collective-permute-start.1 = (bf16[144,1024]{1,0:T(8,128)(2,1)S(1)}, bf16[144,1024]{1,0:T(8,128)(2,1)S(1)}, u32[]{:S(2)}, u32[]{:S(2)}) collective-permute-start(bf16[144,1024]{1,0:T(8,128)(2,1)S(1)} %shard_map.58.part), channel_id=1, source_target_pairs={{0,16},{1,17},{2,18},{3,19},{4,20},{5,21},{6,22},{7,23},{8,24},{9,... | collective-permute-start | bytes 884744 | tf_op jit(solution)/shard_map/ppermute | solution.py:41
  11.7 18.6 %collective-permute-start = (bf16[528,1024]{1,0:T(8,128)(2,1)S(1)}, bf16[528,1024]{1,0:T(8,128)(2,1)S(1)}, u32[]{:S(2)}, u32[]{:S(2)}) collective-permute-start(bf16[528,1024]{1,0:T(8,128)(2,1)S(1)} %shard_map.59.own), channel_id=1, source_target_pairs={{0,24},{1,9},{2,26},{3,11},{4,28},{5,13},{6,30},{7,15},{8,0},{9,17... | collective-permute-start | bytes 3244040 | tf_op jit(solution)/shard_map/ppermute | solution.py:41
  17.4 8.9 %collective-permute-start.5 = (bf16[192,1024]{1,0:T(8,128)(2,1)S(1)}, bf16[192,1024]{1,0:T(8,128)(2,1)S(1)}, u32[]{:S(2)}, u32[]{:S(2)}) collective-permute-start(bf16[192,1024]{1,0:T(8,128)(2,1)S(1)} %shard_map.61), channel_id=1, source_target_pairs={{0,192},{1,65},{2,194},{3,67},{4,196},{5,69},{6,198},{7,71},{8,200... | collective-permute-start | bytes 1179656 | tf_op jit(solution)/shard_map/ppermute | solution.py:41
  17.5 5.6 %collective-permute-start.2 = (bf16[128,1024]{1,0:T(8,128)(2,1)S(1)}, bf16[128,1024]{1,0:T(8,128)(2,1)S(1)}, u32[]{:S(2)}, u32[]{:S(2)}) collective-permute-start(bf16[128,1024]{1,0:T(8,128)(2,1)S(1)} %slice.73), channel_id=1, source_target_pairs={{0,2},{1,3},{2,0},{3,1},{4,6},{5,7},{6,4},{7,5},{8,10},{9,11},{10,... | collective-permute-start | bytes 786440 | tf_op jit(solution)/shard_map/ppermute | solution.py:41
  30.4 4.3 %collective-permute-start.6 = (bf16[720,1024]{1,0:T(8,128)(2,1)S(1)}, bf16[720,1024]{1,0:T(8,128)(2,1)S(1)}, u32[]{:S(2)}, u32[]{:S(2)}) collective-permute-start(bf16[720,1024]{1,0:T(8,128)(2,1)S(1)} %pad_maximum_fusion), channel_id=1, source_target_pairs={{0,1},{1,0},{2,3},{3,2},{4,5},{5,4},{6,7},{7,6},{8,9},{9,8},{10,11... | collective-permute-start | bytes 4423688 | tf_op jit(solution)/shard_map/ppermute | solution.py:41
  39.9 19.6 %copy-start = (f32[1024,1024]{1,0:T(8,128)}, f32[1024,1024]{1,0:T(8,128)S(1)}, u32[]{:S(2)}) copy-start(f32[1024,1024]{1,0:T(8,128)S(1)} %get-tuple-element.29.held.scores) | copy-start | bytes 12582916
  39.9 19.5 %copy-start.2 = (bf16[1024,1024]{1,0:T(8,128)(2,1)}, bf16[1024,1024]{1,0:T(8,128)(2,1)S(1)}, u32[]{:S(2)}) copy-start(bf16[1024,1024]{1,0:T(8,128)(2,1)S(1)} %get-tuple-element.33.captions) | copy-start | bytes 6291460
  39.9 1.3 %collective-permute-start.7 = (f32[8,1024]{1,0:T(8,128)S(1)}, f32[8,1024]{1,0:T(8,128)S(1)}, u32[]{:S(2)}, u32[]{:S(2)}) collective-permute-start(f32[8,1024]{1,0:T(8,128)S(1)} %get-tuple-element.32), channel_id=1, source_target_pairs={{0,1},{1,0},{2,3},{3,2},{4,5},{5,4},{6,7},{7,6},{8,9},{9,8},{10,11... | collective-permute-start | bytes 98312 | tf_op jit(solution)/shard_map/ppermute | solution.py:41
  41.8 3.9 %collective-permute-start.8 = (f32[8,1024]{1,0:T(8,128)S(1)}, f32[8,1024]{1,0:T(8,128)S(1)}, u32[]{:S(2)}, u32[]{:S(2)}) collective-permute-start(f32[8,1024]{1,0:T(8,128)S(1)} %shard_map.63.own), channel_id=1, source_target_pairs={{0,8},{1,33},{2,10},{3,35},{4,12},{5,37},{6,14},{7,39},{8,0},{9,41... | collective-permute-start | bytes 98312 | tf_op jit(solution)/shard_map/ppermute | solution.py:41
  45.7 3.8 %collective-permute-start.9 = (f32[8,1024]{1,0:T(8,128)S(1)}, f32[8,1024]{1,0:T(8,128)S(1)}, u32[]{:S(2)}, u32[]{:S(2)}) collective-permute-start(f32[8,1024]{1,0:T(8,128)S(1)} %shard_map.64.own), channel_id=1, source_target_pairs={{0,16},{1,65},{2,18},{3,67},{4,20},{5,69},{6,22},{7,71},{8,24},{9,... | collective-permute-start | bytes 98312 | tf_op jit(solution)/shard_map/ppermute | solution.py:41
  49.5 6.9 %collective-permute-start.10 = (f32[8,1024]{1,0:T(8,128)S(1)}, f32[8,1024]{1,0:T(8,128)S(1)}, u32[]{:S(2)}, u32[]{:S(2)}) collective-permute-start(f32[8,1024]{1,0:T(8,128)S(1)} %shard_map.65.own), channel_id=1, source_target_pairs={{0,2},{1,129},{2,0},{3,131},{4,6},{5,133},{6,4},{7,135},{8,10},{9,... | collective-permute-start | bytes 98312 | tf_op jit(solution)/shard_map/ppermute | solution.py:41
  56.4 3.0 %collective-permute-start.11 = (f32[8,1024]{1,0:T(8,128)S(1)}, f32[8,1024]{1,0:T(8,128)S(1)}, u32[]{:S(2)}, u32[]{:S(2)}) collective-permute-start(f32[8,1024]{1,0:T(8,128)S(1)} %shard_map.66.own), channel_id=1, source_target_pairs={{0,4},{1,33},{2,6},{3,35},{4,0},{5,37},{6,2},{7,39},{8,12},{9,41},... | collective-permute-start | bytes 98312 | tf_op jit(solution)/shard_map/ppermute | solution.py:41
  60.1 2.9 %collective-permute-start.12 = (f32[8,1024]{1,0:T(8,128)S(1)}, f32[8,1024]{1,0:T(8,128)S(1)}, u32[]{:S(2)}, u32[]{:S(2)}) collective-permute-start(f32[8,1024]{1,0:T(8,128)S(1)} %shard_map.67.mine), channel_id=1, source_target_pairs={{0,1},{1,0},{2,3},{3,2},{4,5},{5,4},{6,7},{7,6},{8,9},{9,8},{10,11... | collective-permute-start | bytes 98312 | tf_op jit(solution)/shard_map/ppermute | solution.py:41
  63.1 2.2 %copy-start.1 = (f32[1024,1024]{1,0:T(8,128)S(1)}, f32[1024,1024]{1,0:T(8,128)}, u32[]{:S(2)}) copy-start(f32[1024,1024]{1,0:T(8,128)} %copy-done) | copy-start | bytes 12582916
  65.2 3.4 %copy-start.3 = (bf16[1024,1024]{1,0:T(8,128)(2,1)S(1)}, bf16[1024,1024]{1,0:T(8,128)(2,1)}, u32[]{:S(2)}) copy-start(bf16[1024,1024]{1,0:T(8,128)(2,1)} %copy-done.2) | copy-start | bytes 6291460
  72.1 7.7 %collective-permute-start.13 = (f16[480,1024]{1,0:T(8,128)(2,1)S(1)}, f16[480,1024]{1,0:T(8,128)(2,1)S(1)}, u32[]{:S(2)}, u32[]{:S(2)}) collective-permute-start(f16[480,1024]{1,0:T(8,128)(2,1)S(1)} %convert_element_type.73), channel_id=1, source_target_pairs={{0,1},{1,0},{2,3},{3,2},{4,5},{5,4},{6,7},{7,6},{8,9},{9,8},{10,11... | collective-permute-start | bytes 2949128 | tf_op jit(solution)/shard_map/ppermute | solution.py:41
  72.5 12.1 %collective-permute-start.18 = (f16[264,1024]{1,0:T(8,128)(2,1)S(1)}, f16[264,1024]{1,0:T(8,128)(2,1)S(1)}, u32[]{:S(2)}, u32[]{:S(2)}) collective-permute-start(f16[264,1024]{1,0:T(8,128)(2,1)S(1)} %convert_element_type.71), channel_id=1, source_target_pairs={{0,16},{1,5},{2,18},{3,7},{4,20},{5,1},{6,22},{7,3},{8,24},{9,13},... | collective-permute-start | bytes 1622024 | tf_op jit(solution)/shard_map/ppermute | solution.py:41
  75.2 13.0 %collective-permute-start.19 = (f16[264,1024]{1,0:T(8,128)(2,1)S(1)}, f16[264,1024]{1,0:T(8,128)(2,1)S(1)}, u32[]{:S(2)}, u32[]{:S(2)}) collective-permute-start(f16[264,1024]{1,0:T(8,128)(2,1)S(1)} %convert_element_type.70), channel_id=1, source_target_pairs={{0,8},{1,3},{2,10},{3,5},{4,12},{5,7},{6,14},{7,1},{8,16},{9,11},{... | collective-permute-start | bytes 1622024 | tf_op jit(solution)/shard_map/ppermute | solution.py:41
  75.5 12.9 %collective-permute-start.20 = (f16[264,1024]{1,0:T(8,128)(2,1)S(1)}, f16[264,1024]{1,0:T(8,128)(2,1)S(1)}, u32[]{:S(2)}, u32[]{:S(2)}) collective-permute-start(f16[264,1024]{1,0:T(8,128)(2,1)S(1)} %convert_element_type.72), channel_id=1, source_target_pairs={{0,24},{1,7},{2,26},{3,1},{4,28},{5,3},{6,30},{7,5},{8,0},{9,15},{... | collective-permute-start | bytes 1622024 | tf_op jit(solution)/shard_map/ppermute | solution.py:41
  80.0 14.2 %collective-permute-start.14 = (f16[272,1024]{1,0:T(8,128)(2,1)S(1)}, f16[272,1024]{1,0:T(8,128)(2,1)S(1)}, u32[]{:S(2)}, u32[]{:S(2)}) collective-permute-start(f16[272,1024]{1,0:T(8,128)(2,1)S(1)} %add_convert_fusion), channel_id=1, source_target_pairs={{0,32},{1,225},{2,34},{3,227},{4,36},{5,229},{6,38},{7,231},{8,40}... | collective-permute-start | bytes 1671176 | tf_op jit(solution)/shard_map/ppermute | solution.py:41
  84.5 9.6 %collective-permute-start.15 = (f16[72,1024]{1,0:T(8,128)(2,1)S(1)}, f16[72,1024]{1,0:T(8,128)(2,1)S(1)}, u32[]{:S(2)}, u32[]{:S(2)}) collective-permute-start(f16[72,1024]{1,0:T(8,128)(2,1)S(1)} %add_convert_fusion.1), channel_id=1, source_target_pairs={{0,64},{1,193},{2,66},{3,195},{4,68},{5,197},{6,70},{7,199},{8,72}... | collective-permute-start | bytes 442376 | tf_op jit(solution)/shard_map/ppermute | solution.py:41
  94.4 10.7 %collective-permute-start.16 = (f16[136,1024]{1,0:T(8,128)(2,1)S(1)}, f16[136,1024]{1,0:T(8,128)(2,1)S(1)}, u32[]{:S(2)}, u32[]{:S(2)}) collective-permute-start(f16[136,1024]{1,0:T(8,128)(2,1)S(1)} %fusion.2), channel_id=1, source_target_pairs={{0,64},{1,193},{2,66},{3,195},{4,68},{5,197},{6,70},{7,199},{8,72}... | collective-permute-start | bytes 835592 | tf_op jit(solution)/shard_map/ppermute | solution.py:41
  99.0 11.3 %collective-permute-start.21 = (f16[72,1024]{1,0:T(8,128)(2,1)S(1)}, f16[72,1024]{1,0:T(8,128)(2,1)S(1)}, u32[]{:S(2)}, u32[]{:S(2)}) collective-permute-start(f16[72,1024]{1,0:T(8,128)(2,1)S(1)} %get-tuple-element.57), channel_id=1, source_target_pairs={{0,4},{1,17},{2,6},{3,19},{4,0},{5,21},{6,2},{7,23},{8,12},{9,25},... | collective-permute-start | bytes 442376 | tf_op jit(solution)/shard_map/ppermute | solution.py:41
  102.0 8.3 %collective-permute-start.22 = (f16[72,1024]{1,0:T(8,128)(2,1)S(1)}, f16[72,1024]{1,0:T(8,128)(2,1)S(1)}, u32[]{:S(2)}, u32[]{:S(2)}) collective-permute-start(f16[72,1024]{1,0:T(8,128)(2,1)S(1)} %get-tuple-element.58), channel_id=1, source_target_pairs={{0,2},{1,9},{2,4},{3,11},{4,6},{5,13},{6,0},{7,15},{8,10},{9,17},{... | collective-permute-start | bytes 442376 | tf_op jit(solution)/shard_map/ppermute | solution.py:41
  102.4 7.9 %collective-permute-start.23 = (f16[72,1024]{1,0:T(8,128)(2,1)S(1)}, f16[72,1024]{1,0:T(8,128)(2,1)S(1)}, u32[]{:S(2)}, u32[]{:S(2)}) collective-permute-start(f16[72,1024]{1,0:T(8,128)(2,1)S(1)} %get-tuple-element.59), channel_id=1, source_target_pairs={{0,6},{1,25},{2,0},{3,27},{4,2},{5,29},{6,4},{7,31},{8,14},{9,1},{... | collective-permute-start | bytes 442376 | tf_op jit(solution)/shard_map/ppermute | solution.py:41
  105.2 6.7 %collective-permute-start.17 = (f32[136,1024]{1,0:T(8,128)S(1)}, f32[136,1024]{1,0:T(8,128)S(1)}, u32[]{:S(2)}, u32[]{:S(2)}) collective-permute-start(f32[136,1024]{1,0:T(8,128)S(1)} %convert_add_fusion), channel_id=1, source_target_pairs={{0,1},{1,0},{2,3},{3,2},{4,5},{5,4},{6,7},{7,6},{8,9},{9,8},{10,11... | collective-permute-start | bytes 1671176 | tf_op jit(solution)/shard_map/ppermute | solution.py:41

commit v4 on v3

--- a/solution.py
+++ b/solution.py
@@ -346,18 +346,15 @@
     return head_room / jnp.maximum(region_top, tiny)
 
 
-def caption_kernel(place, weights, regions, mine, came, near_two, second, own):
+def caption_kernel(place, weights, regions, mine, came, first, third, second, own):
     first_core = place[3] == 0
     part = jnp.dot(
         weights[512:1024, :], regions[...], preferred_element_type=F32
     ) * region_scale(place, mine, came)
     code = digits(jnp.where(first_core, mine[4:5, :], came[4:5, :]), place[0])
-    near_two[0:128, :] = part[0:128, :]
-    near_two[128:136, :] = code
-    near_two[136:264, :] = part[128:256, :]
-    near_two[264:272, :] = code
-    second[0:128, :] = part[256:384, :]
-    second[128:136, :] = code
+    for at, ref in enumerate((first, third, second)):
+        ref[0:128, :] = part[at * 128 : (at + 1) * 128, :]
+        ref[128:136, :] = code
     own[0:128, :] = part[384:512, :]
     own[128:136, :] = jnp.where(first_core, code, 0.0)
 
@@ -442,15 +439,17 @@
     weights, r1, r2, r3 = lax.optimization_barrier(
         (weights, r1.astype(WIRE), r2.astype(WIRE), r3.astype(WIRE))
     )
-    near_two, second, own = call(
+    block = ((136, FEATURES), F32)
+    first, third, second, own = call(
         caption_kernel,
-        [((272, FEATURES), F32), ((136, FEATURES), F32), ((136, FEATURES), F32)],
+        [block] * 4,
         place, weights, region_rows, lse, came,
         us=20.0,
         limit=6 << 20,
     )
-    ahead = along_z((near_two + got[0:272].astype(F32)).astype(WIRE), 1)
+    third = along_z((third + got[136:272].astype(F32)).astype(WIRE), 1)
     skipped = along_z((kept_half + got[408:480].astype(F32)).astype(WIRE), 2)
+    ahead = along_z((first + got[0:136].astype(F32)).astype(WIRE), 1)
 
     def major_from(value, by):
         return moved(
@@ -469,7 +468,7 @@
         jnp.concatenate([late[0:64], nothing, late[64:72]], axis=0),
         jnp.concatenate([nothing, late], axis=0),
     )
-    onward = (second + got[272:408].astype(F32)) + (ahead[136:272].astype(F32) + late)
+    onward = (second + got[272:408].astype(F32)) + (third.astype(F32) + late)
     passed = along_z(onward.astype(WIRE), 2)
     q2 = major_from(r2, 2)
     q1 = major_from(r1, 1)
@@ -483,7 +482,7 @@
         return jnp.concatenate([block, summed[256:264]], axis=0)
 
     t2, t1, t3 = (minor_from(piece(by).astype(WIRE), by) for by in (2, 1, 3))
-    mine = (own + ahead[0:136].astype(F32)) + passed.astype(F32)
+    mine = (own + ahead.astype(F32)) + passed.astype(F32)
     both = mine + swapped(mine)
     all_regions = (piece(0) + t2.astype(F32)) + (t1.astype(F32) + t3.astype(F32))
 

time: 115 us -> 112 us (0.974)
  waiting for transfers between devices: 39.6 us -> 35.7 us
    ppermute x24 -> x25, waiting for transfers between devices: 39.6 us -> 35.7 us  [moved(): return lax.ppermute(value, AXES, pairs)]
    ppermute x24 -> x25, starting transfers between devices: 48.6 us -> 49.4 us  [moved(): return lax.ppermute(value, AXES, pairs)]
  transfers between devices with their start and end apart: 24 -> 25, of which waited for: 16 -> 15; matrix products, arithmetic and copies ran while one was open for 2% -> 2% of each run, Pallas kernels for 3% -> 3%
where the time goes in v4:
time: 112 us
  starting transfers between devices  49.4 us (44%)
  waiting for transfers between devices  35.7 us (32%)
  Pallas kernels  16.5 us (15%)
  other arithmetic  4.13 us (4%)
  local copies, waits for them, and re-layouts  3.5 us (3%)
  between operations  2.75 us (2%)
    ppermute x25, starting transfers between devices, moved(): return lax.ppermute(value, AXES, pairs)  49.4 us
    ppermute x25, waiting for transfers between devices, moved(): return lax.ppermute(value, AXES, pairs)  35.7 us
    pallas_call x13, Pallas kernels, call(): pl.pallas_call(kernel, in_specs=specs, out_specs=[pl.BlockSpec(memory_spa...  16.5 us
    unnamed x14, local copies, waits for them, and re-layouts  3.24 us
  transfers between devices with their start and end apart: 25, of which 15 were waited for; matrix products, arithmetic and copies ran while one was open for 2% of the time, Pallas kernels for 3%

profile of v4, /device:TPU:1, one launch (start us, length us, event | category | flops | bytes accessed | tf_op | source)
XLA Modules:
  0.0 111.9 jit_solution(8643907792708139639)
XLA Ops:
  1.7 2.5 %collective-permute-start.3 = (bf16[128,1024]{1,0:T(8,128)(2,1)S(1)}, bf16[128,1024]{1,0:T(8,128)(2,1)S(1)}, u32[]{:S(2)}, u32[]{:S(2)}) collective-permute-start(bf16[128,1024]{1,0:T(8,128)(2,1)S(1)} %shard_map.60.text), channel_id=1, source_target_pairs={{0,224},{1,33},{2,226},{3,35},{4,228},{5,37},{6,230},{7,39},{8,232... | collective-permute-start | bytes 786440 | tf_op jit(solution)/shard_map/ppermute | solution.py:41
  4.3 3.0 %collective-permute-start.4 = (bf16[128,1024]{1,0:T(8,128)(2,1)S(1)}, bf16[128,1024]{1,0:T(8,128)(2,1)S(1)}, u32[]{:S(2)}, u32[]{:S(2)}) collective-permute-start(bf16[128,1024]{1,0:T(8,128)(2,1)S(1)} %shard_map.60.text), channel_id=1, source_target_pairs={{0,192},{1,65},{2,194},{3,67},{4,196},{5,69},{6,198},{7,71},{8,200... | collective-permute-start | bytes 786440 | tf_op jit(solution)/shard_map/ppermute | solution.py:41
  8.0 3.0 %collective-permute-start.1 = (bf16[144,1024]{1,0:T(8,128)(2,1)S(1)}, bf16[144,1024]{1,0:T(8,128)(2,1)S(1)}, u32[]{:S(2)}, u32[]{:S(2)}) collective-permute-start(bf16[144,1024]{1,0:T(8,128)(2,1)S(1)} %shard_map.58.part), channel_id=1, source_target_pairs={{0,16},{1,17},{2,18},{3,19},{4,20},{5,21},{6,22},{7,23},{8,24},{9,... | collective-permute-start | bytes 884744 | tf_op jit(solution)/shard_map/ppermute | solution.py:41
  12.1 4.6 %collective-permute-done.4.two = bf16[128,1024]{1,0:T(8,128)(2,1)S(1)} collective-permute-done((bf16[128,1024]{1,0:T(8,128)(2,1)S(1)}, bf16[128,1024]{1,0:T(8,128)(2,1)S(1)}, u32[]{:S(2)}, u32[]{:S(2)}) %collective-permute-start.4) | collective-permute-done | bytes 262176 | tf_op jit(solution)/shard_map/ppermute | solution.py:41
  18.8 4.3 %collective-permute-done.2.other = bf16[128,1024]{1,0:T(8,128)(2,1)S(1)} collective-permute-done((bf16[128,1024]{1,0:T(8,128)(2,1)S(1)}, bf16[128,1024]{1,0:T(8,128)(2,1)S(1)}, u32[]{:S(2)}, u32[]{:S(2)}) %collective-permute-start.2) | collective-permute-done | bytes 262176 | tf_op jit(solution)/shard_map/ppermute | solution.py:41
  23.1 3.2 %collective-permute-done.5.skip = bf16[192,1024]{1,0:T(8,128)(2,1)S(1)} collective-permute-done((bf16[192,1024]{1,0:T(8,128)(2,1)S(1)}, bf16[192,1024]{1,0:T(8,128)(2,1)S(1)}, u32[]{:S(2)}, u32[]{:S(2)}) %collective-permute-start.5) | collective-permute-done | bytes 393248 | tf_op jit(solution)/shard_map/ppermute | solution.py:41
  26.3 4.0 %collective-permute-done.full = bf16[528,1024]{1,0:T(8,128)(2,1)S(1)} collective-permute-done((bf16[528,1024]{1,0:T(8,128)(2,1)S(1)}, bf16[528,1024]{1,0:T(8,128)(2,1)S(1)}, u32[]{:S(2)}, u32[]{:S(2)}) %collective-permute-start) | collective-permute-done | bytes 1081376 | tf_op jit(solution)/shard_map/ppermute | solution.py:41
  30.4 1.4 %collective-permute-start.6 = (bf16[720,1024]{1,0:T(8,128)(2,1)S(1)}, bf16[720,1024]{1,0:T(8,128)(2,1)S(1)}, u32[]{:S(2)}, u32[]{:S(2)}) collective-permute-start(bf16[720,1024]{1,0:T(8,128)(2,1)S(1)} %pad_maximum_fusion), channel_id=1, source_target_pairs={{0,1},{1,0},{2,3},{3,2},{4,5},{5,4},{6,7},{7,6},{8,9},{9,8},{10,11... | collective-permute-start | bytes 4423688 | tf_op jit(solution)/shard_map/ppermute | solution.py:41
  31.9 2.9 %collective-permute-done.6.far = bf16[720,1024]{1,0:T(8,128)(2,1)S(1)} collective-permute-done((bf16[720,1024]{1,0:T(8,128)(2,1)S(1)}, bf16[720,1024]{1,0:T(8,128)(2,1)S(1)}, u32[]{:S(2)}, u32[]{:S(2)}) %collective-permute-start.6) | collective-permute-done | bytes 1474592 | tf_op jit(solution)/shard_map/ppermute | solution.py:41
  34.8 5.1 %shard_map.62 = (f32[1024,1024]{1,0:T(8,128)S(1)}, bf16[1024,1024]{1,0:T(8,128)(2,1)S(1)}, bf16[1024,1024]{1,0:T(8,128)(2,1)S(1)}, s32[8,1024]{1,0:T(8,128)S(1)}...) custom-call(s32[4]{0:T(128)S(1)} %pad_add_fusion.place, bf16[528,1024]{1,0:T(8,128)(2,1)S(1)} %shard_map.59.own, ...), custom_call_target="tpu_custom_call" | custom-call | flops 8800000000 | bytes 24000000 | tf_op jit(solution)/shard_map/pallas_call | solution.py:62
  41.8 2.3 %collective-permute-start.8 = (f32[8,1024]{1,0:T(8,128)S(1)}, f32[8,1024]{1,0:T(8,128)S(1)}, u32[]{:S(2)}, u32[]{:S(2)}) collective-permute-start(f32[8,1024]{1,0:T(8,128)S(1)} %shard_map.63.own), channel_id=1, source_target_pairs={{0,8},{1,33},{2,10},{3,35},{4,12},{5,37},{6,14},{7,39},{8,0},{9,41... | collective-permute-start | bytes 98312 | tf_op jit(solution)/shard_map/ppermute | solution.py:41
  44.1 1.6 %collective-permute-done.8.came = f32[8,1024]{1,0:T(8,128)S(1)} collective-permute-done((f32[8,1024]{1,0:T(8,128)S(1)}, f32[8,1024]{1,0:T(8,128)S(1)}, u32[]{:S(2)}, u32[]{:S(2)}) %collective-permute-start.8) | collective-permute-done | bytes 32800 | tf_op jit(solution)/shard_map/ppermute | solution.py:41
  45.7 2.1 %collective-permute-start.9 = (f32[8,1024]{1,0:T(8,128)S(1)}, f32[8,1024]{1,0:T(8,128)S(1)}, u32[]{:S(2)}, u32[]{:S(2)}) collective-permute-start(f32[8,1024]{1,0:T(8,128)S(1)} %shard_map.64.own), channel_id=1, source_target_pairs={{0,16},{1,65},{2,18},{3,67},{4,20},{5,69},{6,22},{7,71},{8,24},{9,... | collective-permute-start | bytes 98312 | tf_op jit(solution)/shard_map/ppermute | solution.py:41
  47.8 1.7 %collective-permute-done.9.came = f32[8,1024]{1,0:T(8,128)S(1)} collective-permute-done((f32[8,1024]{1,0:T(8,128)S(1)}, f32[8,1024]{1,0:T(8,128)S(1)}, u32[]{:S(2)}, u32[]{:S(2)}) %collective-permute-start.9) | collective-permute-done | bytes 32800 | tf_op jit(solution)/shard_map/ppermute | solution.py:41
  49.5 3.0 %collective-permute-start.10 = (f32[8,1024]{1,0:T(8,128)S(1)}, f32[8,1024]{1,0:T(8,128)S(1)}, u32[]{:S(2)}, u32[]{:S(2)}) collective-permute-start(f32[8,1024]{1,0:T(8,128)S(1)} %shard_map.65.own), channel_id=1, source_target_pairs={{0,2},{1,129},{2,0},{3,131},{4,6},{5,133},{6,4},{7,135},{8,10},{9,... | collective-permute-start | bytes 98312 | tf_op jit(solution)/shard_map/ppermute | solution.py:41
  52.5 3.8 %collective-permute-done.10.came = f32[8,1024]{1,0:T(8,128)S(1)} collective-permute-done((f32[8,1024]{1,0:T(8,128)S(1)}, f32[8,1024]{1,0:T(8,128)S(1)}, u32[]{:S(2)}, u32[]{:S(2)}) %collective-permute-start.10) | collective-permute-done | bytes 32800 | tf_op jit(solution)/shard_map/ppermute | solution.py:41
  57.7 1.7 %collective-permute-done.11.came = f32[8,1024]{1,0:T(8,128)S(1)} collective-permute-done((f32[8,1024]{1,0:T(8,128)S(1)}, f32[8,1024]{1,0:T(8,128)S(1)}, u32[]{:S(2)}, u32[]{:S(2)}) %collective-permute-start.11) | collective-permute-done | bytes 32800 | tf_op jit(solution)/shard_map/ppermute | solution.py:41
  60.1 2.1 %collective-permute-start.12 = (f32[8,1024]{1,0:T(8,128)S(1)}, f32[8,1024]{1,0:T(8,128)S(1)}, u32[]{:S(2)}, u32[]{:S(2)}) collective-permute-start(f32[8,1024]{1,0:T(8,128)S(1)} %shard_map.67.mine), channel_id=1, source_target_pairs={{0,1},{1,0},{2,3},{3,2},{4,5},{5,4},{6,7},{7,6},{8,9},{9,8},{10,11... | collective-permute-start | bytes 98312 | tf_op jit(solution)/shard_map/ppermute | solution.py:41
  63.1 2.2 %copy-done.1 = f32[1024,1024]{1,0:T(8,128)S(1)} copy-done((f32[1024,1024]{1,0:T(8,128)S(1)}, f32[1024,1024]{1,0:T(8,128)}, u32[]{:S(2)}) %copy-start.1) | copy-done | bytes 4194328
  65.3 3.4 %shard_map.68 = (bf16[1024,1024]{1,0:T(8,128)(2,1)S(1)}, f32[480,1024]{1,0:T(8,128)S(1)}, f32[72,1024]{1,0:T(8,128)S(1)}) custom-call(s32[4]{0:T(128)S(1)} %pad_add_fusion.place, f32[1024,1024]{1,0:T(8,128)S(1)} %copy-done.1, bf16[1024,1024]{1,0:T(8,128)(2,1)S(1)} %get-tuple-element.31.rows.regions, f32[8,1024]{1,0:T(8,128)S(1)} %shard_map.67.mine, ...), custom_call_target="tpu_custom_call" | custom-call | flops 44000002048 | bytes 120000000 | tf_op jit(solution)/shard_map/pallas_call | solution.py:62
  68.7 2.9 %shard_map.69 = (f32[264,1024]{1,0:T(8,128)S(1)}, f32[264,1024]{1,0:T(8,128)S(1)}, f32[264,1024]{1,0:T(8,128)S(1)}, f32[264,1024]{1,0:T(8,128)S(1)}) custom-call(s32[4]{0:T(128)S(1)} %pad_add_fusion.place, bf16[1024,1024]{1,0:T(8,128)(2,1)S(1)} %get-tuple-element.40.weights, bf16[1024,1024]{1,0:T(8,128)(2,1)S(1)} %copy-done.3, ...), custom_call_target="tpu_custom_call" | custom-call | flops 32999999488 | bytes 90000000 | tf_op jit(solution)/shard_map/pallas_call | solution.py:62
  72.5 2.8 %collective-permute-start.19 = (f16[264,1024]{1,0:T(8,128)(2,1)S(1)}, f16[264,1024]{1,0:T(8,128)(2,1)S(1)}, u32[]{:S(2)}, u32[]{:S(2)}) collective-permute-start(f16[264,1024]{1,0:T(8,128)(2,1)S(1)} %convert_element_type.77), channel_id=1, source_target_pairs={{0,16},{1,5},{2,18},{3,7},{4,20},{5,1},{6,22},{7,3},{8,24},{9,13},... | collective-permute-start | bytes 1622024 | tf_op jit(solution)/shard_map/ppermute | solution.py:41
  75.5 2.4 %collective-permute-start.21 = (f16[264,1024]{1,0:T(8,128)(2,1)S(1)}, f16[264,1024]{1,0:T(8,128)(2,1)S(1)}, u32[]{:S(2)}, u32[]{:S(2)}) collective-permute-start(f16[264,1024]{1,0:T(8,128)(2,1)S(1)} %convert_element_type.78), channel_id=1, source_target_pairs={{0,24},{1,7},{2,26},{3,1},{4,28},{5,3},{6,30},{7,5},{8,0},{9,15},{... | collective-permute-start | bytes 1622024 | tf_op jit(solution)/shard_map/ppermute | solution.py:41
  77.9 1.8 %shard_map.70 = (f32[136,1024]{1,0:T(8,128)S(1)}, f32[136,1024]{1,0:T(8,128)S(1)}, f32[136,1024]{1,0:T(8,128)S(1)}, f32[136,1024]{1,0:T(8,128)S(1)}) custom-call(s32[4]{0:T(128)S(1)} %pad_add_fusion.place, bf16[1024,1024]{1,0:T(8,128)(2,1)S(1)} %get-tuple-element.40.weights, bf16[1024,1024]{1,0:T(8,128)(2,1)S(1)} %get-tuple-element.31.rows.regions, ...), custom_call_target="tpu_custom_call" | custom-call | flops 22000001024 | bytes 60000000 | tf_op jit(solution)/shard_map/pallas_call | solution.py:62
  80.0 4.5 %collective-permute-start.15 = (f16[136,1024]{1,0:T(8,128)(2,1)S(1)}, f16[136,1024]{1,0:T(8,128)(2,1)S(1)}, u32[]{:S(2)}, u32[]{:S(2)}) collective-permute-start(f16[136,1024]{1,0:T(8,128)(2,1)S(1)} %get-tuple-element.58), channel_id=1, source_target_pairs={{0,32},{1,225},{2,34},{3,227},{4,36},{5,229},{6,38},{7,231},{8,40}... | collective-permute-start | bytes 835592 | tf_op jit(solution)/shard_map/ppermute | solution.py:41
  84.6 3.7 %collective-permute-done.20 = f16[264,1024]{1,0:T(8,128)(2,1)S(1)} collective-permute-done((f16[264,1024]{1,0:T(8,128)(2,1)S(1)}, f16[264,1024]{1,0:T(8,128)(2,1)S(1)}, u32[]{:S(2)}, u32[]{:S(2)}) %collective-permute-start.20) | collective-permute-done | bytes 540704 | tf_op jit(solution)/shard_map/ppermute | solution.py:41
  88.8 4.5 %collective-permute-start.14 = (f16[136,1024]{1,0:T(8,128)(2,1)S(1)}, f16[136,1024]{1,0:T(8,128)(2,1)S(1)}, u32[]{:S(2)}, u32[]{:S(2)}) collective-permute-start(f16[136,1024]{1,0:T(8,128)(2,1)S(1)} %get-tuple-element.57), channel_id=1, source_target_pairs={{0,32},{1,225},{2,34},{3,227},{4,36},{5,229},{6,38},{7,231},{8,40}... | collective-permute-start | bytes 835592 | tf_op jit(solution)/shard_map/ppermute | solution.py:41
  93.6 2.1 %collective-permute-start.17 = (f16[136,1024]{1,0:T(8,128)(2,1)S(1)}, f16[136,1024]{1,0:T(8,128)(2,1)S(1)}, u32[]{:S(2)}, u32[]{:S(2)}) collective-permute-start(f16[136,1024]{1,0:T(8,128)(2,1)S(1)} %fusion.2), channel_id=1, source_target_pairs={{0,64},{1,193},{2,66},{3,195},{4,68},{5,197},{6,70},{7,199},{8,72}... | collective-permute-start | bytes 835592 | tf_op jit(solution)/shard_map/ppermute | solution.py:41
  96.0 3.0 %collective-permute-start.22 = (f16[72,1024]{1,0:T(8,128)(2,1)S(1)}, f16[72,1024]{1,0:T(8,128)(2,1)S(1)}, u32[]{:S(2)}, u32[]{:S(2)}) collective-permute-start(f16[72,1024]{1,0:T(8,128)(2,1)S(1)} %get-tuple-element.61), channel_id=1, source_target_pairs={{0,4},{1,17},{2,6},{3,19},{4,0},{5,21},{6,2},{7,23},{8,12},{9,25},... | collective-permute-start | bytes 442376 | tf_op jit(solution)/shard_map/ppermute | solution.py:41
  99.4 2.3 %collective-permute-start.24 = (f16[72,1024]{1,0:T(8,128)(2,1)S(1)}, f16[72,1024]{1,0:T(8,128)(2,1)S(1)}, u32[]{:S(2)}, u32[]{:S(2)}) collective-permute-start(f16[72,1024]{1,0:T(8,128)(2,1)S(1)} %get-tuple-element.63), channel_id=1, source_target_pairs={{0,6},{1,25},{2,0},{3,27},{4,2},{5,29},{6,4},{7,31},{8,14},{9,1},{... | collective-permute-start | bytes 442376 | tf_op jit(solution)/shard_map/ppermute | solution.py:41
  101.7 1.7 %collective-permute-done.17 = f16[136,1024]{1,0:T(8,128)(2,1)S(1)} collective-permute-done((f16[136,1024]{1,0:T(8,128)(2,1)S(1)}, f16[136,1024]{1,0:T(8,128)(2,1)S(1)}, u32[]{:S(2)}, u32[]{:S(2)}) %collective-permute-start.17) | collective-permute-done | bytes 278560 | tf_op jit(solution)/shard_map/ppermute | solution.py:41
  103.5 3.5 %collective-permute-start.18 = (f32[136,1024]{1,0:T(8,128)S(1)}, f32[136,1024]{1,0:T(8,128)S(1)}, u32[]{:S(2)}, u32[]{:S(2)}) collective-permute-start(f32[136,1024]{1,0:T(8,128)S(1)} %convert_add_fusion), channel_id=1, source_target_pairs={{0,1},{1,0},{2,3},{3,2},{4,5},{5,4},{6,7},{7,6},{8,9},{9,8},{10,11... | collective-permute-start | bytes 1671176 | tf_op jit(solution)/shard_map/ppermute | solution.py:41
  (74 shorter events, 16.1 us)
Async XLA Ops:
  0.6 1.0 copy-start.5
  1.7 5.6 %copy-start.4 = (f32[512,1024]{1,0:T(8,128)S(1)}, f32[512,1024]{1,0:T(8,128)}, u32[]{:S(2)}) copy-start(f32[512,1024]{1,0:T(8,128)} %regions.3) | copy-start | bytes 6291460
  1.7 5.7 %copy-start.6 = (s32[512]{0:T(512)S(1)}, s32[512]{0:T(512)}, u32[]{:S(2)}) copy-start(s32[512]{0:T(512)} %param.5) | copy-start | bytes 6148
  1.7 10.4 %collective-permute-start.3 = (bf16[128,1024]{1,0:T(8,128)(2,1)S(1)}, bf16[128,1024]{1,0:T(8,128)(2,1)S(1)}, u32[]{:S(2)}, u32[]{:S(2)}) collective-permute-start(bf16[128,1024]{1,0:T(8,128)(2,1)S(1)} %shard_map.60.text), channel_id=1, source_target_pairs={{0,224},{1,33},{2,226},{3,35},{4,228},{5,37},{6,230},{7,39},{8,232... | collective-permute-start | bytes 786440 | tf_op jit(solution)/shard_map/ppermute | solution.py:41
  4.3 12.5 %collective-permute-start.4 = (bf16[128,1024]{1,0:T(8,128)(2,1)S(1)}, bf16[128,1024]{1,0:T(8,128)(2,1)S(1)}, u32[]{:S(2)}, u32[]{:S(2)}) collective-permute-start(bf16[128,1024]{1,0:T(8,128)(2,1)S(1)} %shard_map.60.text), channel_id=1, source_target_pairs={{0,192},{1,65},{2,194},{3,67},{4,196},{5,69},{6,198},{7,71},{8,200... | collective-permute-start | bytes 786440 | tf_op jit(solution)/shard_map/ppermute | solution.py:41
  8.0 9.4 %collective-permute-start.1 = (bf16[144,1024]{1,0:T(8,128)(2,1)S(1)}, bf16[144,1024]{1,0:T(8,128)(2,1)S(1)}, u32[]{:S(2)}, u32[]{:S(2)}) collective-permute-start(bf16[144,1024]{1,0:T(8,128)(2,1)S(1)} %shard_map.58.part), channel_id=1, source_target_pairs={{0,16},{1,17},{2,18},{3,19},{4,20},{5,21},{6,22},{7,23},{8,24},{9,... | collective-permute-start | bytes 884744 | tf_op jit(solution)/shard_map/ppermute | solution.py:41
  11.7 18.6 %collective-permute-start = (bf16[528,1024]{1,0:T(8,128)(2,1)S(1)}, bf16[528,1024]{1,0:T(8,128)(2,1)S(1)}, u32[]{:S(2)}, u32[]{:S(2)}) collective-permute-start(bf16[528,1024]{1,0:T(8,128)(2,1)S(1)} %shard_map.59.own), channel_id=1, source_target_pairs={{0,24},{1,9},{2,26},{3,11},{4,28},{5,13},{6,30},{7,15},{8,0},{9,17... | collective-permute-start | bytes 3244040 | tf_op jit(solution)/shard_map/ppermute | solution.py:41
  17.4 8.9 %collective-permute-start.5 = (bf16[192,1024]{1,0:T(8,128)(2,1)S(1)}, bf16[192,1024]{1,0:T(8,128)(2,1)S(1)}, u32[]{:S(2)}, u32[]{:S(2)}) collective-permute-start(bf16[192,1024]{1,0:T(8,128)(2,1)S(1)} %shard_map.61), channel_id=1, source_target_pairs={{0,192},{1,65},{2,194},{3,67},{4,196},{5,69},{6,198},{7,71},{8,200... | collective-permute-start | bytes 1179656 | tf_op jit(solution)/shard_map/ppermute | solution.py:41
  17.5 5.6 %collective-permute-start.2 = (bf16[128,1024]{1,0:T(8,128)(2,1)S(1)}, bf16[128,1024]{1,0:T(8,128)(2,1)S(1)}, u32[]{:S(2)}, u32[]{:S(2)}) collective-permute-start(bf16[128,1024]{1,0:T(8,128)(2,1)S(1)} %slice.69), channel_id=1, source_target_pairs={{0,2},{1,3},{2,0},{3,1},{4,6},{5,7},{6,4},{7,5},{8,10},{9,11},{10,... | collective-permute-start | bytes 786440 | tf_op jit(solution)/shard_map/ppermute | solution.py:41
  30.4 4.3 %collective-permute-start.6 = (bf16[720,1024]{1,0:T(8,128)(2,1)S(1)}, bf16[720,1024]{1,0:T(8,128)(2,1)S(1)}, u32[]{:S(2)}, u32[]{:S(2)}) collective-permute-start(bf16[720,1024]{1,0:T(8,128)(2,1)S(1)} %pad_maximum_fusion), channel_id=1, source_target_pairs={{0,1},{1,0},{2,3},{3,2},{4,5},{5,4},{6,7},{7,6},{8,9},{9,8},{10,11... | collective-permute-start | bytes 4423688 | tf_op jit(solution)/shard_map/ppermute | solution.py:41
  39.9 19.6 %copy-start = (f32[1024,1024]{1,0:T(8,128)}, f32[1024,1024]{1,0:T(8,128)S(1)}, u32[]{:S(2)}) copy-start(f32[1024,1024]{1,0:T(8,128)S(1)} %get-tuple-element.30.held.scores) | copy-start | bytes 12582916
  39.9 19.5 %copy-start.2 = (bf16[1024,1024]{1,0:T(8,128)(2,1)}, bf16[1024,1024]{1,0:T(8,128)(2,1)S(1)}, u32[]{:S(2)}) copy-start(bf16[1024,1024]{1,0:T(8,128)(2,1)S(1)} %get-tuple-element.34.captions) | copy-start | bytes 6291460
  39.9 1.3 %collective-permute-start.7 = (f32[8,1024]{1,0:T(8,128)S(1)}, f32[8,1024]{1,0:T(8,128)S(1)}, u32[]{:S(2)}, u32[]{:S(2)}) collective-permute-start(f32[8,1024]{1,0:T(8,128)S(1)} %get-tuple-element.33), channel_id=1, source_target_pairs={{0,1},{1,0},{2,3},{3,2},{4,5},{5,4},{6,7},{7,6},{8,9},{9,8},{10,11... | collective-permute-start | bytes 98312 | tf_op jit(solution)/shard_map/ppermute | solution.py:41
  41.8 3.9 %collective-permute-start.8 = (f32[8,1024]{1,0:T(8,128)S(1)}, f32[8,1024]{1,0:T(8,128)S(1)}, u32[]{:S(2)}, u32[]{:S(2)}) collective-permute-start(f32[8,1024]{1,0:T(8,128)S(1)} %shard_map.63.own), channel_id=1, source_target_pairs={{0,8},{1,33},{2,10},{3,35},{4,12},{5,37},{6,14},{7,39},{8,0},{9,41... | collective-permute-start | bytes 98312 | tf_op jit(solution)/shard_map/ppermute | solution.py:41
  45.7 3.8 %collective-permute-start.9 = (f32[8,1024]{1,0:T(8,128)S(1)}, f32[8,1024]{1,0:T(8,128)S(1)}, u32[]{:S(2)}, u32[]{:S(2)}) collective-permute-start(f32[8,1024]{1,0:T(8,128)S(1)} %shard_map.64.own), channel_id=1, source_target_pairs={{0,16},{1,65},{2,18},{3,67},{4,20},{5,69},{6,22},{7,71},{8,24},{9,... | collective-permute-start | bytes 98312 | tf_op jit(solution)/shard_map/ppermute | solution.py:41
  49.5 6.9 %collective-permute-start.10 = (f32[8,1024]{1,0:T(8,128)S(1)}, f32[8,1024]{1,0:T(8,128)S(1)}, u32[]{:S(2)}, u32[]{:S(2)}) collective-permute-start(f32[8,1024]{1,0:T(8,128)S(1)} %shard_map.65.own), channel_id=1, source_target_pairs={{0,2},{1,129},{2,0},{3,131},{4,6},{5,133},{6,4},{7,135},{8,10},{9,... | collective-permute-start | bytes 98312 | tf_op jit(solution)/shard_map/ppermute | solution.py:41
  56.4 3.0 %collective-permute-start.11 = (f32[8,1024]{1,0:T(8,128)S(1)}, f32[8,1024]{1,0:T(8,128)S(1)}, u32[]{:S(2)}, u32[]{:S(2)}) collective-permute-start(f32[8,1024]{1,0:T(8,128)S(1)} %shard_map.66.own), channel_id=1, source_target_pairs={{0,4},{1,33},{2,6},{3,35},{4,0},{5,37},{6,2},{7,39},{8,12},{9,41},... | collective-permute-start | bytes 98312 | tf_op jit(solution)/shard_map/ppermute | solution.py:41
  60.1 2.9 %collective-permute-start.12 = (f32[8,1024]{1,0:T(8,128)S(1)}, f32[8,1024]{1,0:T(8,128)S(1)}, u32[]{:S(2)}, u32[]{:S(2)}) collective-permute-start(f32[8,1024]{1,0:T(8,128)S(1)} %shard_map.67.mine), channel_id=1, source_target_pairs={{0,1},{1,0},{2,3},{3,2},{4,5},{5,4},{6,7},{7,6},{8,9},{9,8},{10,11... | collective-permute-start | bytes 98312 | tf_op jit(solution)/shard_map/ppermute | solution.py:41
  63.1 2.2 %copy-start.1 = (f32[1024,1024]{1,0:T(8,128)S(1)}, f32[1024,1024]{1,0:T(8,128)}, u32[]{:S(2)}) copy-start(f32[1024,1024]{1,0:T(8,128)} %copy-done) | copy-start | bytes 12582916
  65.2 3.4 %copy-start.3 = (bf16[1024,1024]{1,0:T(8,128)(2,1)S(1)}, bf16[1024,1024]{1,0:T(8,128)(2,1)}, u32[]{:S(2)}) copy-start(bf16[1024,1024]{1,0:T(8,128)(2,1)} %copy-done.2) | copy-start | bytes 6291460
  72.1 7.7 %collective-permute-start.13 = (f16[480,1024]{1,0:T(8,128)(2,1)S(1)}, f16[480,1024]{1,0:T(8,128)(2,1)S(1)}, u32[]{:S(2)}, u32[]{:S(2)}) collective-permute-start(f16[480,1024]{1,0:T(8,128)(2,1)S(1)} %convert_element_type.79), channel_id=1, source_target_pairs={{0,1},{1,0},{2,3},{3,2},{4,5},{5,4},{6,7},{7,6},{8,9},{9,8},{10,11... | collective-permute-start | bytes 2949128 | tf_op jit(solution)/shard_map/ppermute | solution.py:41
  72.5 12.1 %collective-permute-start.19 = (f16[264,1024]{1,0:T(8,128)(2,1)S(1)}, f16[264,1024]{1,0:T(8,128)(2,1)S(1)}, u32[]{:S(2)}, u32[]{:S(2)}) collective-permute-start(f16[264,1024]{1,0:T(8,128)(2,1)S(1)} %convert_element_type.77), channel_id=1, source_target_pairs={{0,16},{1,5},{2,18},{3,7},{4,20},{5,1},{6,22},{7,3},{8,24},{9,13},... | collective-permute-start | bytes 1622024 | tf_op jit(solution)/shard_map/ppermute | solution.py:41
  75.2 13.0 %collective-permute-start.20 = (f16[264,1024]{1,0:T(8,128)(2,1)S(1)}, f16[264,1024]{1,0:T(8,128)(2,1)S(1)}, u32[]{:S(2)}, u32[]{:S(2)}) collective-permute-start(f16[264,1024]{1,0:T(8,128)(2,1)S(1)} %convert_element_type.76), channel_id=1, source_target_pairs={{0,8},{1,3},{2,10},{3,5},{4,12},{5,7},{6,14},{7,1},{8,16},{9,11},{... | collective-permute-start | bytes 1622024 | tf_op jit(solution)/shard_map/ppermute | solution.py:41
  75.5 12.9 %collective-permute-start.21 = (f16[264,1024]{1,0:T(8,128)(2,1)S(1)}, f16[264,1024]{1,0:T(8,128)(2,1)S(1)}, u32[]{:S(2)}, u32[]{:S(2)}) collective-permute-start(f16[264,1024]{1,0:T(8,128)(2,1)S(1)} %convert_element_type.78), channel_id=1, source_target_pairs={{0,24},{1,7},{2,26},{3,1},{4,28},{5,3},{6,30},{7,5},{8,0},{9,15},{... | collective-permute-start | bytes 1622024 | tf_op jit(solution)/shard_map/ppermute | solution.py:41
  80.0 13.4 %collective-permute-start.15 = (f16[136,1024]{1,0:T(8,128)(2,1)S(1)}, f16[136,1024]{1,0:T(8,128)(2,1)S(1)}, u32[]{:S(2)}, u32[]{:S(2)}) collective-permute-start(f16[136,1024]{1,0:T(8,128)(2,1)S(1)} %get-tuple-element.58), channel_id=1, source_target_pairs={{0,32},{1,225},{2,34},{3,227},{4,36},{5,229},{6,38},{7,231},{8,40}... | collective-permute-start | bytes 835592 | tf_op jit(solution)/shard_map/ppermute | solution.py:41
  84.5 8.8 %collective-permute-start.16 = (f16[72,1024]{1,0:T(8,128)(2,1)S(1)}, f16[72,1024]{1,0:T(8,128)(2,1)S(1)}, u32[]{:S(2)}, u32[]{:S(2)}) collective-permute-start(f16[72,1024]{1,0:T(8,128)(2,1)S(1)} %add_convert_fusion.2), channel_id=1, source_target_pairs={{0,64},{1,193},{2,66},{3,195},{4,68},{5,197},{6,70},{7,199},{8,72}... | collective-permute-start | bytes 442376 | tf_op jit(solution)/shard_map/ppermute | solution.py:41
  88.8 12.9 %collective-permute-start.14 = (f16[136,1024]{1,0:T(8,128)(2,1)S(1)}, f16[136,1024]{1,0:T(8,128)(2,1)S(1)}, u32[]{:S(2)}, u32[]{:S(2)}) collective-permute-start(f16[136,1024]{1,0:T(8,128)(2,1)S(1)} %get-tuple-element.57), channel_id=1, source_target_pairs={{0,32},{1,225},{2,34},{3,227},{4,36},{5,229},{6,38},{7,231},{8,40}... | collective-permute-start | bytes 835592 | tf_op jit(solution)/shard_map/ppermute | solution.py:41
  93.6 9.8 %collective-permute-start.17 = (f16[136,1024]{1,0:T(8,128)(2,1)S(1)}, f16[136,1024]{1,0:T(8,128)(2,1)S(1)}, u32[]{:S(2)}, u32[]{:S(2)}) collective-permute-start(f16[136,1024]{1,0:T(8,128)(2,1)S(1)} %fusion.2), channel_id=1, source_target_pairs={{0,64},{1,193},{2,66},{3,195},{4,68},{5,197},{6,70},{7,199},{8,72}... | collective-permute-start | bytes 835592 | tf_op jit(solution)/shard_map/ppermute | solution.py:41
  96.0 11.1 %collective-permute-start.22 = (f16[72,1024]{1,0:T(8,128)(2,1)S(1)}, f16[72,1024]{1,0:T(8,128)(2,1)S(1)}, u32[]{:S(2)}, u32[]{:S(2)}) collective-permute-start(f16[72,1024]{1,0:T(8,128)(2,1)S(1)} %get-tuple-element.61), channel_id=1, source_target_pairs={{0,4},{1,17},{2,6},{3,19},{4,0},{5,21},{6,2},{7,23},{8,12},{9,25},... | collective-permute-start | bytes 442376 | tf_op jit(solution)/shard_map/ppermute | solution.py:41
  99.0 8.1 %collective-permute-start.23 = (f16[72,1024]{1,0:T(8,128)(2,1)S(1)}, f16[72,1024]{1,0:T(8,128)(2,1)S(1)}, u32[]{:S(2)}, u32[]{:S(2)}) collective-permute-start(f16[72,1024]{1,0:T(8,128)(2,1)S(1)} %get-tuple-element.62), channel_id=1, source_target_pairs={{0,2},{1,9},{2,4},{3,11},{4,6},{5,13},{6,0},{7,15},{8,10},{9,17},{... | collective-permute-start | bytes 442376 | tf_op jit(solution)/shard_map/ppermute | solution.py:41
  99.4 7.7 %collective-permute-start.24 = (f16[72,1024]{1,0:T(8,128)(2,1)S(1)}, f16[72,1024]{1,0:T(8,128)(2,1)S(1)}, u32[]{:S(2)}, u32[]{:S(2)}) collective-permute-start(f16[72,1024]{1,0:T(8,128)(2,1)S(1)} %get-tuple-element.63), channel_id=1, source_target_pairs={{0,6},{1,25},{2,0},{3,27},{4,2},{5,29},{6,4},{7,31},{8,14},{9,1},{... | collective-permute-start | bytes 442376 | tf_op jit(solution)/shard_map/ppermute | solution.py:41
  103.5 5.1 %collective-permute-start.18 = (f32[136,1024]{1,0:T(8,128)S(1)}, f32[136,1024]{1,0:T(8,128)S(1)}, u32[]{:S(2)}, u32[]{:S(2)}) collective-permute-start(f32[136,1024]{1,0:T(8,128)S(1)} %convert_add_fusion), channel_id=1, source_target_pairs={{0,1},{1,0},{2,3},{3,2},{4,5},{5,4},{6,7},{7,6},{8,9},{9,8},{10,11... | collective-permute-start | bytes 1671176 | tf_op jit(solution)/shard_map/ppermute | solution.py:41

commit v5 on v4

--- a/solution.py
+++ b/solution.py
@@ -275,11 +275,21 @@
     out[6:8, :] = jnp.zeros((2, TILE), F32)
 
 
+def first_kernel(place, own, came, held, rows, captions, out):
+    lines = lax.broadcasted_iota(jnp.int32, (8, TILE), 0)
+    empty = jnp.where(lines < 2, far_below, 0.0)
+    top, sums, total, peak = merged(own[...], jnp.where(place[3] == 0, came[...], empty))
+    out[0:2, :] = top
+    out[2:4, :] = sums
+    out[4:5, :] = total
+    out[5:6, :] = peak
+    out[6:8, :] = jnp.zeros((2, TILE), F32)
+
+
 def last_kernel(place, own, came, held, rows, captions, out):
     first = place[3] == 0
     lines = lax.broadcasted_iota(jnp.int32, (8, TILE), 0)
-    empty = jnp.where(lines < 2, far_below, 0.0)
-    top, sums, total, peak = merged(own[...], jnp.where(first, came[...], empty))
+    top, sums, total, peak = merged(own[...], came[...])
     lse = top + jnp.log(jnp.where(jnp.logical_or(first, lines[0:2, :] == 0), sums, 1.0))
     both = 0.5 * jnp.sum(lse[0:1, :]) + jnp.where(first, 0.5 * jnp.sum(lse[1:2, :]), 0.0)
     out[0:1, :] = lse[0:1, :]
@@ -374,6 +384,10 @@
         ref[256:264, :] = code
 
 
+def pass_kernel(lse, out):
+    out[...] = lse[...]
+
+
 def shards(regions, captions, positive):
     z = lax.axis_index("z")
     y = lax.axis_index("y")
@@ -414,15 +428,19 @@
     def partner(bit):
         def target(z, y, x, c):
             if c == 1:
-                return (z ^ (1 << bit % 3), y, x, c)
-            return (z, y ^ (1 << bit), x, c) if bit < 2 else (z, y, x ^ (1 << (bit - 2)), c)
+                return (z ^ max(bit, 1) if bit < 3 else NZ - 1 - z, y, x, c)
+            if bit % 2 == 0:
+                return (z, y ^ 1 if bit == 0 else NY - 1 - y, x, c)
+            return (z, y, x ^ 1 if bit == 1 else NX - 1 - x, c)
 
         return target
 
-    for bit in range(3):
+    (stats,) = call(first_kernel, [small], place, stats, moved(stats, partner(0)), *tile)
+    for bit in (1, 2):
         (stats,) = call(merge_kernel, [small], stats, moved(stats, partner(bit)), *tile)
-    (lse,) = call(last_kernel, [small], place, stats, moved(stats, partner(3)), *tile)
+    (lse,) = call(last_kernel, [small], place, stats, moved(stats, partner(3)), stats, stats, stats)
     came = swapped(lse)
+    (lse,) = call(pass_kernel, [small], lse, us=60.0)
 
     weights, give, kept_half = call(
         weight_kernel,

time: 112 us -> 111 us (level)
  local copies, waits for them, and re-layouts: 3.5 us -> 1.88 us
    unnamed x14 -> x18, local copies, waits for them, and re-layouts: 3.24 us -> 1.07 us
    pallas_call x13 -> x14, Pallas kernels: 16.5 us -> 17 us  [call(): pl.pallas_call(kernel, in_specs=specs, out_specs=[pl.BlockSpec(memory_spa...]
  transfers between devices with their start and end apart: 25 -> 25, of which waited for: 15 -> 15; matrix products, arithmetic and copies ran while one was open for 2% -> 3% of each run, Pallas kernels for 3% -> 3%
where the time goes in v5:
time: 111 us
  starting transfers between devices  48.6 us (44%)
  waiting for transfers between devices  35.6 us (32%)
  Pallas kernels  17 us (15%)
  other arithmetic  4.67 us (4%)
  between operations  2.77 us (2%)
  local copies, waits for them, and re-layouts  1.88 us (2%)
    ppermute x25, starting transfers between devices, moved(): return lax.ppermute(value, AXES, pairs)  48.6 us
    ppermute x25, waiting for transfers between devices, moved(): return lax.ppermute(value, AXES, pairs)  35.6 us
    pallas_call x14, Pallas kernels, call(): pl.pallas_call(kernel, in_specs=specs, out_specs=[pl.BlockSpec(memory_spa...  17 us
  transfers between devices with their start and end apart: 25, of which 15 were waited for; matrix products, arithmetic and copies ran while one was open for 3% of the time, Pallas kernels for 3%

profile of v5, /device:TPU:1, one launch (start us, length us, event | category | flops | bytes accessed | tf_op | source)
XLA Modules:
  0.0 110.5 jit_solution(16811965987376138131)
XLA Ops:
  1.7 2.5 %collective-permute-start.3 = (bf16[128,1024]{1,0:T(8,128)(2,1)S(1)}, bf16[128,1024]{1,0:T(8,128)(2,1)S(1)}, u32[]{:S(2)}, u32[]{:S(2)}) collective-permute-start(bf16[128,1024]{1,0:T(8,128)(2,1)S(1)} %shard_map.60.text), channel_id=1, source_target_pairs={{0,224},{1,33},{2,226},{3,35},{4,228},{5,37},{6,230},{7,39},{8,232... | collective-permute-start | bytes 786440 | tf_op jit(solution)/shard_map/ppermute | solution.py:41
  4.3 3.0 %collective-permute-start.4 = (bf16[128,1024]{1,0:T(8,128)(2,1)S(1)}, bf16[128,1024]{1,0:T(8,128)(2,1)S(1)}, u32[]{:S(2)}, u32[]{:S(2)}) collective-permute-start(bf16[128,1024]{1,0:T(8,128)(2,1)S(1)} %shard_map.60.text), channel_id=1, source_target_pairs={{0,192},{1,65},{2,194},{3,67},{4,196},{5,69},{6,198},{7,71},{8,200... | collective-permute-start | bytes 786440 | tf_op jit(solution)/shard_map/ppermute | solution.py:41
  8.0 3.0 %collective-permute-start.1 = (bf16[144,1024]{1,0:T(8,128)(2,1)S(1)}, bf16[144,1024]{1,0:T(8,128)(2,1)S(1)}, u32[]{:S(2)}, u32[]{:S(2)}) collective-permute-start(bf16[144,1024]{1,0:T(8,128)(2,1)S(1)} %shard_map.58.part), channel_id=1, source_target_pairs={{0,16},{1,17},{2,18},{3,19},{4,20},{5,21},{6,22},{7,23},{8,24},{9,... | collective-permute-start | bytes 884744 | tf_op jit(solution)/shard_map/ppermute | solution.py:41
  12.1 4.6 %collective-permute-done.4.two = bf16[128,1024]{1,0:T(8,128)(2,1)S(1)} collective-permute-done((bf16[128,1024]{1,0:T(8,128)(2,1)S(1)}, bf16[128,1024]{1,0:T(8,128)(2,1)S(1)}, u32[]{:S(2)}, u32[]{:S(2)}) %collective-permute-start.4) | collective-permute-done | bytes 262176 | tf_op jit(solution)/shard_map/ppermute | solution.py:41
  17.5 1.3 %collective-permute-start.2 = (bf16[128,1024]{1,0:T(8,128)(2,1)S(1)}, bf16[128,1024]{1,0:T(8,128)(2,1)S(1)}, u32[]{:S(2)}, u32[]{:S(2)}) collective-permute-start(bf16[128,1024]{1,0:T(8,128)(2,1)S(1)} %slice.69), channel_id=1, source_target_pairs={{0,2},{1,3},{2,0},{3,1},{4,6},{5,7},{6,4},{7,5},{8,10},{9,11},{10,... | collective-permute-start | bytes 786440 | tf_op jit(solution)/shard_map/ppermute | solution.py:41
  18.8 4.3 %collective-permute-done.2.other = bf16[128,1024]{1,0:T(8,128)(2,1)S(1)} collective-permute-done((bf16[128,1024]{1,0:T(8,128)(2,1)S(1)}, bf16[128,1024]{1,0:T(8,128)(2,1)S(1)}, u32[]{:S(2)}, u32[]{:S(2)}) %collective-permute-start.2) | collective-permute-done | bytes 262176 | tf_op jit(solution)/shard_map/ppermute | solution.py:41
  23.1 3.2 %collective-permute-done.5.skip = bf16[192,1024]{1,0:T(8,128)(2,1)S(1)} collective-permute-done((bf16[192,1024]{1,0:T(8,128)(2,1)S(1)}, bf16[192,1024]{1,0:T(8,128)(2,1)S(1)}, u32[]{:S(2)}, u32[]{:S(2)}) %collective-permute-start.5) | collective-permute-done | bytes 393248 | tf_op jit(solution)/shard_map/ppermute | solution.py:41
  26.3 4.0 %collective-permute-done.full = bf16[528,1024]{1,0:T(8,128)(2,1)S(1)} collective-permute-done((bf16[528,1024]{1,0:T(8,128)(2,1)S(1)}, bf16[528,1024]{1,0:T(8,128)(2,1)S(1)}, u32[]{:S(2)}, u32[]{:S(2)}) %collective-permute-start) | collective-permute-done | bytes 1081376 | tf_op jit(solution)/shard_map/ppermute | solution.py:41
  30.4 1.4 %collective-permute-start.6 = (bf16[720,1024]{1,0:T(8,128)(2,1)S(1)}, bf16[720,1024]{1,0:T(8,128)(2,1)S(1)}, u32[]{:S(2)}, u32[]{:S(2)}) collective-permute-start(bf16[720,1024]{1,0:T(8,128)(2,1)S(1)} %pad_maximum_fusion), channel_id=1, source_target_pairs={{0,1},{1,0},{2,3},{3,2},{4,5},{5,4},{6,7},{7,6},{8,9},{9,8},{10,11... | collective-permute-start | bytes 4423688 | tf_op jit(solution)/shard_map/ppermute | solution.py:41
  31.9 2.9 %collective-permute-done.6.far = bf16[720,1024]{1,0:T(8,128)(2,1)S(1)} collective-permute-done((bf16[720,1024]{1,0:T(8,128)(2,1)S(1)}, bf16[720,1024]{1,0:T(8,128)(2,1)S(1)}, u32[]{:S(2)}, u32[]{:S(2)}) %collective-permute-start.6) | collective-permute-done | bytes 1474592 | tf_op jit(solution)/shard_map/ppermute | solution.py:41
  34.8 5.1 %shard_map.62 = (f32[1024,1024]{1,0:T(8,128)S(1)}, bf16[1024,1024]{1,0:T(8,128)(2,1)S(1)}, bf16[1024,1024]{1,0:T(8,128)(2,1)S(1)}, s32[8,1024]{1,0:T(8,128)S(1)}...) custom-call(s32[4]{0:T(128)S(1)} %pad_add_fusion.place, bf16[528,1024]{1,0:T(8,128)(2,1)S(1)} %shard_map.59.own, ...), custom_call_target="tpu_custom_call" | custom-call | flops 8800000000 | bytes 24000000 | tf_op jit(solution)/shard_map/pallas_call | solution.py:62
  41.8 2.3 %collective-permute-start.8 = (f32[8,1024]{1,0:T(8,128)S(1)}, f32[8,1024]{1,0:T(8,128)S(1)}, u32[]{:S(2)}, u32[]{:S(2)}) collective-permute-start(f32[8,1024]{1,0:T(8,128)S(1)} %shard_map.63.own), channel_id=1, source_target_pairs={{0,8},{1,33},{2,10},{3,35},{4,12},{5,37},{6,14},{7,39},{8,0},{9,41... | collective-permute-start | bytes 98312 | tf_op jit(solution)/shard_map/ppermute | solution.py:41
  44.1 1.6 %collective-permute-done.8.came = f32[8,1024]{1,0:T(8,128)S(1)} collective-permute-done((f32[8,1024]{1,0:T(8,128)S(1)}, f32[8,1024]{1,0:T(8,128)S(1)}, u32[]{:S(2)}, u32[]{:S(2)}) %collective-permute-start.8) | collective-permute-done | bytes 32800 | tf_op jit(solution)/shard_map/ppermute | solution.py:41
  46.3 1.3 %collective-permute-start.9 = (f32[8,1024]{1,0:T(8,128)S(1)}, f32[8,1024]{1,0:T(8,128)S(1)}, u32[]{:S(2)}, u32[]{:S(2)}) collective-permute-start(f32[8,1024]{1,0:T(8,128)S(1)} %shard_map.64.own), channel_id=1, source_target_pairs={{0,2},{1,33},{2,0},{3,35},{4,6},{5,37},{6,4},{7,39},{8,10},{9,41},... | collective-permute-start | bytes 98312 | tf_op jit(solution)/shard_map/ppermute | solution.py:41
  47.5 1.6 %collective-permute-done.9.came = f32[8,1024]{1,0:T(8,128)S(1)} collective-permute-done((f32[8,1024]{1,0:T(8,128)S(1)}, f32[8,1024]{1,0:T(8,128)S(1)}, u32[]{:S(2)}, u32[]{:S(2)}) %collective-permute-start.9) | collective-permute-done | bytes 32800 | tf_op jit(solution)/shard_map/ppermute | solution.py:41
  49.1 2.1 %collective-permute-start.10 = (f32[8,1024]{1,0:T(8,128)S(1)}, f32[8,1024]{1,0:T(8,128)S(1)}, u32[]{:S(2)}, u32[]{:S(2)}) collective-permute-start(f32[8,1024]{1,0:T(8,128)S(1)} %shard_map.65.own), channel_id=1, source_target_pairs={{0,24},{1,65},{2,26},{3,67},{4,28},{5,69},{6,30},{7,71},{8,16},{9,... | collective-permute-start | bytes 98312 | tf_op jit(solution)/shard_map/ppermute | solution.py:41
  51.2 1.7 %collective-permute-done.10.came = f32[8,1024]{1,0:T(8,128)S(1)} collective-permute-done((f32[8,1024]{1,0:T(8,128)S(1)}, f32[8,1024]{1,0:T(8,128)S(1)}, u32[]{:S(2)}, u32[]{:S(2)}) %collective-permute-start.10) | collective-permute-done | bytes 32800 | tf_op jit(solution)/shard_map/ppermute | solution.py:41
  52.9 3.8 %collective-permute-start.11 = (f32[8,1024]{1,0:T(8,128)S(1)}, f32[8,1024]{1,0:T(8,128)S(1)}, u32[]{:S(2)}, u32[]{:S(2)}) collective-permute-start(f32[8,1024]{1,0:T(8,128)S(1)} %shard_map.66.own.held.rows.captions), channel_id=1, source_target_pairs={{0,6},{1,225},{2,4},{3,227},{4,2},{5,229},{6,0},{7,231},{8,14},{9,... | collective-permute-start | bytes 98312 | tf_op jit(solution)/shard_map/ppermute | solution.py:41
  58.8 3.4 %collective-permute-start.12 = (f32[8,1024]{1,0:T(8,128)S(1)}, f32[8,1024]{1,0:T(8,128)S(1)}, u32[]{:S(2)}, u32[]{:S(2)}) collective-permute-start(f32[8,1024]{1,0:T(8,128)S(1)} %shard_map.67.lse), channel_id=1, source_target_pairs={{0,1},{1,0},{2,3},{3,2},{4,5},{5,4},{6,7},{7,6},{8,9},{9,8},{10,11... | collective-permute-start | bytes 98312 | tf_op jit(solution)/shard_map/ppermute | solution.py:41
  63.0 3.4 %shard_map.69 = (bf16[1024,1024]{1,0:T(8,128)(2,1)S(1)}, f32[480,1024]{1,0:T(8,128)S(1)}, f32[72,1024]{1,0:T(8,128)S(1)}) custom-call(s32[4]{0:T(128)S(1)} %pad_add_fusion.place, f32[1024,1024]{1,0:T(8,128)S(1)} %copy-done.1, bf16[1024,1024]{1,0:T(8,128)(2,1)S(1)} %get-tuple-element.31.rows.regions, f32[8,1024]{1,0:T(8,128)S(1)} %shard_map.68.mine, ...), custom_call_target="tpu_custom_call" | custom-call | flops 44000002048 | bytes 120000000 | tf_op jit(solution)/shard_map/pallas_call | solution.py:62
  66.5 2.9 %shard_map.70 = (f32[264,1024]{1,0:T(8,128)S(1)}, f32[264,1024]{1,0:T(8,128)S(1)}, f32[264,1024]{1,0:T(8,128)S(1)}, f32[264,1024]{1,0:T(8,128)S(1)}) custom-call(s32[4]{0:T(128)S(1)} %pad_add_fusion.place, bf16[1024,1024]{1,0:T(8,128)(2,1)S(1)} %get-tuple-element.40.weights, bf16[1024,1024]{1,0:T(8,128)(2,1)S(1)} %copy-done.3, ...), custom_call_target="tpu_custom_call" | custom-call | flops 32999999488 | bytes 90000000 | tf_op jit(solution)/shard_map/pallas_call | solution.py:62
  69.8 1.3 %collective-permute-start.13 = (f16[480,1024]{1,0:T(8,128)(2,1)S(1)}, f16[480,1024]{1,0:T(8,128)(2,1)S(1)}, u32[]{:S(2)}, u32[]{:S(2)}) collective-permute-start(f16[480,1024]{1,0:T(8,128)(2,1)S(1)} %convert_element_type.79), channel_id=1, source_target_pairs={{0,1},{1,0},{2,3},{3,2},{4,5},{5,4},{6,7},{7,6},{8,9},{9,8},{10,11... | collective-permute-start | bytes 2949128 | tf_op jit(solution)/shard_map/ppermute | solution.py:41
  71.2 1.5 %collective-permute-start.19 = (f16[264,1024]{1,0:T(8,128)(2,1)S(1)}, f16[264,1024]{1,0:T(8,128)(2,1)S(1)}, u32[]{:S(2)}, u32[]{:S(2)}) collective-permute-start(f16[264,1024]{1,0:T(8,128)(2,1)S(1)} %convert_element_type.77), channel_id=1, source_target_pairs={{0,16},{1,5},{2,18},{3,7},{4,20},{5,1},{6,22},{7,3},{8,24},{9,13},... | collective-permute-start | bytes 1622024 | tf_op jit(solution)/shard_map/ppermute | solution.py:41
  72.7 1.5 %collective-permute-start.20 = (f16[264,1024]{1,0:T(8,128)(2,1)S(1)}, f16[264,1024]{1,0:T(8,128)(2,1)S(1)}, u32[]{:S(2)}, u32[]{:S(2)}) collective-permute-start(f16[264,1024]{1,0:T(8,128)(2,1)S(1)} %convert_element_type.76), channel_id=1, source_target_pairs={{0,8},{1,3},{2,10},{3,5},{4,12},{5,7},{6,14},{7,1},{8,16},{9,11},{... | collective-permute-start | bytes 1622024 | tf_op jit(solution)/shard_map/ppermute | solution.py:41
  75.4 1.8 %shard_map.71 = (f32[136,1024]{1,0:T(8,128)S(1)}, f32[136,1024]{1,0:T(8,128)S(1)}, f32[136,1024]{1,0:T(8,128)S(1)}, f32[136,1024]{1,0:T(8,128)S(1)}) custom-call(s32[4]{0:T(128)S(1)} %pad_add_fusion.place, bf16[1024,1024]{1,0:T(8,128)(2,1)S(1)} %get-tuple-element.40.weights, bf16[1024,1024]{1,0:T(8,128)(2,1)S(1)} %get-tuple-element.31.rows.regions, ...), custom_call_target="tpu_custom_call" | custom-call | flops 22000001024 | bytes 60000000 | tf_op jit(solution)/shard_map/pallas_call | solution.py:62
  77.4 4.5 %collective-permute-start.15 = (f16[136,1024]{1,0:T(8,128)(2,1)S(1)}, f16[136,1024]{1,0:T(8,128)(2,1)S(1)}, u32[]{:S(2)}, u32[]{:S(2)}) collective-permute-start(f16[136,1024]{1,0:T(8,128)(2,1)S(1)} %get-tuple-element.58), channel_id=1, source_target_pairs={{0,32},{1,225},{2,34},{3,227},{4,36},{5,229},{6,38},{7,231},{8,40}... | collective-permute-start | bytes 835592 | tf_op jit(solution)/shard_map/ppermute | solution.py:41
  82.0 4.9 %collective-permute-done.20 = f16[264,1024]{1,0:T(8,128)(2,1)S(1)} collective-permute-done((f16[264,1024]{1,0:T(8,128)(2,1)S(1)}, f16[264,1024]{1,0:T(8,128)(2,1)S(1)}, u32[]{:S(2)}, u32[]{:S(2)}) %collective-permute-start.20) | collective-permute-done | bytes 540704 | tf_op jit(solution)/shard_map/ppermute | solution.py:41
  87.5 4.5 %collective-permute-start.14 = (f16[136,1024]{1,0:T(8,128)(2,1)S(1)}, f16[136,1024]{1,0:T(8,128)(2,1)S(1)}, u32[]{:S(2)}, u32[]{:S(2)}) collective-permute-start(f16[136,1024]{1,0:T(8,128)(2,1)S(1)} %get-tuple-element.57), channel_id=1, source_target_pairs={{0,32},{1,225},{2,34},{3,227},{4,36},{5,229},{6,38},{7,231},{8,40}... | collective-permute-start | bytes 835592 | tf_op jit(solution)/shard_map/ppermute | solution.py:41
  93.5 1.8 %collective-permute-start.22 = (f16[72,1024]{1,0:T(8,128)(2,1)S(1)}, f16[72,1024]{1,0:T(8,128)(2,1)S(1)}, u32[]{:S(2)}, u32[]{:S(2)}) collective-permute-start(f16[72,1024]{1,0:T(8,128)(2,1)S(1)} %get-tuple-element.61), channel_id=1, source_target_pairs={{0,4},{1,17},{2,6},{3,19},{4,0},{5,21},{6,2},{7,23},{8,12},{9,25},... | collective-permute-start | bytes 442376 | tf_op jit(solution)/shard_map/ppermute | solution.py:41
  95.2 1.6 %collective-permute-start.23 = (f16[72,1024]{1,0:T(8,128)(2,1)S(1)}, f16[72,1024]{1,0:T(8,128)(2,1)S(1)}, u32[]{:S(2)}, u32[]{:S(2)}) collective-permute-start(f16[72,1024]{1,0:T(8,128)(2,1)S(1)} %get-tuple-element.62), channel_id=1, source_target_pairs={{0,2},{1,9},{2,4},{3,11},{4,6},{5,13},{6,0},{7,15},{8,10},{9,17},{... | collective-permute-start | bytes 442376 | tf_op jit(solution)/shard_map/ppermute | solution.py:41
  97.9 4.1 %collective-permute-done.17 = f16[136,1024]{1,0:T(8,128)(2,1)S(1)} collective-permute-done((f16[136,1024]{1,0:T(8,128)(2,1)S(1)}, f16[136,1024]{1,0:T(8,128)(2,1)S(1)}, u32[]{:S(2)}, u32[]{:S(2)}) %collective-permute-start.17) | collective-permute-done | bytes 278560 | tf_op jit(solution)/shard_map/ppermute | solution.py:41
  102.2 3.5 %collective-permute-start.18 = (f32[136,1024]{1,0:T(8,128)S(1)}, f32[136,1024]{1,0:T(8,128)S(1)}, u32[]{:S(2)}, u32[]{:S(2)}) collective-permute-start(f32[136,1024]{1,0:T(8,128)S(1)} %convert_add_fusion), channel_id=1, source_target_pairs={{0,1},{1,0},{2,3},{3,2},{4,5},{5,4},{6,7},{7,6},{8,9},{9,8},{10,11... | collective-permute-start | bytes 1671176 | tf_op jit(solution)/shard_map/ppermute | solution.py:41
  (79 shorter events, 17.2 us)
Async XLA Ops:
  1.7 5.6 %copy-start.4 = (f32[512,1024]{1,0:T(8,128)S(1)}, f32[512,1024]{1,0:T(8,128)}, u32[]{:S(2)}) copy-start(f32[512,1024]{1,0:T(8,128)} %regions.3) | copy-start | bytes 6291460
  1.7 5.7 %copy-start.6 = (s32[512]{0:T(512)S(1)}, s32[512]{0:T(512)}, u32[]{:S(2)}) copy-start(s32[512]{0:T(512)} %param.5) | copy-start | bytes 6148
  1.7 10.4 %collective-permute-start.3 = (bf16[128,1024]{1,0:T(8,128)(2,1)S(1)}, bf16[128,1024]{1,0:T(8,128)(2,1)S(1)}, u32[]{:S(2)}, u32[]{:S(2)}) collective-permute-start(bf16[128,1024]{1,0:T(8,128)(2,1)S(1)} %shard_map.60.text), channel_id=1, source_target_pairs={{0,224},{1,33},{2,226},{3,35},{4,228},{5,37},{6,230},{7,39},{8,232... | collective-permute-start | bytes 786440 | tf_op jit(solution)/shard_map/ppermute | solution.py:41
  4.3 12.5 %collective-permute-start.4 = (bf16[128,1024]{1,0:T(8,128)(2,1)S(1)}, bf16[128,1024]{1,0:T(8,128)(2,1)S(1)}, u32[]{:S(2)}, u32[]{:S(2)}) collective-permute-start(bf16[128,1024]{1,0:T(8,128)(2,1)S(1)} %shard_map.60.text), channel_id=1, source_target_pairs={{0,192},{1,65},{2,194},{3,67},{4,196},{5,69},{6,198},{7,71},{8,200... | collective-permute-start | bytes 786440 | tf_op jit(solution)/shard_map/ppermute | solution.py:41
  8.0 9.4 %collective-permute-start.1 = (bf16[144,1024]{1,0:T(8,128)(2,1)S(1)}, bf16[144,1024]{1,0:T(8,128)(2,1)S(1)}, u32[]{:S(2)}, u32[]{:S(2)}) collective-permute-start(bf16[144,1024]{1,0:T(8,128)(2,1)S(1)} %shard_map.58.part), channel_id=1, source_target_pairs={{0,16},{1,17},{2,18},{3,19},{4,20},{5,21},{6,22},{7,23},{8,24},{9,... | collective-permute-start | bytes 884744 | tf_op jit(solution)/shard_map/ppermute | solution.py:41
  11.7 18.6 %collective-permute-start = (bf16[528,1024]{1,0:T(8,128)(2,1)S(1)}, bf16[528,1024]{1,0:T(8,128)(2,1)S(1)}, u32[]{:S(2)}, u32[]{:S(2)}) collective-permute-start(bf16[528,1024]{1,0:T(8,128)(2,1)S(1)} %shard_map.59.own), channel_id=1, source_target_pairs={{0,24},{1,9},{2,26},{3,11},{4,28},{5,13},{6,30},{7,15},{8,0},{9,17... | collective-permute-start | bytes 3244040 | tf_op jit(solution)/shard_map/ppermute | solution.py:41
  17.4 8.9 %collective-permute-start.5 = (bf16[192,1024]{1,0:T(8,128)(2,1)S(1)}, bf16[192,1024]{1,0:T(8,128)(2,1)S(1)}, u32[]{:S(2)}, u32[]{:S(2)}) collective-permute-start(bf16[192,1024]{1,0:T(8,128)(2,1)S(1)} %shard_map.61), channel_id=1, source_target_pairs={{0,192},{1,65},{2,194},{3,67},{4,196},{5,69},{6,198},{7,71},{8,200... | collective-permute-start | bytes 1179656 | tf_op jit(solution)/shard_map/ppermute | solution.py:41
  17.5 5.6 %collective-permute-start.2 = (bf16[128,1024]{1,0:T(8,128)(2,1)S(1)}, bf16[128,1024]{1,0:T(8,128)(2,1)S(1)}, u32[]{:S(2)}, u32[]{:S(2)}) collective-permute-start(bf16[128,1024]{1,0:T(8,128)(2,1)S(1)} %slice.69), channel_id=1, source_target_pairs={{0,2},{1,3},{2,0},{3,1},{4,6},{5,7},{6,4},{7,5},{8,10},{9,11},{10,... | collective-permute-start | bytes 786440 | tf_op jit(solution)/shard_map/ppermute | solution.py:41
  30.4 4.3 %collective-permute-start.6 = (bf16[720,1024]{1,0:T(8,128)(2,1)S(1)}, bf16[720,1024]{1,0:T(8,128)(2,1)S(1)}, u32[]{:S(2)}, u32[]{:S(2)}) collective-permute-start(bf16[720,1024]{1,0:T(8,128)(2,1)S(1)} %pad_maximum_fusion), channel_id=1, source_target_pairs={{0,1},{1,0},{2,3},{3,2},{4,5},{5,4},{6,7},{7,6},{8,9},{9,8},{10,11... | collective-permute-start | bytes 4423688 | tf_op jit(solution)/shard_map/ppermute | solution.py:41
  39.9 13.0 %copy-start = (f32[1024,1024]{1,0:T(8,128)}, f32[1024,1024]{1,0:T(8,128)S(1)}, u32[]{:S(2)}) copy-start(f32[1024,1024]{1,0:T(8,128)S(1)} %get-tuple-element.30.held.scores) | copy-start | bytes 12582916
  39.9 13.0 %copy-start.2 = (bf16[1024,1024]{1,0:T(8,128)(2,1)}, bf16[1024,1024]{1,0:T(8,128)(2,1)S(1)}, u32[]{:S(2)}) copy-start(bf16[1024,1024]{1,0:T(8,128)(2,1)S(1)} %get-tuple-element.34.captions) | copy-start | bytes 6291460
  39.9 1.3 %collective-permute-start.7 = (f32[8,1024]{1,0:T(8,128)S(1)}, f32[8,1024]{1,0:T(8,128)S(1)}, u32[]{:S(2)}, u32[]{:S(2)}) collective-permute-start(f32[8,1024]{1,0:T(8,128)S(1)} %get-tuple-element.33), channel_id=1, source_target_pairs={{0,1},{1,0},{2,3},{3,2},{4,5},{5,4},{6,7},{7,6},{8,9},{9,8},{10,11... | collective-permute-start | bytes 98312 | tf_op jit(solution)/shard_map/ppermute | solution.py:41
  41.8 3.9 %collective-permute-start.8 = (f32[8,1024]{1,0:T(8,128)S(1)}, f32[8,1024]{1,0:T(8,128)S(1)}, u32[]{:S(2)}, u32[]{:S(2)}) collective-permute-start(f32[8,1024]{1,0:T(8,128)S(1)} %shard_map.63.own), channel_id=1, source_target_pairs={{0,8},{1,33},{2,10},{3,35},{4,12},{5,37},{6,14},{7,39},{8,0},{9,41... | collective-permute-start | bytes 98312 | tf_op jit(solution)/shard_map/ppermute | solution.py:41
  46.3 2.9 %collective-permute-start.9 = (f32[8,1024]{1,0:T(8,128)S(1)}, f32[8,1024]{1,0:T(8,128)S(1)}, u32[]{:S(2)}, u32[]{:S(2)}) collective-permute-start(f32[8,1024]{1,0:T(8,128)S(1)} %shard_map.64.own), channel_id=1, source_target_pairs={{0,2},{1,33},{2,0},{3,35},{4,6},{5,37},{6,4},{7,39},{8,10},{9,41},... | collective-permute-start | bytes 98312 | tf_op jit(solution)/shard_map/ppermute | solution.py:41
  49.1 3.8 %collective-permute-start.10 = (f32[8,1024]{1,0:T(8,128)S(1)}, f32[8,1024]{1,0:T(8,128)S(1)}, u32[]{:S(2)}, u32[]{:S(2)}) collective-permute-start(f32[8,1024]{1,0:T(8,128)S(1)} %shard_map.65.own), channel_id=1, source_target_pairs={{0,24},{1,65},{2,26},{3,67},{4,28},{5,69},{6,30},{7,71},{8,16},{9,... | collective-permute-start | bytes 98312 | tf_op jit(solution)/shard_map/ppermute | solution.py:41
  52.9 5.2 %collective-permute-start.11 = (f32[8,1024]{1,0:T(8,128)S(1)}, f32[8,1024]{1,0:T(8,128)S(1)}, u32[]{:S(2)}, u32[]{:S(2)}) collective-permute-start(f32[8,1024]{1,0:T(8,128)S(1)} %shard_map.66.own.held.rows.captions), channel_id=1, source_target_pairs={{0,6},{1,225},{2,4},{3,227},{4,2},{5,229},{6,0},{7,231},{8,14},{9,... | collective-permute-start | bytes 98312 | tf_op jit(solution)/shard_map/ppermute | solution.py:41
  58.8 4.2 %copy-start.1 = (f32[1024,1024]{1,0:T(8,128)S(1)}, f32[1024,1024]{1,0:T(8,128)}, u32[]{:S(2)}) copy-start(f32[1024,1024]{1,0:T(8,128)} %copy-done) | copy-start | bytes 12582916
  58.8 4.2 %collective-permute-start.12 = (f32[8,1024]{1,0:T(8,128)S(1)}, f32[8,1024]{1,0:T(8,128)S(1)}, u32[]{:S(2)}, u32[]{:S(2)}) collective-permute-start(f32[8,1024]{1,0:T(8,128)S(1)} %shard_map.67.lse), channel_id=1, source_target_pairs={{0,1},{1,0},{2,3},{3,2},{4,5},{5,4},{6,7},{7,6},{8,9},{9,8},{10,11... | collective-permute-start | bytes 98312 | tf_op jit(solution)/shard_map/ppermute | solution.py:41
  63.0 3.5 %copy-start.3 = (bf16[1024,1024]{1,0:T(8,128)(2,1)S(1)}, bf16[1024,1024]{1,0:T(8,128)(2,1)}, u32[]{:S(2)}) copy-start(bf16[1024,1024]{1,0:T(8,128)(2,1)} %copy-done.2) | copy-start | bytes 6291460
  69.8 7.3 %collective-permute-start.13 = (f16[480,1024]{1,0:T(8,128)(2,1)S(1)}, f16[480,1024]{1,0:T(8,128)(2,1)S(1)}, u32[]{:S(2)}, u32[]{:S(2)}) collective-permute-start(f16[480,1024]{1,0:T(8,128)(2,1)S(1)} %convert_element_type.79), channel_id=1, source_target_pairs={{0,1},{1,0},{2,3},{3,2},{4,5},{5,4},{6,7},{7,6},{8,9},{9,8},{10,11... | collective-permute-start | bytes 2949128 | tf_op jit(solution)/shard_map/ppermute | solution.py:41
  71.2 10.9 %collective-permute-start.19 = (f16[264,1024]{1,0:T(8,128)(2,1)S(1)}, f16[264,1024]{1,0:T(8,128)(2,1)S(1)}, u32[]{:S(2)}, u32[]{:S(2)}) collective-permute-start(f16[264,1024]{1,0:T(8,128)(2,1)S(1)} %convert_element_type.77), channel_id=1, source_target_pairs={{0,16},{1,5},{2,18},{3,7},{4,20},{5,1},{6,22},{7,3},{8,24},{9,13},... | collective-permute-start | bytes 1622024 | tf_op jit(solution)/shard_map/ppermute | solution.py:41
  72.7 14.3 %collective-permute-start.20 = (f16[264,1024]{1,0:T(8,128)(2,1)S(1)}, f16[264,1024]{1,0:T(8,128)(2,1)S(1)}, u32[]{:S(2)}, u32[]{:S(2)}) collective-permute-start(f16[264,1024]{1,0:T(8,128)(2,1)S(1)} %convert_element_type.76), channel_id=1, source_target_pairs={{0,8},{1,3},{2,10},{3,5},{4,12},{5,7},{6,14},{7,1},{8,16},{9,11},{... | collective-permute-start | bytes 1622024 | tf_op jit(solution)/shard_map/ppermute | solution.py:41
  74.2 12.9 %collective-permute-start.21 = (f16[264,1024]{1,0:T(8,128)(2,1)S(1)}, f16[264,1024]{1,0:T(8,128)(2,1)S(1)}, u32[]{:S(2)}, u32[]{:S(2)}) collective-permute-start(f16[264,1024]{1,0:T(8,128)(2,1)S(1)} %convert_element_type.78), channel_id=1, source_target_pairs={{0,24},{1,7},{2,26},{3,1},{4,28},{5,3},{6,30},{7,5},{8,0},{9,15},{... | collective-permute-start | bytes 1622024 | tf_op jit(solution)/shard_map/ppermute | solution.py:41
  77.4 14.6 %collective-permute-start.15 = (f16[136,1024]{1,0:T(8,128)(2,1)S(1)}, f16[136,1024]{1,0:T(8,128)(2,1)S(1)}, u32[]{:S(2)}, u32[]{:S(2)}) collective-permute-start(f16[136,1024]{1,0:T(8,128)(2,1)S(1)} %get-tuple-element.58), channel_id=1, source_target_pairs={{0,32},{1,225},{2,34},{3,227},{4,36},{5,229},{6,38},{7,231},{8,40}... | collective-permute-start | bytes 835592 | tf_op jit(solution)/shard_map/ppermute | solution.py:41
  81.9 10.0 %collective-permute-start.16 = (f16[72,1024]{1,0:T(8,128)(2,1)S(1)}, f16[72,1024]{1,0:T(8,128)(2,1)S(1)}, u32[]{:S(2)}, u32[]{:S(2)}) collective-permute-start(f16[72,1024]{1,0:T(8,128)(2,1)S(1)} %add_convert_fusion.2), channel_id=1, source_target_pairs={{0,64},{1,193},{2,66},{3,195},{4,68},{5,197},{6,70},{7,199},{8,72}... | collective-permute-start | bytes 442376 | tf_op jit(solution)/shard_map/ppermute | solution.py:41
  87.1 5.0 %copy-start.7 = (f32[136]{0:T(256)S(1)}, f32[136]{0:T(256)}, u32[]{:S(2)}) copy-start(f32[136]{0:T(256)} %pad.10.clone) | copy-start | bytes 1636
  87.5 10.5 %collective-permute-start.14 = (f16[136,1024]{1,0:T(8,128)(2,1)S(1)}, f16[136,1024]{1,0:T(8,128)(2,1)S(1)}, u32[]{:S(2)}, u32[]{:S(2)}) collective-permute-start(f16[136,1024]{1,0:T(8,128)(2,1)S(1)} %get-tuple-element.57), channel_id=1, source_target_pairs={{0,32},{1,225},{2,34},{3,227},{4,36},{5,229},{6,38},{7,231},{8,40}... | collective-permute-start | bytes 835592 | tf_op jit(solution)/shard_map/ppermute | solution.py:41
  92.3 9.8 %collective-permute-start.17 = (f16[136,1024]{1,0:T(8,128)(2,1)S(1)}, f16[136,1024]{1,0:T(8,128)(2,1)S(1)}, u32[]{:S(2)}, u32[]{:S(2)}) collective-permute-start(f16[136,1024]{1,0:T(8,128)(2,1)S(1)} %fusion.2), channel_id=1, source_target_pairs={{0,64},{1,193},{2,66},{3,195},{4,68},{5,197},{6,70},{7,199},{8,72}... | collective-permute-start | bytes 835592 | tf_op jit(solution)/shard_map/ppermute | solution.py:41
  93.5 12.2 %collective-permute-start.22 = (f16[72,1024]{1,0:T(8,128)(2,1)S(1)}, f16[72,1024]{1,0:T(8,128)(2,1)S(1)}, u32[]{:S(2)}, u32[]{:S(2)}) collective-permute-start(f16[72,1024]{1,0:T(8,128)(2,1)S(1)} %get-tuple-element.61), channel_id=1, source_target_pairs={{0,4},{1,17},{2,6},{3,19},{4,0},{5,21},{6,2},{7,23},{8,12},{9,25},... | collective-permute-start | bytes 442376 | tf_op jit(solution)/shard_map/ppermute | solution.py:41
  95.2 10.4 %collective-permute-start.23 = (f16[72,1024]{1,0:T(8,128)(2,1)S(1)}, f16[72,1024]{1,0:T(8,128)(2,1)S(1)}, u32[]{:S(2)}, u32[]{:S(2)}) collective-permute-start(f16[72,1024]{1,0:T(8,128)(2,1)S(1)} %get-tuple-element.62), channel_id=1, source_target_pairs={{0,2},{1,9},{2,4},{3,11},{4,6},{5,13},{6,0},{7,15},{8,10},{9,17},{... | collective-permute-start | bytes 442376 | tf_op jit(solution)/shard_map/ppermute | solution.py:41
  96.9 8.8 %collective-permute-start.24 = (f16[72,1024]{1,0:T(8,128)(2,1)S(1)}, f16[72,1024]{1,0:T(8,128)(2,1)S(1)}, u32[]{:S(2)}, u32[]{:S(2)}) collective-permute-start(f16[72,1024]{1,0:T(8,128)(2,1)S(1)} %get-tuple-element.63), channel_id=1, source_target_pairs={{0,6},{1,25},{2,0},{3,27},{4,2},{5,29},{6,4},{7,31},{8,14},{9,1},{... | collective-permute-start | bytes 442376 | tf_op jit(solution)/shard_map/ppermute | solution.py:41
  102.2 5.0 %collective-permute-start.18 = (f32[136,1024]{1,0:T(8,128)S(1)}, f32[136,1024]{1,0:T(8,128)S(1)}, u32[]{:S(2)}, u32[]{:S(2)}) collective-permute-start(f32[136,1024]{1,0:T(8,128)S(1)} %convert_add_fusion), channel_id=1, source_target_pairs={{0,1},{1,0},{2,3},{3,2},{4,5},{5,4},{6,7},{7,6},{8,9},{9,8},{10,11... | collective-permute-start | bytes 1671176 | tf_op jit(solution)/shard_map/ppermute | solution.py:41
  (2 other events, 2.7 us)

commit v6 on v5

--- a/solution.py
+++ b/solution.py
@@ -467,7 +467,7 @@
     )
     third = along_z((third + got[136:272].astype(F32)).astype(WIRE), 1)
     skipped = along_z((kept_half + got[408:480].astype(F32)).astype(WIRE), 2)
-    ahead = along_z((first + got[0:136].astype(F32)).astype(WIRE), 1)
+    first = (first + got[0:136].astype(F32)).astype(WIRE)
 
     def major_from(value, by):
         return moved(
@@ -487,7 +487,9 @@
         jnp.concatenate([nothing, late], axis=0),
     )
     onward = (second + got[272:408].astype(F32)) + (third.astype(F32) + late)
-    passed = along_z(onward.astype(WIRE), 2)
+    onward, first = lax.optimization_barrier((onward.astype(WIRE), first))
+    passed = along_z(onward, 2)
+    ahead = along_z(first, 1)
     q2 = major_from(r2, 2)
     q1 = major_from(r1, 1)
     q3 = major_from(r3, 3)

time: 111 us -> 111 us (level)
  transfers between devices with their start and end apart: 25 -> 25, of which waited for: 15 -> 17; matrix products, arithmetic and copies ran while one was open for 3% -> 3% of each run, Pallas kernels for 3% -> 3%
where the time goes in v6:
time: 111 us
  starting transfers between devices  48.1 us (43%)
  waiting for transfers between devices  36.6 us (33%)
  Pallas kernels  17 us (15%)
  other arithmetic  4.66 us (4%)
  between operations  2.77 us (2%)
  local copies, waits for them, and re-layouts  1.89 us (2%)
    ppermute x25, starting transfers between devices, moved(): return lax.ppermute(value, AXES, pairs)  48.1 us
    ppermute x25, waiting for transfers between devices, moved(): return lax.ppermute(value, AXES, pairs)  36.6 us
    pallas_call x14, Pallas kernels, call(): pl.pallas_call(kernel, in_specs=specs, out_specs=[pl.BlockSpec(memory_spa...  17 us
  transfers between devices with their start and end apart: 25, of which 17 were waited for; matrix products, arithmetic and copies ran while one was open for 3% of the time, Pallas kernels for 3%

profile of v6, /device:TPU:1, one launch (start us, length us, event | category | flops | bytes accessed | tf_op | source)
XLA Modules:
  0.0 111.0 jit_solution(11610290569629243760)
XLA Ops:
  1.7 2.5 %collective-permute-start.3 = (bf16[128,1024]{1,0:T(8,128)(2,1)S(1)}, bf16[128,1024]{1,0:T(8,128)(2,1)S(1)}, u32[]{:S(2)}, u32[]{:S(2)}) collective-permute-start(bf16[128,1024]{1,0:T(8,128)(2,1)S(1)} %shard_map.60.text), channel_id=1, source_target_pairs={{0,224},{1,33},{2,226},{3,35},{4,228},{5,37},{6,230},{7,39},{8,232... | collective-permute-start | bytes 786440 | tf_op jit(solution)/shard_map/ppermute | solution.py:41
  4.3 3.0 %collective-permute-start.4 = (bf16[128,1024]{1,0:T(8,128)(2,1)S(1)}, bf16[128,1024]{1,0:T(8,128)(2,1)S(1)}, u32[]{:S(2)}, u32[]{:S(2)}) collective-permute-start(bf16[128,1024]{1,0:T(8,128)(2,1)S(1)} %shard_map.60.text), channel_id=1, source_target_pairs={{0,192},{1,65},{2,194},{3,67},{4,196},{5,69},{6,198},{7,71},{8,200... | collective-permute-start | bytes 786440 | tf_op jit(solution)/shard_map/ppermute | solution.py:41
  8.0 3.0 %collective-permute-start.1 = (bf16[144,1024]{1,0:T(8,128)(2,1)S(1)}, bf16[144,1024]{1,0:T(8,128)(2,1)S(1)}, u32[]{:S(2)}, u32[]{:S(2)}) collective-permute-start(bf16[144,1024]{1,0:T(8,128)(2,1)S(1)} %shard_map.58.part), channel_id=1, source_target_pairs={{0,16},{1,17},{2,18},{3,19},{4,20},{5,21},{6,22},{7,23},{8,24},{9,... | collective-permute-start | bytes 884744 | tf_op jit(solution)/shard_map/ppermute | solution.py:41
  12.1 4.6 %collective-permute-done.4.two = bf16[128,1024]{1,0:T(8,128)(2,1)S(1)} collective-permute-done((bf16[128,1024]{1,0:T(8,128)(2,1)S(1)}, bf16[128,1024]{1,0:T(8,128)(2,1)S(1)}, u32[]{:S(2)}, u32[]{:S(2)}) %collective-permute-start.4) | collective-permute-done | bytes 262176 | tf_op jit(solution)/shard_map/ppermute | solution.py:41
  17.5 1.3 %collective-permute-start.2 = (bf16[128,1024]{1,0:T(8,128)(2,1)S(1)}, bf16[128,1024]{1,0:T(8,128)(2,1)S(1)}, u32[]{:S(2)}, u32[]{:S(2)}) collective-permute-start(bf16[128,1024]{1,0:T(8,128)(2,1)S(1)} %slice.69), channel_id=1, source_target_pairs={{0,2},{1,3},{2,0},{3,1},{4,6},{5,7},{6,4},{7,5},{8,10},{9,11},{10,... | collective-permute-start | bytes 786440 | tf_op jit(solution)/shard_map/ppermute | solution.py:41
  18.8 4.3 %collective-permute-done.2.other = bf16[128,1024]{1,0:T(8,128)(2,1)S(1)} collective-permute-done((bf16[128,1024]{1,0:T(8,128)(2,1)S(1)}, bf16[128,1024]{1,0:T(8,128)(2,1)S(1)}, u32[]{:S(2)}, u32[]{:S(2)}) %collective-permute-start.2) | collective-permute-done | bytes 262176 | tf_op jit(solution)/shard_map/ppermute | solution.py:41
  23.1 3.2 %collective-permute-done.5.skip = bf16[192,1024]{1,0:T(8,128)(2,1)S(1)} collective-permute-done((bf16[192,1024]{1,0:T(8,128)(2,1)S(1)}, bf16[192,1024]{1,0:T(8,128)(2,1)S(1)}, u32[]{:S(2)}, u32[]{:S(2)}) %collective-permute-start.5) | collective-permute-done | bytes 393248 | tf_op jit(solution)/shard_map/ppermute | solution.py:41
  26.3 4.0 %collective-permute-done.full = bf16[528,1024]{1,0:T(8,128)(2,1)S(1)} collective-permute-done((bf16[528,1024]{1,0:T(8,128)(2,1)S(1)}, bf16[528,1024]{1,0:T(8,128)(2,1)S(1)}, u32[]{:S(2)}, u32[]{:S(2)}) %collective-permute-start) | collective-permute-done | bytes 1081376 | tf_op jit(solution)/shard_map/ppermute | solution.py:41
  30.4 1.4 %collective-permute-start.6 = (bf16[720,1024]{1,0:T(8,128)(2,1)S(1)}, bf16[720,1024]{1,0:T(8,128)(2,1)S(1)}, u32[]{:S(2)}, u32[]{:S(2)}) collective-permute-start(bf16[720,1024]{1,0:T(8,128)(2,1)S(1)} %pad_maximum_fusion), channel_id=1, source_target_pairs={{0,1},{1,0},{2,3},{3,2},{4,5},{5,4},{6,7},{7,6},{8,9},{9,8},{10,11... | collective-permute-start | bytes 4423688 | tf_op jit(solution)/shard_map/ppermute | solution.py:41
  31.9 2.9 %collective-permute-done.6.far = bf16[720,1024]{1,0:T(8,128)(2,1)S(1)} collective-permute-done((bf16[720,1024]{1,0:T(8,128)(2,1)S(1)}, bf16[720,1024]{1,0:T(8,128)(2,1)S(1)}, u32[]{:S(2)}, u32[]{:S(2)}) %collective-permute-start.6) | collective-permute-done | bytes 1474592 | tf_op jit(solution)/shard_map/ppermute | solution.py:41
  34.8 5.1 %shard_map.62 = (f32[1024,1024]{1,0:T(8,128)S(1)}, bf16[1024,1024]{1,0:T(8,128)(2,1)S(1)}, bf16[1024,1024]{1,0:T(8,128)(2,1)S(1)}, s32[8,1024]{1,0:T(8,128)S(1)}...) custom-call(s32[4]{0:T(128)S(1)} %pad_add_fusion.place, bf16[528,1024]{1,0:T(8,128)(2,1)S(1)} %shard_map.59.own, ...), custom_call_target="tpu_custom_call" | custom-call | flops 8800000000 | bytes 24000000 | tf_op jit(solution)/shard_map/pallas_call | solution.py:62
  41.8 2.3 %collective-permute-start.8 = (f32[8,1024]{1,0:T(8,128)S(1)}, f32[8,1024]{1,0:T(8,128)S(1)}, u32[]{:S(2)}, u32[]{:S(2)}) collective-permute-start(f32[8,1024]{1,0:T(8,128)S(1)} %shard_map.63.own), channel_id=1, source_target_pairs={{0,8},{1,33},{2,10},{3,35},{4,12},{5,37},{6,14},{7,39},{8,0},{9,41... | collective-permute-start | bytes 98312 | tf_op jit(solution)/shard_map/ppermute | solution.py:41
  44.1 1.6 %collective-permute-done.8.came = f32[8,1024]{1,0:T(8,128)S(1)} collective-permute-done((f32[8,1024]{1,0:T(8,128)S(1)}, f32[8,1024]{1,0:T(8,128)S(1)}, u32[]{:S(2)}, u32[]{:S(2)}) %collective-permute-start.8) | collective-permute-done | bytes 32800 | tf_op jit(solution)/shard_map/ppermute | solution.py:41
  46.3 1.3 %collective-permute-start.9 = (f32[8,1024]{1,0:T(8,128)S(1)}, f32[8,1024]{1,0:T(8,128)S(1)}, u32[]{:S(2)}, u32[]{:S(2)}) collective-permute-start(f32[8,1024]{1,0:T(8,128)S(1)} %shard_map.64.own), channel_id=1, source_target_pairs={{0,2},{1,33},{2,0},{3,35},{4,6},{5,37},{6,4},{7,39},{8,10},{9,41},... | collective-permute-start | bytes 98312 | tf_op jit(solution)/shard_map/ppermute | solution.py:41
  47.5 1.6 %collective-permute-done.9.came = f32[8,1024]{1,0:T(8,128)S(1)} collective-permute-done((f32[8,1024]{1,0:T(8,128)S(1)}, f32[8,1024]{1,0:T(8,128)S(1)}, u32[]{:S(2)}, u32[]{:S(2)}) %collective-permute-start.9) | collective-permute-done | bytes 32800 | tf_op jit(solution)/shard_map/ppermute | solution.py:41
  49.1 2.1 %collective-permute-start.10 = (f32[8,1024]{1,0:T(8,128)S(1)}, f32[8,1024]{1,0:T(8,128)S(1)}, u32[]{:S(2)}, u32[]{:S(2)}) collective-permute-start(f32[8,1024]{1,0:T(8,128)S(1)} %shard_map.65.own), channel_id=1, source_target_pairs={{0,24},{1,65},{2,26},{3,67},{4,28},{5,69},{6,30},{7,71},{8,16},{9,... | collective-permute-start | bytes 98312 | tf_op jit(solution)/shard_map/ppermute | solution.py:41
  51.2 1.7 %collective-permute-done.10.came = f32[8,1024]{1,0:T(8,128)S(1)} collective-permute-done((f32[8,1024]{1,0:T(8,128)S(1)}, f32[8,1024]{1,0:T(8,128)S(1)}, u32[]{:S(2)}, u32[]{:S(2)}) %collective-permute-start.10) | collective-permute-done | bytes 32800 | tf_op jit(solution)/shard_map/ppermute | solution.py:41
  52.9 3.8 %collective-permute-start.11 = (f32[8,1024]{1,0:T(8,128)S(1)}, f32[8,1024]{1,0:T(8,128)S(1)}, u32[]{:S(2)}, u32[]{:S(2)}) collective-permute-start(f32[8,1024]{1,0:T(8,128)S(1)} %shard_map.66.own.held.rows.captions), channel_id=1, source_target_pairs={{0,6},{1,225},{2,4},{3,227},{4,2},{5,229},{6,0},{7,231},{8,14},{9,... | collective-permute-start | bytes 98312 | tf_op jit(solution)/shard_map/ppermute | solution.py:41
  58.8 3.4 %collective-permute-start.12 = (f32[8,1024]{1,0:T(8,128)S(1)}, f32[8,1024]{1,0:T(8,128)S(1)}, u32[]{:S(2)}, u32[]{:S(2)}) collective-permute-start(f32[8,1024]{1,0:T(8,128)S(1)} %shard_map.67.lse), channel_id=1, source_target_pairs={{0,1},{1,0},{2,3},{3,2},{4,5},{5,4},{6,7},{7,6},{8,9},{9,8},{10,11... | collective-permute-start | bytes 98312 | tf_op jit(solution)/shard_map/ppermute | solution.py:41
  63.0 3.4 %shard_map.69 = (bf16[1024,1024]{1,0:T(8,128)(2,1)S(1)}, f32[480,1024]{1,0:T(8,128)S(1)}, f32[72,1024]{1,0:T(8,128)S(1)}) custom-call(s32[4]{0:T(128)S(1)} %pad_add_fusion.place, f32[1024,1024]{1,0:T(8,128)S(1)} %copy-done.1, bf16[1024,1024]{1,0:T(8,128)(2,1)S(1)} %get-tuple-element.33.rows.regions, f32[8,1024]{1,0:T(8,128)S(1)} %shard_map.68.mine, ...), custom_call_target="tpu_custom_call" | custom-call | flops 44000002048 | bytes 120000000 | tf_op jit(solution)/shard_map/pallas_call | solution.py:62
  66.5 2.9 %shard_map.70 = (f32[264,1024]{1,0:T(8,128)S(1)}, f32[264,1024]{1,0:T(8,128)S(1)}, f32[264,1024]{1,0:T(8,128)S(1)}, f32[264,1024]{1,0:T(8,128)S(1)}) custom-call(s32[4]{0:T(128)S(1)} %pad_add_fusion.place, bf16[1024,1024]{1,0:T(8,128)(2,1)S(1)} %get-tuple-element.42.weights, bf16[1024,1024]{1,0:T(8,128)(2,1)S(1)} %copy-done.3, ...), custom_call_target="tpu_custom_call" | custom-call | flops 32999999488 | bytes 90000000 | tf_op jit(solution)/shard_map/pallas_call | solution.py:62
  69.8 1.3 %collective-permute-start.13 = (f16[480,1024]{1,0:T(8,128)(2,1)S(1)}, f16[480,1024]{1,0:T(8,128)(2,1)S(1)}, u32[]{:S(2)}, u32[]{:S(2)}) collective-permute-start(f16[480,1024]{1,0:T(8,128)(2,1)S(1)} %convert_element_type.79), channel_id=1, source_target_pairs={{0,1},{1,0},{2,3},{3,2},{4,5},{5,4},{6,7},{7,6},{8,9},{9,8},{10,11... | collective-permute-start | bytes 2949128 | tf_op jit(solution)/shard_map/ppermute | solution.py:41
  71.2 1.5 %collective-permute-start.19 = (f16[264,1024]{1,0:T(8,128)(2,1)S(1)}, f16[264,1024]{1,0:T(8,128)(2,1)S(1)}, u32[]{:S(2)}, u32[]{:S(2)}) collective-permute-start(f16[264,1024]{1,0:T(8,128)(2,1)S(1)} %convert_element_type.77), channel_id=1, source_target_pairs={{0,16},{1,5},{2,18},{3,7},{4,20},{5,1},{6,22},{7,3},{8,24},{9,13},... | collective-permute-start | bytes 1622024 | tf_op jit(solution)/shard_map/ppermute | solution.py:41
  72.7 1.5 %collective-permute-start.20 = (f16[264,1024]{1,0:T(8,128)(2,1)S(1)}, f16[264,1024]{1,0:T(8,128)(2,1)S(1)}, u32[]{:S(2)}, u32[]{:S(2)}) collective-permute-start(f16[264,1024]{1,0:T(8,128)(2,1)S(1)} %convert_element_type.76), channel_id=1, source_target_pairs={{0,8},{1,3},{2,10},{3,5},{4,12},{5,7},{6,14},{7,1},{8,16},{9,11},{... | collective-permute-start | bytes 1622024 | tf_op jit(solution)/shard_map/ppermute | solution.py:41
  75.4 1.8 %shard_map.71 = (f32[136,1024]{1,0:T(8,128)S(1)}, f32[136,1024]{1,0:T(8,128)S(1)}, f32[136,1024]{1,0:T(8,128)S(1)}, f32[136,1024]{1,0:T(8,128)S(1)}) custom-call(s32[4]{0:T(128)S(1)} %pad_add_fusion.place, bf16[1024,1024]{1,0:T(8,128)(2,1)S(1)} %get-tuple-element.42.weights, bf16[1024,1024]{1,0:T(8,128)(2,1)S(1)} %get-tuple-element.33.rows.regions, ...), custom_call_target="tpu_custom_call" | custom-call | flops 22000001024 | bytes 60000000 | tf_op jit(solution)/shard_map/pallas_call | solution.py:62
  77.4 4.5 %collective-permute-start.14 = (f16[136,1024]{1,0:T(8,128)(2,1)S(1)}, f16[136,1024]{1,0:T(8,128)(2,1)S(1)}, u32[]{:S(2)}, u32[]{:S(2)}) collective-permute-start(f16[136,1024]{1,0:T(8,128)(2,1)S(1)} %get-tuple-element.62), channel_id=1, source_target_pairs={{0,32},{1,225},{2,34},{3,227},{4,36},{5,229},{6,38},{7,231},{8,40}... | collective-permute-start | bytes 835592 | tf_op jit(solution)/shard_map/ppermute | solution.py:41
  82.0 4.9 %collective-permute-done.20 = f16[264,1024]{1,0:T(8,128)(2,1)S(1)} collective-permute-done((f16[264,1024]{1,0:T(8,128)(2,1)S(1)}, f16[264,1024]{1,0:T(8,128)(2,1)S(1)}, u32[]{:S(2)}, u32[]{:S(2)}) %collective-permute-start.20) | collective-permute-done | bytes 540704 | tf_op jit(solution)/shard_map/ppermute | solution.py:41
  88.8 3.6 %collective-permute-start.16 = (f16[136,1024]{1,0:T(8,128)(2,1)S(1)}, f16[136,1024]{1,0:T(8,128)(2,1)S(1)}, u32[]{:S(2)}, u32[]{:S(2)}) collective-permute-start(f16[136,1024]{1,0:T(8,128)(2,1)S(1)} %get-tuple-element.49), channel_id=1, source_target_pairs={{0,32},{1,225},{2,34},{3,227},{4,36},{5,229},{6,38},{7,231},{8,40}... | collective-permute-start | bytes 835592 | tf_op jit(solution)/shard_map/ppermute | solution.py:41
  93.6 1.8 %collective-permute-start.22 = (f16[72,1024]{1,0:T(8,128)(2,1)S(1)}, f16[72,1024]{1,0:T(8,128)(2,1)S(1)}, u32[]{:S(2)}, u32[]{:S(2)}) collective-permute-start(f16[72,1024]{1,0:T(8,128)(2,1)S(1)} %get-tuple-element.65), channel_id=1, source_target_pairs={{0,4},{1,17},{2,6},{3,19},{4,0},{5,21},{6,2},{7,23},{8,12},{9,25},... | collective-permute-start | bytes 442376 | tf_op jit(solution)/shard_map/ppermute | solution.py:41
  95.3 1.6 %collective-permute-start.23 = (f16[72,1024]{1,0:T(8,128)(2,1)S(1)}, f16[72,1024]{1,0:T(8,128)(2,1)S(1)}, u32[]{:S(2)}, u32[]{:S(2)}) collective-permute-start(f16[72,1024]{1,0:T(8,128)(2,1)S(1)} %get-tuple-element.66), channel_id=1, source_target_pairs={{0,2},{1,9},{2,4},{3,11},{4,6},{5,13},{6,0},{7,15},{8,10},{9,17},{... | collective-permute-start | bytes 442376 | tf_op jit(solution)/shard_map/ppermute | solution.py:41
  98.5 3.5 %collective-permute-done.17 = f16[136,1024]{1,0:T(8,128)(2,1)S(1)} collective-permute-done((f16[136,1024]{1,0:T(8,128)(2,1)S(1)}, f16[136,1024]{1,0:T(8,128)(2,1)S(1)}, u32[]{:S(2)}, u32[]{:S(2)}) %collective-permute-start.17) | collective-permute-done | bytes 278560 | tf_op jit(solution)/shard_map/ppermute | solution.py:41
  102.2 3.9 %collective-permute-start.18 = (f32[136,1024]{1,0:T(8,128)S(1)}, f32[136,1024]{1,0:T(8,128)S(1)}, u32[]{:S(2)}, u32[]{:S(2)}) collective-permute-start(f32[136,1024]{1,0:T(8,128)S(1)} %convert_add_fusion), channel_id=1, source_target_pairs={{0,1},{1,0},{2,3},{3,2},{4,5},{5,4},{6,7},{7,6},{8,9},{9,8},{10,11... | collective-permute-start | bytes 1671176 | tf_op jit(solution)/shard_map/ppermute | solution.py:41
  (79 shorter events, 18.7 us)
Async XLA Ops:
  1.7 5.6 %copy-start.4 = (f32[512,1024]{1,0:T(8,128)S(1)}, f32[512,1024]{1,0:T(8,128)}, u32[]{:S(2)}) copy-start(f32[512,1024]{1,0:T(8,128)} %regions.3) | copy-start | bytes 6291460
  1.7 5.7 %copy-start.6 = (s32[512]{0:T(512)S(1)}, s32[512]{0:T(512)}, u32[]{:S(2)}) copy-start(s32[512]{0:T(512)} %param.5) | copy-start | bytes 6148
  1.7 10.4 %collective-permute-start.3 = (bf16[128,1024]{1,0:T(8,128)(2,1)S(1)}, bf16[128,1024]{1,0:T(8,128)(2,1)S(1)}, u32[]{:S(2)}, u32[]{:S(2)}) collective-permute-start(bf16[128,1024]{1,0:T(8,128)(2,1)S(1)} %shard_map.60.text), channel_id=1, source_target_pairs={{0,224},{1,33},{2,226},{3,35},{4,228},{5,37},{6,230},{7,39},{8,232... | collective-permute-start | bytes 786440 | tf_op jit(solution)/shard_map/ppermute | solution.py:41
  4.3 12.5 %collective-permute-start.4 = (bf16[128,1024]{1,0:T(8,128)(2,1)S(1)}, bf16[128,1024]{1,0:T(8,128)(2,1)S(1)}, u32[]{:S(2)}, u32[]{:S(2)}) collective-permute-start(bf16[128,1024]{1,0:T(8,128)(2,1)S(1)} %shard_map.60.text), channel_id=1, source_target_pairs={{0,192},{1,65},{2,194},{3,67},{4,196},{5,69},{6,198},{7,71},{8,200... | collective-permute-start | bytes 786440 | tf_op jit(solution)/shard_map/ppermute | solution.py:41
  8.0 9.4 %collective-permute-start.1 = (bf16[144,1024]{1,0:T(8,128)(2,1)S(1)}, bf16[144,1024]{1,0:T(8,128)(2,1)S(1)}, u32[]{:S(2)}, u32[]{:S(2)}) collective-permute-start(bf16[144,1024]{1,0:T(8,128)(2,1)S(1)} %shard_map.58.part), channel_id=1, source_target_pairs={{0,16},{1,17},{2,18},{3,19},{4,20},{5,21},{6,22},{7,23},{8,24},{9,... | collective-permute-start | bytes 884744 | tf_op jit(solution)/shard_map/ppermute | solution.py:41
  11.7 18.6 %collective-permute-start = (bf16[528,1024]{1,0:T(8,128)(2,1)S(1)}, bf16[528,1024]{1,0:T(8,128)(2,1)S(1)}, u32[]{:S(2)}, u32[]{:S(2)}) collective-permute-start(bf16[528,1024]{1,0:T(8,128)(2,1)S(1)} %shard_map.59.own), channel_id=1, source_target_pairs={{0,24},{1,9},{2,26},{3,11},{4,28},{5,13},{6,30},{7,15},{8,0},{9,17... | collective-permute-start | bytes 3244040 | tf_op jit(solution)/shard_map/ppermute | solution.py:41
  17.4 8.9 %collective-permute-start.5 = (bf16[192,1024]{1,0:T(8,128)(2,1)S(1)}, bf16[192,1024]{1,0:T(8,128)(2,1)S(1)}, u32[]{:S(2)}, u32[]{:S(2)}) collective-permute-start(bf16[192,1024]{1,0:T(8,128)(2,1)S(1)} %shard_map.61), channel_id=1, source_target_pairs={{0,192},{1,65},{2,194},{3,67},{4,196},{5,69},{6,198},{7,71},{8,200... | collective-permute-start | bytes 1179656 | tf_op jit(solution)/shard_map/ppermute | solution.py:41
  17.5 5.6 %collective-permute-start.2 = (bf16[128,1024]{1,0:T(8,128)(2,1)S(1)}, bf16[128,1024]{1,0:T(8,128)(2,1)S(1)}, u32[]{:S(2)}, u32[]{:S(2)}) collective-permute-start(bf16[128,1024]{1,0:T(8,128)(2,1)S(1)} %slice.69), channel_id=1, source_target_pairs={{0,2},{1,3},{2,0},{3,1},{4,6},{5,7},{6,4},{7,5},{8,10},{9,11},{10,... | collective-permute-start | bytes 786440 | tf_op jit(solution)/shard_map/ppermute | solution.py:41
  30.4 4.3 %collective-permute-start.6 = (bf16[720,1024]{1,0:T(8,128)(2,1)S(1)}, bf16[720,1024]{1,0:T(8,128)(2,1)S(1)}, u32[]{:S(2)}, u32[]{:S(2)}) collective-permute-start(bf16[720,1024]{1,0:T(8,128)(2,1)S(1)} %pad_maximum_fusion), channel_id=1, source_target_pairs={{0,1},{1,0},{2,3},{3,2},{4,5},{5,4},{6,7},{7,6},{8,9},{9,8},{10,11... | collective-permute-start | bytes 4423688 | tf_op jit(solution)/shard_map/ppermute | solution.py:41
  39.9 13.0 %copy-start = (f32[1024,1024]{1,0:T(8,128)}, f32[1024,1024]{1,0:T(8,128)S(1)}, u32[]{:S(2)}) copy-start(f32[1024,1024]{1,0:T(8,128)S(1)} %get-tuple-element.32.held.scores) | copy-start | bytes 12582916
  39.9 13.0 %copy-start.2 = (bf16[1024,1024]{1,0:T(8,128)(2,1)}, bf16[1024,1024]{1,0:T(8,128)(2,1)S(1)}, u32[]{:S(2)}) copy-start(bf16[1024,1024]{1,0:T(8,128)(2,1)S(1)} %get-tuple-element.36.captions) | copy-start | bytes 6291460
  39.9 1.3 %collective-permute-start.7 = (f32[8,1024]{1,0:T(8,128)S(1)}, f32[8,1024]{1,0:T(8,128)S(1)}, u32[]{:S(2)}, u32[]{:S(2)}) collective-permute-start(f32[8,1024]{1,0:T(8,128)S(1)} %get-tuple-element.35), channel_id=1, source_target_pairs={{0,1},{1,0},{2,3},{3,2},{4,5},{5,4},{6,7},{7,6},{8,9},{9,8},{10,11... | collective-permute-start | bytes 98312 | tf_op jit(solution)/shard_map/ppermute | solution.py:41
  41.8 3.9 %collective-permute-start.8 = (f32[8,1024]{1,0:T(8,128)S(1)}, f32[8,1024]{1,0:T(8,128)S(1)}, u32[]{:S(2)}, u32[]{:S(2)}) collective-permute-start(f32[8,1024]{1,0:T(8,128)S(1)} %shard_map.63.own), channel_id=1, source_target_pairs={{0,8},{1,33},{2,10},{3,35},{4,12},{5,37},{6,14},{7,39},{8,0},{9,41... | collective-permute-start | bytes 98312 | tf_op jit(solution)/shard_map/ppermute | solution.py:41
  46.3 2.9 %collective-permute-start.9 = (f32[8,1024]{1,0:T(8,128)S(1)}, f32[8,1024]{1,0:T(8,128)S(1)}, u32[]{:S(2)}, u32[]{:S(2)}) collective-permute-start(f32[8,1024]{1,0:T(8,128)S(1)} %shard_map.64.own), channel_id=1, source_target_pairs={{0,2},{1,33},{2,0},{3,35},{4,6},{5,37},{6,4},{7,39},{8,10},{9,41},... | collective-permute-start | bytes 98312 | tf_op jit(solution)/shard_map/ppermute | solution.py:41
  49.1 3.8 %collective-permute-start.10 = (f32[8,1024]{1,0:T(8,128)S(1)}, f32[8,1024]{1,0:T(8,128)S(1)}, u32[]{:S(2)}, u32[]{:S(2)}) collective-permute-start(f32[8,1024]{1,0:T(8,128)S(1)} %shard_map.65.own), channel_id=1, source_target_pairs={{0,24},{1,65},{2,26},{3,67},{4,28},{5,69},{6,30},{7,71},{8,16},{9,... | collective-permute-start | bytes 98312 | tf_op jit(solution)/shard_map/ppermute | solution.py:41
  52.9 5.2 %collective-permute-start.11 = (f32[8,1024]{1,0:T(8,128)S(1)}, f32[8,1024]{1,0:T(8,128)S(1)}, u32[]{:S(2)}, u32[]{:S(2)}) collective-permute-start(f32[8,1024]{1,0:T(8,128)S(1)} %shard_map.66.own.held.rows.captions), channel_id=1, source_target_pairs={{0,6},{1,225},{2,4},{3,227},{4,2},{5,229},{6,0},{7,231},{8,14},{9,... | collective-permute-start | bytes 98312 | tf_op jit(solution)/shard_map/ppermute | solution.py:41
  58.8 4.2 %copy-start.1 = (f32[1024,1024]{1,0:T(8,128)S(1)}, f32[1024,1024]{1,0:T(8,128)}, u32[]{:S(2)}) copy-start(f32[1024,1024]{1,0:T(8,128)} %copy-done) | copy-start | bytes 12582916
  58.8 4.2 %collective-permute-start.12 = (f32[8,1024]{1,0:T(8,128)S(1)}, f32[8,1024]{1,0:T(8,128)S(1)}, u32[]{:S(2)}, u32[]{:S(2)}) collective-permute-start(f32[8,1024]{1,0:T(8,128)S(1)} %shard_map.67.lse), channel_id=1, source_target_pairs={{0,1},{1,0},{2,3},{3,2},{4,5},{5,4},{6,7},{7,6},{8,9},{9,8},{10,11... | collective-permute-start | bytes 98312 | tf_op jit(solution)/shard_map/ppermute | solution.py:41
  63.0 3.5 %copy-start.3 = (bf16[1024,1024]{1,0:T(8,128)(2,1)S(1)}, bf16[1024,1024]{1,0:T(8,128)(2,1)}, u32[]{:S(2)}) copy-start(bf16[1024,1024]{1,0:T(8,128)(2,1)} %copy-done.2) | copy-start | bytes 6291460
  69.8 7.3 %collective-permute-start.13 = (f16[480,1024]{1,0:T(8,128)(2,1)S(1)}, f16[480,1024]{1,0:T(8,128)(2,1)S(1)}, u32[]{:S(2)}, u32[]{:S(2)}) collective-permute-start(f16[480,1024]{1,0:T(8,128)(2,1)S(1)} %convert_element_type.79), channel_id=1, source_target_pairs={{0,1},{1,0},{2,3},{3,2},{4,5},{5,4},{6,7},{7,6},{8,9},{9,8},{10,11... | collective-permute-start | bytes 2949128 | tf_op jit(solution)/shard_map/ppermute | solution.py:41
  71.2 10.9 %collective-permute-start.19 = (f16[264,1024]{1,0:T(8,128)(2,1)S(1)}, f16[264,1024]{1,0:T(8,128)(2,1)S(1)}, u32[]{:S(2)}, u32[]{:S(2)}) collective-permute-start(f16[264,1024]{1,0:T(8,128)(2,1)S(1)} %convert_element_type.77), channel_id=1, source_target_pairs={{0,16},{1,5},{2,18},{3,7},{4,20},{5,1},{6,22},{7,3},{8,24},{9,13},... | collective-permute-start | bytes 1622024 | tf_op jit(solution)/shard_map/ppermute | solution.py:41
  72.7 14.3 %collective-permute-start.20 = (f16[264,1024]{1,0:T(8,128)(2,1)S(1)}, f16[264,1024]{1,0:T(8,128)(2,1)S(1)}, u32[]{:S(2)}, u32[]{:S(2)}) collective-permute-start(f16[264,1024]{1,0:T(8,128)(2,1)S(1)} %convert_element_type.76), channel_id=1, source_target_pairs={{0,8},{1,3},{2,10},{3,5},{4,12},{5,7},{6,14},{7,1},{8,16},{9,11},{... | collective-permute-start | bytes 1622024 | tf_op jit(solution)/shard_map/ppermute | solution.py:41
  74.2 12.9 %collective-permute-start.21 = (f16[264,1024]{1,0:T(8,128)(2,1)S(1)}, f16[264,1024]{1,0:T(8,128)(2,1)S(1)}, u32[]{:S(2)}, u32[]{:S(2)}) collective-permute-start(f16[264,1024]{1,0:T(8,128)(2,1)S(1)} %convert_element_type.78), channel_id=1, source_target_pairs={{0,24},{1,7},{2,26},{3,1},{4,28},{5,3},{6,30},{7,5},{8,0},{9,15},{... | collective-permute-start | bytes 1622024 | tf_op jit(solution)/shard_map/ppermute | solution.py:41
  77.4 11.2 %collective-permute-start.14 = (f16[136,1024]{1,0:T(8,128)(2,1)S(1)}, f16[136,1024]{1,0:T(8,128)(2,1)S(1)}, u32[]{:S(2)}, u32[]{:S(2)}) collective-permute-start(f16[136,1024]{1,0:T(8,128)(2,1)S(1)} %get-tuple-element.62), channel_id=1, source_target_pairs={{0,32},{1,225},{2,34},{3,227},{4,36},{5,229},{6,38},{7,231},{8,40}... | collective-permute-start | bytes 835592 | tf_op jit(solution)/shard_map/ppermute | solution.py:41
  81.9 6.6 %collective-permute-start.15 = (f16[72,1024]{1,0:T(8,128)(2,1)S(1)}, f16[72,1024]{1,0:T(8,128)(2,1)S(1)}, u32[]{:S(2)}, u32[]{:S(2)}) collective-permute-start(f16[72,1024]{1,0:T(8,128)(2,1)S(1)} %add_convert_fusion.2), channel_id=1, source_target_pairs={{0,64},{1,193},{2,66},{3,195},{4,68},{5,197},{6,70},{7,199},{8,72}... | collective-permute-start | bytes 442376 | tf_op jit(solution)/shard_map/ppermute | solution.py:41
  88.8 9.7 %collective-permute-start.16 = (f16[136,1024]{1,0:T(8,128)(2,1)S(1)}, f16[136,1024]{1,0:T(8,128)(2,1)S(1)}, u32[]{:S(2)}, u32[]{:S(2)}) collective-permute-start(f16[136,1024]{1,0:T(8,128)(2,1)S(1)} %get-tuple-element.49), channel_id=1, source_target_pairs={{0,32},{1,225},{2,34},{3,227},{4,36},{5,229},{6,38},{7,231},{8,40}... | collective-permute-start | bytes 835592 | tf_op jit(solution)/shard_map/ppermute | solution.py:41
  92.5 9.6 %collective-permute-start.17 = (f16[136,1024]{1,0:T(8,128)(2,1)S(1)}, f16[136,1024]{1,0:T(8,128)(2,1)S(1)}, u32[]{:S(2)}, u32[]{:S(2)}) collective-permute-start(f16[136,1024]{1,0:T(8,128)(2,1)S(1)} %fusion.2), channel_id=1, source_target_pairs={{0,64},{1,193},{2,66},{3,195},{4,68},{5,197},{6,70},{7,199},{8,72}... | collective-permute-start | bytes 835592 | tf_op jit(solution)/shard_map/ppermute | solution.py:41
  93.6 12.6 %collective-permute-start.22 = (f16[72,1024]{1,0:T(8,128)(2,1)S(1)}, f16[72,1024]{1,0:T(8,128)(2,1)S(1)}, u32[]{:S(2)}, u32[]{:S(2)}) collective-permute-start(f16[72,1024]{1,0:T(8,128)(2,1)S(1)} %get-tuple-element.65), channel_id=1, source_target_pairs={{0,4},{1,17},{2,6},{3,19},{4,0},{5,21},{6,2},{7,23},{8,12},{9,25},... | collective-permute-start | bytes 442376 | tf_op jit(solution)/shard_map/ppermute | solution.py:41
  95.3 10.8 %collective-permute-start.23 = (f16[72,1024]{1,0:T(8,128)(2,1)S(1)}, f16[72,1024]{1,0:T(8,128)(2,1)S(1)}, u32[]{:S(2)}, u32[]{:S(2)}) collective-permute-start(f16[72,1024]{1,0:T(8,128)(2,1)S(1)} %get-tuple-element.66), channel_id=1, source_target_pairs={{0,2},{1,9},{2,4},{3,11},{4,6},{5,13},{6,0},{7,15},{8,10},{9,17},{... | collective-permute-start | bytes 442376 | tf_op jit(solution)/shard_map/ppermute | solution.py:41
  97.0 9.2 %collective-permute-start.24 = (f16[72,1024]{1,0:T(8,128)(2,1)S(1)}, f16[72,1024]{1,0:T(8,128)(2,1)S(1)}, u32[]{:S(2)}, u32[]{:S(2)}) collective-permute-start(f16[72,1024]{1,0:T(8,128)(2,1)S(1)} %get-tuple-element.67), channel_id=1, source_target_pairs={{0,6},{1,25},{2,0},{3,27},{4,2},{5,29},{6,4},{7,31},{8,14},{9,1},{... | collective-permute-start | bytes 442376 | tf_op jit(solution)/shard_map/ppermute | solution.py:41
  102.2 5.5 %collective-permute-start.18 = (f32[136,1024]{1,0:T(8,128)S(1)}, f32[136,1024]{1,0:T(8,128)S(1)}, u32[]{:S(2)}, u32[]{:S(2)}) collective-permute-start(f32[136,1024]{1,0:T(8,128)S(1)} %convert_add_fusion), channel_id=1, source_target_pairs={{0,1},{1,0},{2,3},{3,2},{4,5},{5,4},{6,7},{7,6},{8,9},{9,8},{10,11... | collective-permute-start | bytes 1671176 | tf_op jit(solution)/shard_map/ppermute | solution.py:41
  107.0 1.7 %copy-start.8 = (f32[128]{0:T(128)S(1)}, f32[128]{0:T(128)}, u32[]{:S(2)}) copy-start(f32[128]{0:T(128)} %compare_select_fusion) | copy-start | bytes 1540
  (2 other events, 2.6 us)
